TPU v7x, 32 devices: a whole 2x2x4 slice. The times are simulated.
32 devices in a mesh: grp: 2 (over y), row: 4 (over z), col: 4 (over x, core).
Axes of the slice: x: 2, y: 2, z: 4, core: 2. Of those that a mesh axis runs over, the one named last changes fastest.
Arguments:
- matrix: bfloat16 [8192, 16384], P(('grp', 'row'), 'col'), parts along dimension 0, may hold values from -6 to 6
- row_factor: float32 [8192, 128], P(('grp', 'row')), parts along dimension 0, may hold values from -1.8 to 1.8
- col_factor: float32 [32768, 128], P(('grp', 'col')), parts along dimension 0, may hold values from -1.8 to 1.8
- row_mean: float32 [8192, 128], P(('grp', 'row')), parts along dimension 0
- row_square: float32 [8192, 128], P(('grp', 'row')), parts along dimension 0, may hold values from 6.1035155e-07 to 1.2207031e-05
- col_mean: float32 [32768, 128], P(('grp', 'col')), parts along dimension 0
- col_square: float32 [32768, 128], P(('grp', 'col')), parts along dimension 0, may hold values from 2.4414064e-07 to 2.4414062e-06
Outputs:
- new_rows: float32 [8192, 128], P(('grp', 'row')), parts along dimension 0
- new_cols: float32 [32768, 128], P(('grp', 'col')), parts along dimension 0
There are 2 independent parts, one for each index of `grp`. A program takes and returns all parts, laid end to end along the dimension named above; each array names one. Nothing has to cross between parts.
All inputs are finite; a program needn't handle non-finite values.
Results may differ from a plain program's by a relative error of at most 0.0003.
Values sent between devices are 32-bit elements; how exact they have to be, the bound alone decides.
No kernel may reach another device: no remote copies, remote signals or barrier semaphores. Data moves between devices by JAX's collectives and lax.ppermute only.
A program may use at most 128 MiB of HBM per device.

v0:
```python
import jax
import jax.numpy as jnp
from jax import lax
from jax.sharding import PartitionSpec as P

START = 100


DELTA = 1.0
LEARN_RATE = 0.05
BETA_ONE = 0.9
BETA_TWO = 0.999
EPSILON = 1e-08
HIGH = lax.Precision.HIGHEST


def adam_move(values, gradient, first_moment, square, counter):
    first_moment = BETA_ONE * first_moment + (1.0 - BETA_ONE) * gradient
    square = BETA_TWO * square + (1.0 - BETA_TWO) * gradient * gradient
    fixed_mean = first_moment / (1.0 - BETA_ONE**counter)
    fixed_square = square / (1.0 - BETA_TWO**counter)
    return (
        values - LEARN_RATE * fixed_mean / (jnp.sqrt(fixed_square) + EPSILON),
        first_moment,
        square,
    )


def clipped(block, row_part, col_part):
    fitted = lax.dot_general(row_part, col_part, (((1,), (1,)), ((), ())), precision=HIGH)
    return jnp.clip(fitted - block.astype(jnp.float32), -DELTA, DELTA)


def on_device(matrix, row_factor, col_factor, row_mean, row_square, col_mean, col_square):
    n_row = lax.axis_size("row")
    n_col = lax.axis_size("col")
    rows_total = matrix.shape[0] * n_row
    cols_total = matrix.shape[1] * n_col
    for inner_step in range(2):
        slopes = clipped(matrix, row_factor, col_factor)
        partial_sum = lax.dot_general(slopes, row_factor, (((0,), (0,)), ((), ())), precision=HIGH)
        summed = lax.psum(partial_sum, "row")
        col_factor, col_mean, col_square = adam_move(
            col_factor, summed / rows_total, col_mean, col_square, START + 1 + inner_step
        )
    slopes = clipped(matrix, row_factor, col_factor)
    partial_sum = jnp.dot(slopes, col_factor, precision=HIGH)
    summed = lax.psum(partial_sum, "col")
    new_rows, own_mean, own_square = adam_move(
        row_factor, summed / cols_total, row_mean, row_square, START + 1
    )
    return (new_rows, col_factor)


def solution(mesh):
    return jax.shard_map(
        on_device,
        mesh=mesh,
        in_specs=(
            P(("grp", "row"), "col"),
            P(("grp", "row"), None),
            P(("grp", "col"), None),
            P(("grp", "row"), None),
            P(("grp", "row"), None),
            P(("grp", "col"), None),
            P(("grp", "col"), None),
        ),
        out_specs=(P(("grp", "row"), None), P(("grp", "col"), None)),
        check_vma=False,
    )
```

profile of v0, /device:TPU:0, one launch (start us, length us, event | category | flops | bytes accessed | tf_op | source)
XLA Modules:
  0.0 365.8 jit_solution(3680058474274111493)
XLA Ops:
  7.2 0.0 copy-start.3
  7.2 0.0 all-reduce.4.cloned.1.call-start
  7.2 0.0 copy-start
  7.2 15.9 %fusion.24 = f32[1024,4096]{1,0:T(8,128)S(1)} fusion(f32[1024,128]{1,0:T(8,128)} %param.8, f32[4096,128]{1,0:T(8,128)} %param.9), kind=kOutput, calls=%fused_computation.29 | convolution fusion | flops 6442450944 | bytes 19398656 | tf_op jit(solution)/shard_map/dot_general | solution.py:30
  23.2 0.0 copy-done.3
  23.2 0.0 copy-done
  23.2 42.3 %fusion.1 = f32[4096,128]{1,0:T(8,128)} fusion(f32[1024,128]{1,0:T(8,128)S(1)} %copy-done.3, f32[1024,4096]{1,0:T(8,128)S(1)} %fusion.24, bf16[1024,4096]{1,0:T(8,128)(2,1)S(1)} %copy-done), kind=kOutput, calls=%fused_computation.4 | convolution fusion | flops 6455033856 | bytes 27787264 | tf_op jit(solution)/shard_map/dot_general | solution.py:41
  65.4 0.0 copy-start.1
  65.5 0.0 all-reduce.4.cloned.1.call-update
  65.5 0.0 all-reduce.6.cloned.1.call-start
  65.5 89.3 %all-reduce.4.cloned.1.call-done = f32[4096,128]{1,0:T(8,128)} async-done(((f32[4096,128]{1,0:T(8,128)}), f32[4096,128]{1,0:T(8,128)}) %all-reduce.4.cloned.1.call-update) | async-done | bytes 2097168 | tf_op jit(solution)/shard_map/psum | solution.py:42
  154.9 0.0 copy-done.1
  154.9 16.2 %fusion.23 = f32[4096,1024]{0,1:T(8,128)S(1)} fusion(f32[1024,128]{1,0:T(8,128)S(1)} %copy-done.3, f32[4096,128]{1,0:T(8,128)S(1)} %copy-done.1, f32[4096,128]{1,0:T(8,128)} %all-reduce.4.cloned.1.call-done, f32[4096,128]{1,0:T(8,128)} %param.12, f32[4096,128]{1,0:T(8,128)} %param.13), kind=kOutput, calls=%fused_computation.28 | convolution fusion | flops 6449266688 | bytes 25690112 | tf_op jit(solution)/shard_map/dot_general | solution.py:30
  171.1 30.4 %fusion.4 = f32[4096,128]{1,0:T(8,128)} fusion(f32[1024,128]{1,0:T(8,128)S(1)} %copy-done.3, bf16[1024,4096]{1,0:T(8,128)(2,1)} %param.7, f32[4096,1024]{0,1:T(8,128)S(1)} %fusion.23), kind=kOutput, calls=%fused_computation.6 | convolution fusion | flops 6455033856 | bytes 27787264 | tf_op jit(solution)/shard_map/dot_general | solution.py:41
  201.5 0.0 all-reduce.6.cloned.1.call-update
  201.5 0.0 all-reduce.8.cloned.1.call-start
  201.5 85.6 %all-reduce.6.cloned.1.call-done = f32[4096,128]{1,0:T(8,128)} async-done(((f32[4096,128]{1,0:T(8,128)}), f32[4096,128]{1,0:T(8,128)}) %all-reduce.6.cloned.1.call-update) | async-done | bytes 2097168 | tf_op jit(solution)/shard_map/psum | solution.py:42
  287.1 0.0 slice-start
  287.1 5.2 %divide_subtract_fusion = f32[4096,128]{1,0:T(8,128)S(1)} fusion(f32[4096,128]{1,0:T(8,128)} %all-reduce.6.cloned.1.call-done, f32[4096,128]{1,0:T(8,128)} %all-reduce.4.cloned.1.call-done, f32[4096,128]{1,0:T(8,128)} %param.12, f32[4096,128]{1,0:T(8,128)} %param.13, f32[4096,128]{1,0:T(8,128)S(1)} %copy-done.1), kind=kLoop, calls=%fused_computation.17 | loop fusion | flops 13631488 | bytes 12582912 | tf_op jit(solution)/shard_map/sub | solution.py:23
  292.3 0.0 copy-start.2
  292.3 1.3 copy-done.2
  293.7 13.8 %fusion.25 = f32[4096,1024]{0,1:T(8,128)S(1)} fusion(f32[4096,128]{1,0:T(8,128)S(1)} %divide_subtract_fusion, f32[1024,128]{1,0:T(8,128)S(1)} %copy-done.3), kind=kOutput, calls=%fused_computation.30 | convolution fusion | flops 6442450944 | bytes 19398656 | tf_op jit(solution)/shard_map/dot_general | solution.py:30
  307.5 0.0 slice-done
  307.5 0.0 slice-done.1
  307.5 0.0 copy-start.4
  307.5 0.0 copy-start.5
  307.5 17.0 %fusion.7 = f32[1024,128]{1,0:T(8,128)} fusion(f32[4096,128]{1,0:T(8,128)} %copy-done.2, bf16[1024,4096]{1,0:T(8,128)(2,1)S(1)} %bitcast.19, f32[4096,1024]{0,1:T(8,128)S(1)} %fusion.25), kind=kOutput, calls=%fused_computation.8 | convolution fusion | flops 6455033856 | bytes 27787264 | tf_op jit(solution)/shard_map/dot_general | solution.py:47
  324.5 0.0 all-reduce.8.cloned.1.call-update
  324.6 32.3 %all-reduce.8.cloned.1.call-done = f32[1024,128]{1,0:T(8,128)} async-done(((f32[1024,128]{1,0:T(8,128)}), f32[1024,128]{1,0:T(8,128)}) %all-reduce.8.cloned.1.call-update) | async-done | bytes 524304 | tf_op jit(solution)/shard_map/psum | solution.py:48
  356.9 0.0 copy-done.4
  356.9 0.0 copy-done.5
  356.9 2.2 divide_subtract_fusion.2
  (2 shorter events, 0.0 us)
Async XLA Ops:
  7.2 16.0 %copy-start.3 = (f32[1024,128]{1,0:T(8,128)S(1)}, f32[1024,128]{1,0:T(8,128)}, u32[]{:S(2)}) copy-start(f32[1024,128]{1,0:T(8,128)} %param.8) | copy-start | bytes 1572868
  7.2 147.7 %all-reduce.4.cloned.1.call-start = ((), (), s32[]{:S(2)}) async-start(), calls=%async_computation | async-start | bytes 4194304 | tf_op jit(solution)/shard_map/psum | solution.py:42
  7.2 16.0 %copy-start = (bf16[1024,4096]{1,0:T(8,128)(2,1)S(1)}, bf16[1024,4096]{1,0:T(8,128)(2,1)}, u32[]{:S(2)}) copy-start(bf16[1024,4096]{1,0:T(8,128)(2,1)} %param.7) | copy-start | bytes 25165828
  65.4 89.4 %copy-start.1 = (f32[4096,128]{1,0:T(8,128)S(1)}, f32[4096,128]{1,0:T(8,128)}, u32[]{:S(2)}) copy-start(f32[4096,128]{1,0:T(8,128)} %param.9) | copy-start | bytes 6291460
  65.5 221.6 %all-reduce.6.cloned.1.call-start = ((), (), s32[]{:S(2)}) async-start(), calls=%async_computation.1 | async-start | bytes 4194304 | tf_op jit(solution)/shard_map/psum | solution.py:42
  201.5 155.4 %all-reduce.8.cloned.1.call-start = ((), (), s32[]{:S(2)}) async-start(), calls=%async_computation.2 | async-start | bytes 1048576 | tf_op jit(solution)/shard_map/psum | solution.py:48
  287.1 20.4 %slice-start = ((s8[8388608]{0:T(1024)(128)(4,1)}), s8[4194304]{0:T(1024)(128)(4,1)S(1)}, s32[]{:S(2)}) async-start(s8[8388608]{0:T(1024)(128)(4,1)} %bitcast.18), calls=%async_computation.3 | async-start | bytes 8388608
  292.3 1.3 copy-start.2
  293.6 13.9 %slice-start.1 = ((s8[8388608]{0:T(1024)(128)(4,1)}), s8[4194304]{0:T(1024)(128)(4,1)S(1)}, s32[]{:S(2)}) async-start(s8[8388608]{0:T(1024)(128)(4,1)} %bitcast.18), calls=%async_computation.4 | async-start | bytes 8388608
  307.5 49.3 %copy-start.4 = (f32[1024,128]{1,0:T(8,128)S(1)}, f32[1024,128]{1,0:T(8,128)}, u32[]{:S(2)}) copy-start(f32[1024,128]{1,0:T(8,128)} %param.11) | copy-start | bytes 1572868
  307.5 49.3 %copy-start.5 = (f32[1024,128]{1,0:T(8,128)S(1)}, f32[1024,128]{1,0:T(8,128)}, u32[]{:S(2)}) copy-start(f32[1024,128]{1,0:T(8,128)} %param.10) | copy-start | bytes 1572868
Sparse Core Ops, SparseCore 0:
  65.6 89.2 all-reduce.3
  201.6 85.4 all-reduce.5
  324.7 32.1 all-reduce.7
where the time goes:
time: 370 us; the launch traced here: 366 us
  waiting for transfers between devices  207 us (56%)
  matrix products  136 us (37%)
  between operations  14.1 us (4%)
  other arithmetic  7.41 us (2%)
    psum x2, waiting for transfers between devices, on_device(): summed = lax.psum(partial_sum, 'row')  175 us
    dot_general x2, matrix products, on_device(): lax.dot_general(slopes, row_factor, (((0,), (0,)), ((), ())), precision=H...  72.7 us
    dot_general x3, matrix products, clipped(): lax.dot_general(row_part, col_part, (((1,), (1,)), ((), ())), precision=H...  46 us
    psum x1, waiting for transfers between devices, on_device(): summed = lax.psum(partial_sum, 'col')  32.3 us
    dot_general x1, matrix products, on_device(): partial_sum = jnp.dot(slopes, col_factor, precision=HIGH)  17 us
    sub x2, other arithmetic, adam_move(): values - LEARN_RATE * fixed_mean / (jnp.sqrt(fixed_square) + EPSILON)  7.41 us
  transfers between devices with their start and end apart: 3, of which 3 were waited for; matrix products, arithmetic and copies ran while one was open for 0% of the time, Pallas kernels for 0%

commit v1 on v0

v1 whole, which is shorter than its diff:
```python
import functools

import jax
import jax.numpy as jnp
from jax import lax
from jax.experimental import pallas as pl
from jax.experimental.pallas import tpu as pltpu
from jax.sharding import PartitionSpec as P

START = 100
DELTA = 1.0
LEARN_RATE = 0.05
BETA_ONE = 0.9
BETA_TWO = 0.999
EPSILON = 1e-08
F32, BF16 = jnp.float32, jnp.bfloat16
NT = (((1,), (1,)), ((), ()))
ROW_BLOCK = 256
CHUNKS = 8
LAG = 2


def adam_move(values, gradient, first_moment, square, counter):
    first_moment = BETA_ONE * first_moment + (1.0 - BETA_ONE) * gradient
    square = BETA_TWO * square + (1.0 - BETA_TWO) * gradient * gradient
    fixed_mean = first_moment / (1.0 - BETA_ONE**counter)
    fixed_square = square / (1.0 - BETA_TWO**counter)
    return (
        values - LEARN_RATE * fixed_mean / (jnp.sqrt(fixed_square) + EPSILON),
        first_moment,
        square,
    )


def split(values):
    high = values.astype(BF16)
    return high, (values - high.astype(F32)).astype(BF16)


def slopes_of(row_pair, col_pair, block):
    fitted = lax.dot_general(row_pair, col_pair, NT, preferred_element_type=F32)
    return jnp.clip(fitted - block.astype(F32), -DELTA, DELTA).astype(BF16)


def col_partial(twice_ref, turned_ref, col, mat_ref, first_col):
    col_pair = jnp.concatenate(split(col), axis=1)
    width, rank = col.shape
    total = None
    for at in range(0, mat_ref.shape[0], ROW_BLOCK):
        rows = pl.ds(at, ROW_BLOCK)
        slopes = slopes_of(twice_ref[rows, :], col_pair, mat_ref[rows, pl.ds(first_col, width)])
        term = jnp.dot(turned_ref[:, rows], slopes, preferred_element_type=F32)
        total = term if total is None else total + term
    return (total[:rank] + total[rank:]).T


def first_kernel(row_ref, col_ref, mat_ref, twice_ref, pair_ref, turned_ref, out_ref):
    high, low = split(row_ref[...])
    twice_ref[...] = jnp.concatenate([high, high], axis=1)
    pair_ref[...] = jnp.concatenate([high, low], axis=1)
    turned_ref[...] = jnp.concatenate([high.T, low.T], axis=0)
    out_ref[...] = col_partial(twice_ref, turned_ref, col_ref[...], mat_ref, 0)


def fresh_kernel(at, token_ref, twice_ref, turned_ref, col_ref, mat_ref, out_ref):
    del token_ref
    width = out_ref.shape[0]
    col = col_ref[pl.ds(at, width), :]
    out_ref[...] = col_partial(twice_ref, turned_ref, col, mat_ref, at)


def middle_kernel(
    at, rows_total, token_ref, twice_ref, turned_ref, sum_ref, col_ref, mean_ref, square_ref, mat_ref,
    new_ref, new_mean_ref, new_square_ref, out_ref,
):
    del token_ref
    own = pl.ds(at, out_ref.shape[0])
    new, new_mean_ref[...], new_square_ref[...] = adam_move(
        col_ref[own, :], sum_ref[...] / rows_total, mean_ref[own, :], square_ref[own, :], START + 1
    )
    new_ref[...] = new
    out_ref[...] = col_partial(twice_ref, turned_ref, new, mat_ref, at)


def last_kernel(
    at, rows_total, token_ref, pair_ref, sum_ref, col_ref, mean_ref, square_ref, mat_ref, grad_ref,
    new_ref, out_ref,
):
    del token_ref
    new, _, _ = adam_move(
        col_ref[...], sum_ref[...] / rows_total, mean_ref[...], square_ref[...], START + 2
    )
    new_ref[...] = new
    high, low = split(new)
    twice = jnp.concatenate([high, high], axis=1)
    pair = jnp.concatenate([high, low], axis=1)
    width, rank = new.shape
    for at_row in range(0, mat_ref.shape[0], ROW_BLOCK):
        rows = pl.ds(at_row, ROW_BLOCK)
        slopes = slopes_of(pair_ref[rows, :], twice, mat_ref[rows, pl.ds(at, width)])
        term = jnp.dot(slopes, pair, preferred_element_type=F32)
        out_ref[rows, :] = grad_ref[rows, :] + term[:, :rank] + term[:, rank:]


def call(kernel, outs, *args, name, token=None):
    vmem = pl.BlockSpec(memory_space=pltpu.VMEM)
    in_specs = [vmem] * len(args)
    if token is not None:
        in_specs, args = [pl.BlockSpec(memory_space=pl.ANY), *in_specs], (token, *args)
    return pl.pallas_call(
        kernel,
        out_shape=[jax.ShapeDtypeStruct(shape, kind) for shape, kind in outs],
        in_specs=in_specs,
        out_specs=[vmem] * len(outs),
        compiler_params=pltpu.CompilerParams(vmem_limit_bytes=16 << 20),
        name=name,
    )(*args)


class Work:
    def __init__(self, matrix, row_factor, col_factor, col_mean, col_square, rows_total):
        self.matrix, self.row, self.rows_total = matrix, row_factor, rows_total
        self.col, self.mean, self.square = col_factor, col_mean, col_square
        self.width = col_factor.shape[0] // CHUNKS
        self.rank = col_factor.shape[1]
        self.small = ((self.width, self.rank), F32)
        self.moved = {}
        self.new = {}
        self.grad = jnp.zeros(row_factor.shape, F32)

    def first(self):
        rows, rank = self.row.shape
        wide = ((rows, 2 * rank), BF16)
        self.twice, self.pair, self.turned, out = call(
            first_kernel,
            [wide, wide, ((2 * rank, rows), BF16), self.small],
            self.row, self.col[: self.width], self.matrix[:, : self.width],
            name="first",
        )
        return out

    def fresh(self, chunk, token):
        (out,) = call(
            functools.partial(fresh_kernel, chunk * self.width),
            [self.small],
            self.twice, self.turned, self.col, self.matrix,
            name="fresh", token=token,
        )
        return out

    def middle(self, chunk, total, token):
        *self.moved[chunk], out = call(
            functools.partial(middle_kernel, chunk * self.width, self.rows_total),
            [self.small] * 4,
            self.twice, self.turned, total, self.col, self.mean, self.square, self.matrix,
            name="middle", token=token,
        )
        return out

    def last(self, chunk, total, token):
        self.new[chunk], self.grad = call(
            functools.partial(last_kernel, chunk * self.width, self.rows_total),
            [self.small, (self.row.shape, F32)],
            self.pair, total, *self.moved[chunk], self.matrix, self.grad,
            name="last", token=token,
        )


def plain_columns(work):
    sums = [lax.psum(work.first(), "row")]
    for chunk in range(1, CHUNKS):
        sums.append(lax.psum(work.fresh(chunk, sums[0]), "row"))
    sums = [lax.psum(work.middle(chunk, sums[chunk], sums[chunk]), "row") for chunk in range(CHUNKS)]
    for chunk in range(CHUNKS):
        work.last(chunk, sums[chunk], sums[chunk])


def line_columns(work):
    n_col = lax.axis_size("col")
    row = lax.axis_index("row")
    outer = (row == 0) | (row == 3)
    outer_pairs = [(0, 1), (1, 0), (2, 3), (3, 2)]
    inner_pairs = []
    for col in range(n_col):
        inner_pairs += [(n_col + col, 2 * n_col + col), (2 * n_col + col, n_col + col)]
        inner_pairs += [(at * n_col + col, at * n_col + (col ^ 1)) for at in (0, 3)]
    slots = 2 * CHUNKS
    own, joined, whole, from_outer, from_inner = {}, {}, {}, {}, {}
    own[0] = work.first()
    token = own[0]
    for k in range(slots + 4 * LAG):
        if 0 <= k - LAG < slots:
            joined[k - LAG] = own[k - LAG] + from_outer[k - LAG]
        if 0 <= k - 2 * LAG < slots:
            whole[k - 2 * LAG] = joined[k - 2 * LAG] + from_inner[k - LAG]
        if k < slots + 2 * LAG:
            if k < 2 * LAG:
                payload = own[k]
            elif k < slots:
                payload = jnp.where(outer, own[k], whole[k - 2 * LAG])
            else:
                payload = whole[k - 2 * LAG]
            token = payload
            from_outer[k] = lax.ppermute(payload, "row", outer_pairs)
        if 0 <= k - LAG < slots:
            from_inner[k] = lax.ppermute(joined[k - LAG], ("row", "col"), inner_pairs)
        nxt = k + 1
        if nxt < CHUNKS:
            own[nxt] = work.fresh(nxt, token)
        elif nxt < slots:
            done = nxt - CHUNKS
            total = jnp.where(outer, from_outer[done + 2 * LAG], whole[done])
            own[nxt] = work.middle(done, total, token)
        done = k - 3 * LAG
        if CHUNKS <= done < slots:
            total = jnp.where(outer, from_outer[done + 2 * LAG], whole[done])
            work.last(done - CHUNKS, total, token)


def row_step(grad, row_factor, row_mean, row_square, cols_total):
    half = grad.shape[0] // 2
    high = lax.rem(lax.axis_index("col"), 2) == 1
    swap = [(0, 1), (1, 0), (2, 3), (3, 2)]
    across = [(0, 2), (2, 0), (1, 3), (3, 1)]

    def mine(array):
        return jnp.where(high, array[half:], array[:half])

    part = mine(grad) + lax.ppermute(jnp.where(high, grad[:half], grad[half:]), "col", swap)
    part = part + lax.ppermute(part, "col", across)
    new, _, _ = adam_move(
        mine(row_factor), part / cols_total, mine(row_mean), mine(row_square), START + 1
    )
    other = lax.ppermute(new, "col", swap)
    return jnp.concatenate([jnp.where(high, other, new), jnp.where(high, new, other)], axis=0)


def on_device(matrix, row_factor, col_factor, row_mean, row_square, col_mean, col_square):
    n_row = lax.axis_size("row")
    n_col = lax.axis_size("col")
    work = Work(matrix, row_factor, col_factor, col_mean, col_square, matrix.shape[0] * n_row)
    if n_row == 4 and n_col % 2 == 0:
        line_columns(work)
    else:
        plain_columns(work)
    cols_total = matrix.shape[1] * n_col
    if n_col == 4:
        new_rows = row_step(work.grad, row_factor, row_mean, row_square, cols_total)
    else:
        summed = lax.psum(work.grad, "col")
        new_rows, _, _ = adam_move(row_factor, summed / cols_total, row_mean, row_square, START + 1)
    return new_rows, jnp.concatenate([work.new[chunk] for chunk in range(CHUNKS)], axis=0)


def solution(mesh):
    return jax.shard_map(
        on_device,
        mesh=mesh,
        in_specs=(
            P(("grp", "row"), "col"),
            P(("grp", "row"), None),
            P(("grp", "col"), None),
            P(("grp", "row"), None),
            P(("grp", "row"), None),
            P(("grp", "col"), None),
            P(("grp", "col"), None),
        ),
        out_specs=(P(("grp", "row"), None), P(("grp", "col"), None)),
        check_vma=False,
    )
```

time: 370 us -> 168 us (0.45)
  waiting for transfers between devices: 207 us -> 68.9 us
  matrix products: 136 us -> 0 us
  starting transfers between devices: 0.12 us -> 34.6 us
  Pallas kernels: 0 us -> 30.6 us
  local copies, waits for them, and re-layouts: 1.35 us -> 17.8 us
  between operations: 14.1 us -> 1.86 us
  other arithmetic: 7.41 us -> 13.6 us
    psum x3 -> x0, waiting for transfers between devices: 207 us -> none  [the longest x2 175 us: on_device(): summed = lax.psum(partial_sum, 'row')]
    dot_general x6 -> x0, matrix products: 136 us -> none  [the longest x2 72.7 us: on_device(): lax.dot_general(slopes, row_factor, (((0,), (0,)), ((), ())), precision=H...]
    ppermute x0 -> x39, waiting for transfers between devices: none -> 68.9 us  [the longest x20 59.2 us: line_columns(): from_outer[k] = lax.ppermute(payload, 'row', outer_pairs)]
    ppermute x0 -> x39, starting transfers between devices: none -> 34.6 us  [the longest x20 30.5 us: line_columns(): from_outer[k] = lax.ppermute(payload, 'row', outer_pairs)]
    pallas_call x0 -> x24, Pallas kernels: none -> 30.6 us  [call(): pl.pallas_call(kernel, out_shape=[jax.ShapeDtypeStruct(shape, kind) for s...]
    unnamed x16 -> x131, local copies, waits for them, and re-layouts: 1.35 us -> 15.3 us
    sub x2 -> x1, other arithmetic: 7.41 us -> 0.23 us  [adam_move(): values - LEARN_RATE * fixed_mean / (jnp.sqrt(fixed_square) + EPSILON)]
    select_n x0 -> x22, other arithmetic: none -> 6.31 us  [the longest x8 3.63 us: line_columns(): total = jnp.where(outer, from_outer[done + 2 * LAG], whole[done])]
  transfers between devices with their start and end apart: 3 -> 39, of which waited for: 3 -> 14; matrix products, arithmetic and copies ran while one was open for 0% -> 7% of each run, Pallas kernels for 0% -> 17%
where the time goes in v1:
time: 168 us; the launch traced here: 167 us
  waiting for transfers between devices  68.9 us (41%)
  starting transfers between devices  34.6 us (21%)
  Pallas kernels  30.6 us (18%)
  local copies, waits for them, and re-layouts  17.8 us (11%)
  other arithmetic  13.6 us (8%)
  between operations  1.86 us (1%)
    ppermute x20, waiting for transfers between devices, line_columns(): from_outer[k] = lax.ppermute(payload, 'row', outer_pairs)  59.2 us
    pallas_call x24, Pallas kernels, call(): pl.pallas_call(kernel, out_shape=[jax.ShapeDtypeStruct(shape, kind) for s...  30.6 us
    ppermute x20, starting transfers between devices, line_columns(): from_outer[k] = lax.ppermute(payload, 'row', outer_pairs)  30.5 us
    unnamed x131, local copies, waits for them, and re-layouts  15.3 us
    ppermute x1, waiting for transfers between devices, row_step(): part = part + lax.ppermute(part, 'col', across)  6.78 us
    add x12, other arithmetic, line_columns(): joined[k - LAG] = own[k - LAG] + from_outer[k - LAG]  3.98 us
    select_n x8, other arithmetic, line_columns(): total = jnp.where(outer, from_outer[done + 2 * LAG], whole[done])  3.63 us
  transfers between devices with their start and end apart: 39, of which 14 were waited for; matrix products, arithmetic and copies ran while one was open for 7% of the time, Pallas kernels for 17%

profile of v1, /device:TPU:0, one launch (start us, length us, event | category | flops | bytes accessed | tf_op | source)
XLA Modules:
  0.0 167.4 jit_solution(7394704074122744691)
XLA Ops:
  1.7 1.4 slice.37.mat_ref
  4.4 3.1 %collective-permute-start = (f32[512,128]{1,0:T(8,128)S(1)}, f32[512,128]{1,0:T(8,128)S(1)}, u32[]{:S(2)}, u32[]{:S(2)}) collective-permute-start(f32[512,128]{1,0:T(8,128)S(1)} %get-tuple-element.54.token_ref), channel_id=1, source_target_pairs={{0,4},{4,0},{8,12},{12,8},{1,5},{5,1},{9,13},{13,9},{2,6},{6,2},{1... | collective-permute-start | bytes 786440 | tf_op jit(solution)/shard_map/ppermute | solution.py:204
  7.5 3.4 %copy-done = bf16[1024,4096]{1,0:T(8,128)(2,1)S(1)} copy-done((bf16[1024,4096]{1,0:T(8,128)(2,1)S(1)}, bf16[1024,4096]{1,0:T(8,128)(2,1)}, u32[]{:S(2)}) %copy-start) | copy-done | bytes 8388632
  12.3 1.9 %copy-done.1 = bf16[1024,4096]{1,0:T(8,128)(2,1)S(1)} copy-done((bf16[1024,4096]{1,0:T(8,128)(2,1)S(1)}, bf16[1024,4096]{1,0:T(8,128)(2,1)}, u32[]{:S(2)}) %copy-start.1) | copy-done | bytes 8388632
  14.3 2.0 %fresh.8.token_ref = f32[512,128]{1,0:T(8,128)} custom-call(f32[512,128]{1,0:T(8,128)S(1)} %fresh.7.token_ref, bf16[1024,256]{1,0:T(8,128)(2,1)S(1)} %get-tuple-element.55.twice_ref, bf16[256,1024]{1,0:T(8,128)(2,1)S(1)} %get-tuple-element.56.turned_ref, f32[4096,128]{1,0:T(8,128)S(1)} %copy-done.4, bf16[1024,4096]{1,0:T(8,128)(2,1)S(1)} %copy-done.1), custom_call_target="tpu_custom_call" | custom-call | tf_op jit(solution)/shard_map/fresh/pallas_call | solution.py:110
  16.2 2.0 %fresh.9.token_ref = f32[512,128]{1,0:T(8,128)} custom-call(f32[512,128]{1,0:T(8,128)} %fresh.8.token_ref, bf16[1024,256]{1,0:T(8,128)(2,1)S(1)} %get-tuple-element.55.twice_ref, bf16[256,1024]{1,0:T(8,128)(2,1)S(1)} %get-tuple-element.56.turned_ref, f32[4096,128]{1,0:T(8,128)S(1)} %copy-done.4, bf16[1024,4096]{1,0:T(8,128)(2,1)S(1)} %copy-done.1), custom_call_target="tpu_custom_call" | custom-call | tf_op jit(solution)/shard_map/fresh/pallas_call | solution.py:110
  18.3 1.9 %collective-permute-start.4 = (f32[512,128]{1,0:T(8,128)}, f32[512,128]{1,0:T(8,128)}, u32[]{:S(2)}, u32[]{:S(2)}) collective-permute-start(f32[512,128]{1,0:T(8,128)} %fresh.8.token_ref), channel_id=1, source_target_pairs={{0,4},{4,0},{8,12},{12,8},{1,5},{5,1},{9,13},{13,9},{2,6},{6,2},{1... | collective-permute-start | bytes 786440 | tf_op jit(solution)/shard_map/ppermute | solution.py:204
  23.5 4.3 %collective-permute-done.6 = f32[512,128]{1,0:T(8,128)} collective-permute-done((f32[512,128]{1,0:T(8,128)}, f32[512,128]{1,0:T(8,128)}, u32[]{:S(2)}, u32[]{:S(2)}) %collective-permute-start.6) | collective-permute-done | bytes 262176 | tf_op jit(solution)/shard_map/ppermute | solution.py:204
  28.9 3.0 %collective-permute-done.4 = f32[512,128]{1,0:T(8,128)} collective-permute-done((f32[512,128]{1,0:T(8,128)}, f32[512,128]{1,0:T(8,128)}, u32[]{:S(2)}, u32[]{:S(2)}) %collective-permute-start.4) | collective-permute-done | bytes 262176 | tf_op jit(solution)/shard_map/ppermute | solution.py:204
  34.2 3.4 %copy-done.2 = bf16[1024,4096]{1,0:T(8,128)(2,1)S(1)} copy-done((bf16[1024,4096]{1,0:T(8,128)(2,1)S(1)}, bf16[1024,4096]{1,0:T(8,128)(2,1)}, u32[]{:S(2)}) %copy-start.2) | copy-done | bytes 8388632
  42.5 5.6 %collective-permute-start.14 = (f32[512,128]{1,0:T(8,128)S(1)}, f32[512,128]{1,0:T(8,128)S(1)}, u32[]{:S(2)}, u32[]{:S(2)}) collective-permute-start(f32[512,128]{1,0:T(8,128)S(1)} %get-tuple-element.122.token_ref), channel_id=1, source_target_pairs={{0,4},{4,0},{8,12},{12,8},{1,5},{5,1},{9,13},{13,9},{2,6},{6,2},{1... | collective-permute-start | bytes 786440 | tf_op jit(solution)/shard_map/ppermute | solution.py:204
  48.2 1.9 %collective-permute-start.12 = (f32[512,128]{1,0:T(8,128)S(1)}, f32[512,128]{1,0:T(8,128)S(1)}, u32[]{:S(2)}, u32[]{:S(2)}) collective-permute-start(f32[512,128]{1,0:T(8,128)S(1)} %get-tuple-element.124.token_ref), channel_id=1, source_target_pairs={{0,4},{4,0},{8,12},{12,8},{1,5},{5,1},{9,13},{13,9},{2,6},{6,2},{1... | collective-permute-start | bytes 786440 | tf_op jit(solution)/shard_map/ppermute | solution.py:204
  50.2 5.1 %collective-permute-done.14 = f32[512,128]{1,0:T(8,128)S(1)} collective-permute-done((f32[512,128]{1,0:T(8,128)S(1)}, f32[512,128]{1,0:T(8,128)S(1)}, u32[]{:S(2)}, u32[]{:S(2)}) %collective-permute-start.14) | collective-permute-done | bytes 262176 | tf_op jit(solution)/shard_map/ppermute | solution.py:204
  55.5 5.5 %collective-permute-done.8 = f32[512,128]{1,0:T(8,128)S(1)} collective-permute-done((f32[512,128]{1,0:T(8,128)S(1)}, f32[512,128]{1,0:T(8,128)S(1)}, u32[]{:S(2)}, u32[]{:S(2)}) %collective-permute-start.8) | collective-permute-done | bytes 262176 | tf_op jit(solution)/shard_map/ppermute | solution.py:204
  61.1 8.7 %collective-permute-done.10 = f32[512,128]{1,0:T(8,128)S(1)} collective-permute-done((f32[512,128]{1,0:T(8,128)S(1)}, f32[512,128]{1,0:T(8,128)S(1)}, u32[]{:S(2)}, u32[]{:S(2)}) %collective-permute-start.10) | collective-permute-done | bytes 262176 | tf_op jit(solution)/shard_map/ppermute | solution.py:204
  72.7 3.3 %collective-permute-start.16 = (f32[512,128]{1,0:T(8,128)S(1)}, f32[512,128]{1,0:T(8,128)S(1)}, u32[]{:S(2)}, u32[]{:S(2)}) collective-permute-start(f32[512,128]{1,0:T(8,128)S(1)} %get-tuple-element.120.token_ref), channel_id=1, source_target_pairs={{0,4},{4,0},{8,12},{12,8},{1,5},{5,1},{9,13},{13,9},{2,6},{6,2},{1... | collective-permute-start | bytes 786440 | tf_op jit(solution)/shard_map/ppermute | solution.py:204
  77.6 2.6 %collective-permute-start.18 = (f32[512,128]{1,0:T(8,128)S(1)}, f32[512,128]{1,0:T(8,128)S(1)}, u32[]{:S(2)}, u32[]{:S(2)}) collective-permute-start(f32[512,128]{1,0:T(8,128)S(1)} %get-tuple-element.118.token_ref), channel_id=1, source_target_pairs={{0,4},{4,0},{8,12},{12,8},{1,5},{5,1},{9,13},{13,9},{2,6},{6,2},{1... | collective-permute-start | bytes 786440 | tf_op jit(solution)/shard_map/ppermute | solution.py:204
  83.0 1.6 middle.11
  86.4 2.4 %collective-permute-done.18 = f32[512,128]{1,0:T(8,128)S(1)} collective-permute-done((f32[512,128]{1,0:T(8,128)S(1)}, f32[512,128]{1,0:T(8,128)S(1)}, u32[]{:S(2)}, u32[]{:S(2)}) %collective-permute-start.18) | collective-permute-done | bytes 262176 | tf_op jit(solution)/shard_map/ppermute | solution.py:204
  89.0 5.5 %collective-permute-done.20 = f32[512,128]{1,0:T(8,128)S(1)} collective-permute-done((f32[512,128]{1,0:T(8,128)S(1)}, f32[512,128]{1,0:T(8,128)S(1)}, u32[]{:S(2)}, u32[]{:S(2)}) %collective-permute-start.20) | collective-permute-done | bytes 262176 | tf_op jit(solution)/shard_map/ppermute | solution.py:204
  94.7 3.2 %collective-permute-done.22 = f32[512,128]{1,0:T(8,128)S(1)} collective-permute-done((f32[512,128]{1,0:T(8,128)S(1)}, f32[512,128]{1,0:T(8,128)S(1)}, u32[]{:S(2)}, u32[]{:S(2)}) %collective-permute-start.22) | collective-permute-done | bytes 262176 | tf_op jit(solution)/shard_map/ppermute | solution.py:204
  99.5 2.1 %collective-permute-start.33 = (f32[512,128]{1,0:T(8,128)S(1)}, f32[512,128]{1,0:T(8,128)S(1)}, u32[]{:S(2)}, u32[]{:S(2)}) collective-permute-start(f32[512,128]{1,0:T(8,128)S(1)} %get-tuple-element.112.token_ref), channel_id=1, source_target_pairs={{0,4},{4,0},{8,12},{12,8},{1,5},{5,1},{9,13},{13,9},{2,6},{6,2},{1... | collective-permute-start | bytes 786440 | tf_op jit(solution)/shard_map/ppermute | solution.py:204
  105.3 1.5 collective-permute-start.27
  109.1 5.2 %collective-permute-done.30 = f32[512,128]{1,0:T(8,128)S(1)} collective-permute-done((f32[512,128]{1,0:T(8,128)S(1)}, f32[512,128]{1,0:T(8,128)S(1)}, u32[]{:S(2)}, u32[]{:S(2)}) %collective-permute-start.30) | collective-permute-done | bytes 262176 | tf_op jit(solution)/shard_map/ppermute | solution.py:204
  114.4 10.7 %collective-permute-done.24 = f32[512,128]{1,0:T(8,128)S(1)} collective-permute-done((f32[512,128]{1,0:T(8,128)S(1)}, f32[512,128]{1,0:T(8,128)S(1)}, u32[]{:S(2)}, u32[]{:S(2)}) %collective-permute-start.24) | collective-permute-done | bytes 262176 | tf_op jit(solution)/shard_map/ppermute | solution.py:204
  127.3 1.9 %collective-permute-start.35 = (f32[512,128]{1,0:T(8,128)S(1)}, f32[512,128]{1,0:T(8,128)}, u32[]{:S(2)}, u32[]{:S(2)}) collective-permute-start(f32[512,128]{1,0:T(8,128)S(1)} %add.145.token_ref), channel_id=1, source_target_pairs={{0,4},{4,0},{8,12},{12,8},{1,5},{5,1},{9,13},{13,9},{2,6},{6,2},{1... | collective-permute-start | bytes 786440 | tf_op jit(solution)/shard_map/ppermute | solution.py:204
  129.6 3.4 %copy-done.3 = bf16[1024,4096]{1,0:T(8,128)(2,1)S(1)} copy-done((bf16[1024,4096]{1,0:T(8,128)(2,1)S(1)}, bf16[1024,4096]{1,0:T(8,128)(2,1)}, u32[]{:S(2)}) %copy-start.3) | copy-done | bytes 8388632
  137.0 1.9 %collective-permute-start.26 = (f32[512,128]{1,0:T(8,128)S(1)}, f32[512,128]{1,0:T(8,128)S(1)}, u32[]{:S(2)}, u32[]{:S(2)}) collective-permute-start(f32[512,128]{1,0:T(8,128)S(1)} %add.139.token_ref), channel_id=1, source_target_pairs={{0,4},{4,0},{8,12},{12,8},{1,5},{5,1},{9,13},{13,9},{2,6},{6,2},{1... | collective-permute-start | bytes 786440 | tf_op jit(solution)/shard_map/ppermute | solution.py:204
  146.9 5.5 %collective-permute-done.29 = f32[512,128]{1,0:T(8,128)S(1)} collective-permute-done((f32[512,128]{1,0:T(8,128)S(1)}, f32[512,128]{1,0:T(8,128)S(1)}, u32[]{:S(2)}, u32[]{:S(2)}) %collective-permute-start.29) | collective-permute-done | bytes 262176 | tf_op jit(solution)/shard_map/ppermute | solution.py:204
  154.7 1.5 collective-permute-done.36
  156.3 1.6 collective-permute-start.37
  157.9 6.8 %collective-permute-done.37 = f32[512,128]{1,0:T(8,128)S(1)} collective-permute-done((f32[512,128]{1,0:T(8,128)S(1)}, f32[512,128]{1,0:T(8,128)S(1)}, u32[]{:S(2)}, u32[]{:S(2)}) %collective-permute-start.37) | collective-permute-done | bytes 262176 | tf_op jit(solution)/shard_map/ppermute | solution.py:230
  (246 shorter events, 51.7 us)
Async XLA Ops:
  4.4 15.8 %collective-permute-start = (f32[512,128]{1,0:T(8,128)S(1)}, f32[512,128]{1,0:T(8,128)S(1)}, u32[]{:S(2)}, u32[]{:S(2)}) collective-permute-start(f32[512,128]{1,0:T(8,128)S(1)} %get-tuple-element.54.token_ref), channel_id=1, source_target_pairs={{0,4},{4,0},{8,12},{12,8},{1,5},{5,1},{9,13},{13,9},{2,6},{6,2},{1... | collective-permute-start | bytes 786440 | tf_op jit(solution)/shard_map/ppermute | solution.py:204
  18.2 9.5 %collective-permute-start.6 = (f32[512,128]{1,0:T(8,128)}, f32[512,128]{1,0:T(8,128)}, u32[]{:S(2)}, u32[]{:S(2)}) collective-permute-start(f32[512,128]{1,0:T(8,128)} %fresh.9.token_ref), channel_id=1, source_target_pairs={{0,4},{4,0},{8,12},{12,8},{1,5},{5,1},{9,13},{13,9},{2,6},{6,2},{1... | collective-permute-start | bytes 786440 | tf_op jit(solution)/shard_map/ppermute | solution.py:204
  18.3 13.6 %collective-permute-start.4 = (f32[512,128]{1,0:T(8,128)}, f32[512,128]{1,0:T(8,128)}, u32[]{:S(2)}, u32[]{:S(2)}) collective-permute-start(f32[512,128]{1,0:T(8,128)} %fresh.8.token_ref), channel_id=1, source_target_pairs={{0,4},{4,0},{8,12},{12,8},{1,5},{5,1},{9,13},{13,9},{2,6},{6,2},{1... | collective-permute-start | bytes 786440 | tf_op jit(solution)/shard_map/ppermute | solution.py:204
  21.0 12.1 %collective-permute-start.1 = (f32[512,128]{1,0:T(8,128)}, f32[512,128]{1,0:T(8,128)}, u32[]{:S(2)}, u32[]{:S(2)}) collective-permute-start(f32[512,128]{1,0:T(8,128)} %add.114), channel_id=1, source_target_pairs={{4,8},{8,4},{0,1},{12,13},{5,9},{9,5},{1,0},{13,12},{6,10},{10,6},... | collective-permute-start | bytes 786440 | tf_op jit(solution)/shard_map/ppermute | solution.py:206
  21.7 17.1 %collective-permute-start.3 = (f32[512,128]{1,0:T(8,128)}, f32[512,128]{1,0:T(8,128)}, u32[]{:S(2)}, u32[]{:S(2)}) collective-permute-start(f32[512,128]{1,0:T(8,128)} %add.116), channel_id=1, source_target_pairs={{4,8},{8,4},{0,1},{12,13},{5,9},{9,5},{1,0},{13,12},{6,10},{10,6},... | collective-permute-start | bytes 786440 | tf_op jit(solution)/shard_map/ppermute | solution.py:206
  28.8 13.6 %collective-permute-start.7 = (f32[512,128]{1,0:T(8,128)S(1)}, f32[512,128]{1,0:T(8,128)S(1)}, u32[]{:S(2)}, u32[]{:S(2)}) collective-permute-start(f32[512,128]{1,0:T(8,128)S(1)} %add.120), channel_id=1, source_target_pairs={{4,8},{8,4},{0,1},{12,13},{5,9},{9,5},{1,0},{13,12},{6,10},{10,6},... | collective-permute-start | bytes 786440 | tf_op jit(solution)/shard_map/ppermute | solution.py:206
  42.5 12.8 %collective-permute-start.14 = (f32[512,128]{1,0:T(8,128)S(1)}, f32[512,128]{1,0:T(8,128)S(1)}, u32[]{:S(2)}, u32[]{:S(2)}) collective-permute-start(f32[512,128]{1,0:T(8,128)S(1)} %get-tuple-element.122.token_ref), channel_id=1, source_target_pairs={{0,4},{4,0},{8,12},{12,8},{1,5},{5,1},{9,13},{13,9},{2,6},{6,2},{1... | collective-permute-start | bytes 786440 | tf_op jit(solution)/shard_map/ppermute | solution.py:204
  48.1 12.8 %collective-permute-start.8 = (f32[512,128]{1,0:T(8,128)S(1)}, f32[512,128]{1,0:T(8,128)S(1)}, u32[]{:S(2)}, u32[]{:S(2)}) collective-permute-start(f32[512,128]{1,0:T(8,128)S(1)} %get-tuple-element.128.token_ref), channel_id=1, source_target_pairs={{0,4},{4,0},{8,12},{12,8},{1,5},{5,1},{9,13},{13,9},{2,6},{6,2},{1... | collective-permute-start | bytes 786440 | tf_op jit(solution)/shard_map/ppermute | solution.py:204
  48.2 21.7 %collective-permute-start.12 = (f32[512,128]{1,0:T(8,128)S(1)}, f32[512,128]{1,0:T(8,128)S(1)}, u32[]{:S(2)}, u32[]{:S(2)}) collective-permute-start(f32[512,128]{1,0:T(8,128)S(1)} %get-tuple-element.124.token_ref), channel_id=1, source_target_pairs={{0,4},{4,0},{8,12},{12,8},{1,5},{5,1},{9,13},{13,9},{2,6},{6,2},{1... | collective-permute-start | bytes 786440 | tf_op jit(solution)/shard_map/ppermute | solution.py:204
  50.1 19.7 %collective-permute-start.10 = (f32[512,128]{1,0:T(8,128)S(1)}, f32[512,128]{1,0:T(8,128)S(1)}, u32[]{:S(2)}, u32[]{:S(2)}) collective-permute-start(f32[512,128]{1,0:T(8,128)S(1)} %get-tuple-element.126.token_ref), channel_id=1, source_target_pairs={{0,4},{4,0},{8,12},{12,8},{1,5},{5,1},{9,13},{13,9},{2,6},{6,2},{1... | collective-permute-start | bytes 786440 | tf_op jit(solution)/shard_map/ppermute | solution.py:204
  55.4 30.0 %collective-permute-start.15 = (f32[512,128]{1,0:T(8,128)S(1)}, f32[512,128]{1,0:T(8,128)S(1)}, u32[]{:S(2)}, u32[]{:S(2)}) collective-permute-start(f32[512,128]{1,0:T(8,128)S(1)} %get-tuple-element.148), channel_id=1, source_target_pairs={{4,8},{8,4},{0,1},{12,13},{5,9},{9,5},{1,0},{13,12},{6,10},{10,6},... | collective-permute-start | bytes 786440 | tf_op jit(solution)/shard_map/ppermute | solution.py:206
  61.0 11.7 %collective-permute-start.9 = (f32[512,128]{1,0:T(8,128)S(1)}, f32[512,128]{1,0:T(8,128)S(1)}, u32[]{:S(2)}, u32[]{:S(2)}) collective-permute-start(f32[512,128]{1,0:T(8,128)S(1)} %get-tuple-element.154), channel_id=1, source_target_pairs={{4,8},{8,4},{0,1},{12,13},{5,9},{9,5},{1,0},{13,12},{6,10},{10,6},... | collective-permute-start | bytes 786440 | tf_op jit(solution)/shard_map/ppermute | solution.py:206
  70.0 11.7 %collective-permute-start.13 = (f32[512,128]{1,0:T(8,128)S(1)}, f32[512,128]{1,0:T(8,128)S(1)}, u32[]{:S(2)}, u32[]{:S(2)}) collective-permute-start(f32[512,128]{1,0:T(8,128)S(1)} %get-tuple-element.150), channel_id=1, source_target_pairs={{4,8},{8,4},{0,1},{12,13},{5,9},{9,5},{1,0},{13,12},{6,10},{10,6},... | collective-permute-start | bytes 786440 | tf_op jit(solution)/shard_map/ppermute | solution.py:206
  72.7 13.6 %collective-permute-start.16 = (f32[512,128]{1,0:T(8,128)S(1)}, f32[512,128]{1,0:T(8,128)S(1)}, u32[]{:S(2)}, u32[]{:S(2)}) collective-permute-start(f32[512,128]{1,0:T(8,128)S(1)} %get-tuple-element.120.token_ref), channel_id=1, source_target_pairs={{0,4},{4,0},{8,12},{12,8},{1,5},{5,1},{9,13},{13,9},{2,6},{6,2},{1... | collective-permute-start | bytes 786440 | tf_op jit(solution)/shard_map/ppermute | solution.py:204
  77.6 11.3 %collective-permute-start.18 = (f32[512,128]{1,0:T(8,128)S(1)}, f32[512,128]{1,0:T(8,128)S(1)}, u32[]{:S(2)}, u32[]{:S(2)}) collective-permute-start(f32[512,128]{1,0:T(8,128)S(1)} %get-tuple-element.118.token_ref), channel_id=1, source_target_pairs={{0,4},{4,0},{8,12},{12,8},{1,5},{5,1},{9,13},{13,9},{2,6},{6,2},{1... | collective-permute-start | bytes 786440 | tf_op jit(solution)/shard_map/ppermute | solution.py:204
  81.8 12.7 %collective-permute-start.20 = (f32[512,128]{1,0:T(8,128)S(1)}, f32[512,128]{1,0:T(8,128)S(1)}, u32[]{:S(2)}, u32[]{:S(2)}) collective-permute-start(f32[512,128]{1,0:T(8,128)S(1)} %get-tuple-element.116.token_ref), channel_id=1, source_target_pairs={{0,4},{4,0},{8,12},{12,8},{1,5},{5,1},{9,13},{13,9},{2,6},{6,2},{1... | collective-permute-start | bytes 786440 | tf_op jit(solution)/shard_map/ppermute | solution.py:204
  85.4 12.5 %collective-permute-start.22 = (f32[512,128]{1,0:T(8,128)S(1)}, f32[512,128]{1,0:T(8,128)S(1)}, u32[]{:S(2)}, u32[]{:S(2)}) collective-permute-start(f32[512,128]{1,0:T(8,128)S(1)} %get-tuple-element.114.token_ref), channel_id=1, source_target_pairs={{0,4},{4,0},{8,12},{12,8},{1,5},{5,1},{9,13},{13,9},{2,6},{6,2},{1... | collective-permute-start | bytes 786440 | tf_op jit(solution)/shard_map/ppermute | solution.py:204
  86.4 13.1 %collective-permute-start.17 = (f32[512,128]{1,0:T(8,128)S(1)}, f32[512,128]{1,0:T(8,128)S(1)}, u32[]{:S(2)}, u32[]{:S(2)}) collective-permute-start(f32[512,128]{1,0:T(8,128)S(1)} %get-tuple-element.146), channel_id=1, source_target_pairs={{4,8},{8,4},{0,1},{12,13},{5,9},{9,5},{1,0},{13,12},{6,10},{10,6},... | collective-permute-start | bytes 786440 | tf_op jit(solution)/shard_map/ppermute | solution.py:206
  88.9 14.1 %collective-permute-start.19 = (f32[512,128]{1,0:T(8,128)S(1)}, f32[512,128]{1,0:T(8,128)S(1)}, u32[]{:S(2)}, u32[]{:S(2)}) collective-permute-start(f32[512,128]{1,0:T(8,128)S(1)} %get-tuple-element.144), channel_id=1, source_target_pairs={{4,8},{8,4},{0,1},{12,13},{5,9},{9,5},{1,0},{13,12},{6,10},{10,6},... | collective-permute-start | bytes 786440 | tf_op jit(solution)/shard_map/ppermute | solution.py:206
  94.6 10.6 %collective-permute-start.21 = (f32[512,128]{1,0:T(8,128)S(1)}, f32[512,128]{1,0:T(8,128)S(1)}, u32[]{:S(2)}, u32[]{:S(2)}) collective-permute-start(f32[512,128]{1,0:T(8,128)S(1)} %get-tuple-element.142), channel_id=1, source_target_pairs={{4,8},{8,4},{0,1},{12,13},{5,9},{9,5},{1,0},{13,12},{6,10},{10,6},... | collective-permute-start | bytes 786440 | tf_op jit(solution)/shard_map/ppermute | solution.py:206
  97.9 10.4 %collective-permute-start.23 = (f32[512,128]{1,0:T(8,128)S(1)}, f32[512,128]{1,0:T(8,128)S(1)}, u32[]{:S(2)}, u32[]{:S(2)}) collective-permute-start(f32[512,128]{1,0:T(8,128)S(1)} %get-tuple-element.140), channel_id=1, source_target_pairs={{4,8},{8,4},{0,1},{12,13},{5,9},{9,5},{1,0},{13,12},{6,10},{10,6},... | collective-permute-start | bytes 786440 | tf_op jit(solution)/shard_map/ppermute | solution.py:206
  103.1 11.2 %collective-permute-start.30 = (f32[512,128]{1,0:T(8,128)S(1)}, f32[512,128]{1,0:T(8,128)S(1)}, u32[]{:S(2)}, u32[]{:S(2)}) collective-permute-start(f32[512,128]{1,0:T(8,128)S(1)} %get-tuple-element.110.token_ref), channel_id=1, source_target_pairs={{0,4},{4,0},{8,12},{12,8},{1,5},{5,1},{9,13},{13,9},{2,6},{6,2},{1... | collective-permute-start | bytes 786440 | tf_op jit(solution)/shard_map/ppermute | solution.py:204
  105.3 20.7 %collective-permute-start.27 = (f32[512,128]{1,0:T(8,128)S(1)}, f32[512,128]{1,0:T(8,128)S(1)}, u32[]{:S(2)}, u32[]{:S(2)}) collective-permute-start(f32[512,128]{1,0:T(8,128)S(1)} %get-tuple-element.108.token_ref), channel_id=1, source_target_pairs={{0,4},{4,0},{8,12},{12,8},{1,5},{5,1},{9,13},{13,9},{2,6},{6,2},{1... | collective-permute-start | bytes 786440 | tf_op jit(solution)/shard_map/ppermute | solution.py:204
  108.4 16.8 %collective-permute-start.24 = (f32[512,128]{1,0:T(8,128)S(1)}, f32[512,128]{1,0:T(8,128)S(1)}, u32[]{:S(2)}, u32[]{:S(2)}) collective-permute-start(f32[512,128]{1,0:T(8,128)S(1)} %get-tuple-element.106.token_ref), channel_id=1, source_target_pairs={{0,4},{4,0},{8,12},{12,8},{1,5},{5,1},{9,13},{13,9},{2,6},{6,2},{1... | collective-permute-start | bytes 786440 | tf_op jit(solution)/shard_map/ppermute | solution.py:204
  109.0 18.2 %collective-permute-start.34 = (f32[512,128]{1,0:T(8,128)S(1)}, f32[512,128]{1,0:T(8,128)S(1)}, u32[]{:S(2)}, u32[]{:S(2)}) collective-permute-start(f32[512,128]{1,0:T(8,128)S(1)} %get-tuple-element.133), channel_id=1, source_target_pairs={{4,8},{8,4},{0,1},{12,13},{5,9},{9,5},{1,0},{13,12},{6,10},{10,6},... | collective-permute-start | bytes 786440 | tf_op jit(solution)/shard_map/ppermute | solution.py:206
  114.4 14.8 %collective-permute-start.31 = (f32[512,128]{1,0:T(8,128)S(1)}, f32[512,128]{1,0:T(8,128)S(1)}, u32[]{:S(2)}, u32[]{:S(2)}) collective-permute-start(f32[512,128]{1,0:T(8,128)S(1)} %get-tuple-element.135), channel_id=1, source_target_pairs={{4,8},{8,4},{0,1},{12,13},{5,9},{9,5},{1,0},{13,12},{6,10},{10,6},... | collective-permute-start | bytes 786440 | tf_op jit(solution)/shard_map/ppermute | solution.py:206
  125.9 10.0 %collective-permute-start.25 = (f32[512,128]{1,0:T(8,128)}, f32[512,128]{1,0:T(8,128)}, u32[]{:S(2)}, u32[]{:S(2)}) collective-permute-start(f32[512,128]{1,0:T(8,128)} %get-tuple-element.139), channel_id=1, source_target_pairs={{4,8},{8,4},{0,1},{12,13},{5,9},{9,5},{1,0},{13,12},{6,10},{10,6},... | collective-permute-start | bytes 786440 | tf_op jit(solution)/shard_map/ppermute | solution.py:206
  126.8 12.1 %collective-permute-start.28 = (f32[512,128]{1,0:T(8,128)}, f32[512,128]{1,0:T(8,128)}, u32[]{:S(2)}, u32[]{:S(2)}) collective-permute-start(f32[512,128]{1,0:T(8,128)} %get-tuple-element.137), channel_id=1, source_target_pairs={{4,8},{8,4},{0,1},{12,13},{5,9},{9,5},{1,0},{13,12},{6,10},{10,6},... | collective-permute-start | bytes 786440 | tf_op jit(solution)/shard_map/ppermute | solution.py:206
  127.3 15.3 %collective-permute-start.35 = (f32[512,128]{1,0:T(8,128)S(1)}, f32[512,128]{1,0:T(8,128)}, u32[]{:S(2)}, u32[]{:S(2)}) collective-permute-start(f32[512,128]{1,0:T(8,128)S(1)} %add.145.token_ref), channel_id=1, source_target_pairs={{0,4},{4,0},{8,12},{12,8},{1,5},{5,1},{9,13},{13,9},{2,6},{6,2},{1... | collective-permute-start | bytes 786440 | tf_op jit(solution)/shard_map/ppermute | solution.py:204
  129.2 14.4 %collective-permute-start.32 = (f32[512,128]{1,0:T(8,128)S(1)}, f32[512,128]{1,0:T(8,128)}, u32[]{:S(2)}, u32[]{:S(2)}) collective-permute-start(f32[512,128]{1,0:T(8,128)S(1)} %add.143.token_ref), channel_id=1, source_target_pairs={{0,4},{4,0},{8,12},{12,8},{1,5},{5,1},{9,13},{13,9},{2,6},{6,2},{1... | collective-permute-start | bytes 786440 | tf_op jit(solution)/shard_map/ppermute | solution.py:204
  137.0 16.5 %collective-permute-start.26 = (f32[512,128]{1,0:T(8,128)S(1)}, f32[512,128]{1,0:T(8,128)S(1)}, u32[]{:S(2)}, u32[]{:S(2)}) collective-permute-start(f32[512,128]{1,0:T(8,128)S(1)} %add.139.token_ref), channel_id=1, source_target_pairs={{0,4},{4,0},{8,12},{12,8},{1,5},{5,1},{9,13},{13,9},{2,6},{6,2},{1... | collective-permute-start | bytes 786440 | tf_op jit(solution)/shard_map/ppermute | solution.py:204
  139.9 12.5 %collective-permute-start.29 = (f32[512,128]{1,0:T(8,128)S(1)}, f32[512,128]{1,0:T(8,128)S(1)}, u32[]{:S(2)}, u32[]{:S(2)}) collective-permute-start(f32[512,128]{1,0:T(8,128)S(1)} %add.141.token_ref), channel_id=1, source_target_pairs={{0,4},{4,0},{8,12},{12,8},{1,5},{5,1},{9,13},{13,9},{2,6},{6,2},{1... | collective-permute-start | bytes 786440 | tf_op jit(solution)/shard_map/ppermute | solution.py:204
  (69 other events, 333.2 us)

commit v2 on v1

v2 whole, which is shorter than its diff:
```python
import functools

import jax
import jax.numpy as jnp
from jax import lax
from jax.experimental import pallas as pl
from jax.experimental.pallas import tpu as pltpu
from jax.sharding import PartitionSpec as P

START = 100
DELTA = 1.0
LEARN_RATE = 0.05
BETA_ONE = 0.9
BETA_TWO = 0.999
EPSILON = 1e-08
F32, BF16 = jnp.float32, jnp.bfloat16
NT = (((1,), (1,)), ((), ()))
ROW_BLOCK = 256
UNIT = 128
TARGET = 384
LAG = 2


def adam_move(values, gradient, first_moment, square, counter):
    first_moment = BETA_ONE * first_moment + (1.0 - BETA_ONE) * gradient
    square = BETA_TWO * square + (1.0 - BETA_TWO) * gradient * gradient
    fixed_mean = first_moment / (1.0 - BETA_ONE**counter)
    fixed_square = square / (1.0 - BETA_TWO**counter)
    return (
        values - LEARN_RATE * fixed_mean / (jnp.sqrt(fixed_square) + EPSILON),
        first_moment,
        square,
    )


def split(values):
    high = values.astype(BF16)
    return high, (values - high.astype(F32)).astype(BF16)


def slopes_of(row_pair, col_pair, block):
    fitted = lax.dot_general(row_pair, col_pair, NT, preferred_element_type=F32)
    return jnp.clip(fitted - block.astype(F32), -DELTA, DELTA).astype(BF16)


def col_partial(twice_ref, turned_ref, col, mat_ref, first_col):
    col_pair = jnp.concatenate(split(col), axis=1)
    width, rank = col.shape
    total = None
    for at in range(0, mat_ref.shape[0], ROW_BLOCK):
        rows = pl.ds(at, ROW_BLOCK)
        slopes = slopes_of(twice_ref[rows, :], col_pair, mat_ref[rows, pl.ds(first_col, width)])
        term = jnp.dot(turned_ref[:, rows], slopes, preferred_element_type=F32)
        total = term if total is None else total + term
    return (total[:rank] + total[rank:]).T


def first_kernel(outer_ref, high_ref, row_ref, col_ref, mat_ref, twice_ref, pair_ref, turned_ref, out_ref):
    del outer_ref, high_ref
    high, low = split(row_ref[...])
    twice_ref[...] = jnp.concatenate([high, high], axis=1)
    pair_ref[...] = jnp.concatenate([high, low], axis=1)
    turned_ref[...] = jnp.concatenate([high.T, low.T], axis=0)
    out_ref[...] = col_partial(twice_ref, turned_ref, col_ref[: out_ref.shape[0], :], mat_ref, 0)


def pick(outer_ref, far_ref, near_ref):
    near = near_ref[...]
    return jnp.where(outer_ref[0] == 1, far_ref[: near.shape[0], :], near)


def fresh_kernel(at, token_ref, twice_ref, turned_ref, col_ref, mat_ref, out_ref):
    del token_ref
    width = out_ref.shape[0]
    col = col_ref[pl.ds(at, width), :]
    out_ref[...] = col_partial(twice_ref, turned_ref, col, mat_ref, at)


def middle_kernel(
    at, rows_total, token_ref, outer_ref, far_ref, near_ref, twice_ref, turned_ref, mat_ref, col_ref, mean_ref,
    square_ref, new_ref, new_mean_ref, new_square_ref, out_ref,
):
    del token_ref
    total = pick(outer_ref, far_ref, near_ref)
    own = pl.ds(at, out_ref.shape[0])
    new, new_mean_ref[...], new_square_ref[...] = adam_move(
        col_ref[own, :], total / rows_total, mean_ref[own, :], square_ref[own, :], START + 1
    )
    new_ref[...] = new
    out_ref[...] = col_partial(twice_ref, turned_ref, new, mat_ref, at)


def last_kernel(at, rows_total, begun, *refs):
    _, outer_ref, far_ref, near_ref, pair_ref, mat_ref, col_ref, mean_ref, square_ref, *grad_ref = refs[:-2]
    new_ref, out_ref = refs[-2:]
    total = pick(outer_ref, far_ref, near_ref)
    width, rank = total.shape
    own = pl.ds(at, width)
    new, _, _ = adam_move(
        col_ref[...], total / rows_total, mean_ref[...], square_ref[...], START + 2
    )
    new_ref[...] = new
    high, low = split(new)
    twice = jnp.concatenate([high, high], axis=1)
    pair = jnp.concatenate([high, low], axis=1)
    for at_row in range(0, mat_ref.shape[0], ROW_BLOCK):
        rows = pl.ds(at_row, ROW_BLOCK)
        slopes = slopes_of(pair_ref[rows, :], twice, mat_ref[rows, own])
        term = jnp.dot(slopes, pair, preferred_element_type=F32)
        term = term[:, :rank] + term[:, rank:]
        out_ref[rows, :] = grad_ref[0][rows, :] + term if begun else term


def store_kernel(token_ref, *refs):
    del token_ref
    *chunk_refs, out_hbm, done_ref, sems = refs
    done_ref[...] = jnp.zeros_like(done_ref)
    stores, at = [], 0
    for index, chunk_ref in enumerate(chunk_refs):
        target = out_hbm.at[pl.ds(at, chunk_ref.shape[0]), :]
        stores.append(pltpu.make_async_copy(chunk_ref, target, sems.at[index]))
        at += chunk_ref.shape[0]
    for store in stores:
        store.start()
    for store in stores:
        store.wait()


def halves_kernel(high_ref, grad_ref, keep_ref, send_ref):
    half = keep_ref.shape[0]
    keep_ref[...] = grad_ref[pl.ds(pl.multiple_of(high_ref[0] * half, half), half), :]
    send_ref[...] = grad_ref[pl.ds(pl.multiple_of((1 - high_ref[0]) * half, half), half), :]


def row_kernel(cols_total, token_ref, high_ref, part_ref, other_ref, row_ref, mean_ref, square_ref, new_ref):
    del token_ref
    half = part_ref.shape[0]
    own = pl.ds(pl.multiple_of(high_ref[0] * half, half), half)
    gradient = (part_ref[...] + other_ref[...]) / cols_total
    new_ref[...], _, _ = adam_move(row_ref[own, :], gradient, mean_ref[own, :], square_ref[own, :], START + 1)


def join_kernel(high_ref, new_ref, other_ref, out_hbm, sems):
    half = new_ref.shape[0]
    own = pl.multiple_of(high_ref[0] * half, half)
    far = pl.multiple_of((1 - high_ref[0]) * half, half)
    stores = [
        pltpu.make_async_copy(new_ref, out_hbm.at[pl.ds(own, half), :], sems.at[0]),
        pltpu.make_async_copy(other_ref, out_hbm.at[pl.ds(far, half), :], sems.at[1]),
    ]
    for store in stores:
        store.start()
    for store in stores:
        store.wait()


VMEM = pl.BlockSpec(memory_space=pltpu.VMEM)
SMEM = pl.BlockSpec(memory_space=pltpu.SMEM)
ANY = pl.BlockSpec(memory_space=pl.ANY)
HBM = pl.BlockSpec(memory_space=pltpu.HBM)


def call(kernel, name, ins, outs, scratch=(), aliases=None):
    return pl.pallas_call(
        kernel,
        out_shape=[jax.ShapeDtypeStruct(shape, kind) for _, shape, kind in outs],
        in_specs=[spec for spec, _ in ins],
        out_specs=[spec for spec, _, _ in outs],
        scratch_shapes=scratch,
        input_output_aliases=aliases or {},
        compiler_params=pltpu.CompilerParams(vmem_limit_bytes=4 << 20),
        cost_estimate=pl.CostEstimate(flops=1, bytes_accessed=1, transcendentals=0),
        name=name,
    )(*[array for _, array in ins])


def chunks_of(columns):
    if columns % UNIT:
        return [(0, columns)]
    widths = [TARGET] * (columns // TARGET)
    if columns % TARGET:
        widths.append(columns % TARGET)
    return [(sum(widths[:index]), width) for index, width in enumerate(widths)]


class Work:
    def __init__(self, outer, high, matrix, row_factor, col_factor, col_mean, col_square, rows_total):
        self.outer, self.high, self.rows_total = outer, high, rows_total
        self.matrix, self.row = matrix, row_factor
        self.state = [col_factor, col_mean, col_square]
        self.rank = col_factor.shape[1]
        self.chunks = chunks_of(col_factor.shape[0])
        self.moved = {}
        self.new = {}
        self.grad = None

    def chunk(self, index):
        return (VMEM, (self.chunks[index][1], self.rank), F32)

    def first(self):
        rows, rank = self.row.shape
        width = self.chunks[0][1]
        wide = (VMEM, (rows, 2 * rank), BF16)
        self.twice, self.pair, self.turned, out = call(
            first_kernel, "first",
            [(SMEM, self.outer), (SMEM, self.high), (VMEM, self.row)]
            + [(VMEM, self.state[0][:width]), (VMEM, self.matrix[:, :width])],
            [wide, wide, (VMEM, (2 * rank, rows), BF16), self.chunk(0)],
        )
        return out

    def fresh(self, index, token):
        (out,) = call(
            functools.partial(fresh_kernel, self.chunks[index][0]), "fresh",
            [(ANY, token), (VMEM, self.twice), (VMEM, self.turned), (VMEM, self.state[0]), (VMEM, self.matrix)],
            [self.chunk(index)],
        )
        return out

    def middle(self, index, far, near, token):
        *self.moved[index], out = call(
            functools.partial(middle_kernel, self.chunks[index][0], self.rows_total), "middle",
            [(ANY, token), (SMEM, self.outer), (VMEM, far), (VMEM, near), (VMEM, self.twice), (VMEM, self.turned)]
            + [(VMEM, array) for array in (self.matrix, *self.state)],
            [self.chunk(index)] * 4,
        )
        return out

    def last(self, index, far, near, token):
        ins = [(ANY, token), (SMEM, self.outer), (VMEM, far), (VMEM, near), (VMEM, self.pair)]
        ins += [(VMEM, array) for array in (self.matrix, *self.moved[index])]
        begun = self.grad is not None
        if begun:
            ins += [(VMEM, self.grad)]
        self.new[index], self.grad = call(
            functools.partial(last_kernel, self.chunks[index][0], self.rows_total, begun), "last",
            ins,
            [self.chunk(index), (VMEM, self.row.shape, F32)],
            aliases={9: 1} if begun else None,
        )

    def new_cols(self, token):
        return call(
            store_kernel, "store",
            [(ANY, token)] + [(VMEM, self.new[index]) for index in range(len(self.chunks))],
            [(HBM, self.state[0].shape, F32), (VMEM, (8, self.rank), F32)],
            scratch=[pltpu.SemaphoreType.DMA((len(self.chunks),))],
        )


def plain_columns(work):
    every = range(len(work.chunks))
    sums = [lax.psum(work.first(), "row")]
    for index in every[1:]:
        sums.append(lax.psum(work.fresh(index, sums[0]), "row"))
    sums = [lax.psum(work.middle(index, sums[index], sums[index], sums[index]), "row") for index in every]
    for index in every:
        work.last(index, sums[index], sums[index], sums[index])


def join_sums_kernel(token_ref, own_ref, arrived_ref, out_ref):
    del token_ref
    out_ref[...] = own_ref[...] + arrived_ref[: out_ref.shape[0], :]


def merge_kernel(which, outer_ref, token_ref, *refs):
    del token_ref
    refs = dict(zip(which, refs, strict=True))
    outer = outer_ref[0] == 1
    if "whole" in refs:
        whole = refs["joined"][...] + refs["from_inner"][...]
        refs["whole"][...] = whole
        if "payload" in refs:
            own = refs["own"][...]
            low, high = sorted((own.shape[0], whole.shape[0]))
            refs["payload"][:low, :] = jnp.where(outer, own[:low], whole[:low])
            if high > low:
                refs["payload"][low:, :] = own[low:] if own.shape[0] == high else whole[low:]
    elif "payload" in refs:
        refs["payload"][...] = refs["own"][...]


def line_columns(work):
    n_col = lax.axis_size("col")
    outer_pairs = [(0, 1), (1, 0), (2, 3), (3, 2)]
    inner_pairs = []
    for col in range(n_col):
        inner_pairs += [(n_col + col, 2 * n_col + col), (2 * n_col + col, n_col + col)]
        inner_pairs += [(at * n_col + col, at * n_col + (col ^ 1)) for at in (0, 3)]
    chunks = len(work.chunks)
    slots = 2 * chunks
    own, joined, whole, from_outer, from_inner = {}, {}, {}, {}, {}
    own[0] = work.first()
    token = own[0]
    for k in range(slots + 3 * LAG):
        here, then, done = k - LAG, k - 2 * LAG, k - 3 * LAG
        if 0 <= here < slots:
            (joined[here],) = call(
                join_sums_kernel, "sum",
                [(ANY, token), (VMEM, own[here]), (VMEM, from_outer[here])],
                [work.chunk(here % chunks)],
            )
            token = joined[here]
            from_inner[k] = lax.ppermute(joined[here], ("row", "col"), inner_pairs)
        ins, outs = {}, {}
        if 0 <= then < slots:
            ins["joined"], ins["from_inner"] = joined[then], from_inner[here]
            outs["whole"] = work.chunk(then % chunks)
            if k < slots:
                ins["own"] = own[k]
                outs["payload"] = max(work.chunk(then % chunks), work.chunk(k % chunks), key=lambda o: o[1])
        if k < 2 * LAG:
            ins["own"], outs["payload"] = own[k], work.chunk(k)
        if outs:
            got = call(
                functools.partial(merge_kernel, [*ins, *outs]), "merge",
                [(SMEM, work.outer), (ANY, token)] + [(VMEM, array) for array in ins.values()],
                [*outs.values()],
            )
            got = dict(zip(outs, got, strict=True))
            token = got[[*outs][-1]]
            if "whole" in got:
                whole[then] = got["whole"]
        if k < slots + 2 * LAG:
            payload = got["payload"] if k < slots else whole[then]
            from_outer[k] = lax.ppermute(payload, "row", outer_pairs)
        nxt = k + 1
        if nxt < chunks:
            token = own[nxt] = work.fresh(nxt, token)
        elif nxt < slots:
            at = nxt - chunks
            token = own[nxt] = work.middle(at, from_outer[at + 2 * LAG], whole[at], token)
        if done >= chunks:
            work.last(done - chunks, from_outer[done + 2 * LAG], whole[done], token)
            token = work.grad


def row_step(work, row_mean, row_square, cols_total):
    high, grad = work.high, work.grad
    rows, rank = grad.shape
    half = (VMEM, (rows // 2, rank), F32)
    swap = [(0, 1), (1, 0), (2, 3), (3, 2)]
    across = [(0, 2), (2, 0), (1, 3), (3, 1)]
    keep, send = call(halves_kernel, "halves", [(SMEM, high), (VMEM, grad)], [half, half])
    part = keep + lax.ppermute(send, "col", swap)
    other = lax.ppermute(part, "col", across)
    new_cols, stored = work.new_cols(part)
    ins = [(VMEM, array) for array in (part, other, work.row, row_mean, row_square)]
    (new,) = call(
        functools.partial(row_kernel, cols_total), "row", [(ANY, stored), (SMEM, high), *ins], [half]
    )
    other = lax.ppermute(new, "col", swap)
    (out,) = call(
        join_kernel, "join",
        [(SMEM, high), (VMEM, new), (VMEM, other)],
        [(HBM, grad.shape, F32)],
        scratch=[pltpu.SemaphoreType.DMA((2,))],
    )
    return out, new_cols


def on_device(matrix, row_factor, col_factor, row_mean, row_square, col_mean, col_square):
    n_row = lax.axis_size("row")
    n_col = lax.axis_size("col")
    row, col = lax.axis_index("row"), lax.axis_index("col")
    outer = ((row == 0) | (row == n_row - 1)).astype(jnp.int32).reshape(1)
    high = (col & 1).astype(jnp.int32).reshape(1)
    work = Work(outer, high, matrix, row_factor, col_factor, col_mean, col_square, matrix.shape[0] * n_row)
    if n_row == 4 and n_col % 2 == 0:
        line_columns(work)
    else:
        plain_columns(work)
    cols_total = matrix.shape[1] * n_col
    if n_col == 4:
        new_rows, new_cols = row_step(work, row_mean, row_square, cols_total)
    else:
        new_cols, _ = work.new_cols(work.grad)
        summed = lax.psum(work.grad, "col")
        new_rows, _, _ = adam_move(row_factor, summed / cols_total, row_mean, row_square, START + 1)
    return new_rows, new_cols


def solution(mesh):
    return jax.shard_map(
        on_device,
        mesh=mesh,
        in_specs=(
            P(("grp", "row"), "col"),
            P(("grp", "row"), None),
            P(("grp", "col"), None),
            P(("grp", "row"), None),
            P(("grp", "row"), None),
            P(("grp", "col"), None),
            P(("grp", "col"), None),
        ),
        out_specs=(P(("grp", "row"), None), P(("grp", "col"), None)),
        check_vma=False,
    )
```

time: 168 us -> 133 us (0.79)
  waiting for transfers between devices: 68.9 us -> 44.4 us
  other arithmetic: 13.6 us -> 0.03 us
  Pallas kernels: 30.6 us -> 40.3 us
  local copies, waits for them, and re-layouts: 17.8 us -> 8.91 us
  starting transfers between devices: 34.6 us -> 37.5 us
    ppermute x20 -> x26, waiting for transfers between devices: 59.2 us -> 35.8 us  [line_columns(): from_outer[k] = lax.ppermute(payload, 'row', outer_pairs)]
    pallas_call x24 -> x85, Pallas kernels: 30.6 us -> 40.3 us  [call(): pl.pallas_call(kernel, out_shape=[jax.ShapeDtypeStruct(shape, kind) for _...]
    unnamed x131 -> x20, local copies, waits for them, and re-layouts: 15.3 us -> 6.61 us
    select_n x22 -> x0, other arithmetic: 6.31 us -> none  [the longest x8 3.63 us: line_columns(): total = jnp.where(outer, from_outer[done + 2 * LAG], whole[done])]
    add x17 -> x1, other arithmetic: 6.19 us -> 0.03 us  [row_step(): part = keep + lax.ppermute(send, 'col', swap)]
    ppermute x20 -> x26, starting transfers between devices: 30.5 us -> 35.6 us  [line_columns(): from_outer[k] = lax.ppermute(payload, 'row', outer_pairs)]
    ppermute x18 -> x24, starting transfers between devices: 4.02 us -> 1.88 us  [the longest x1 1.56 us: row_step(): other = lax.ppermute(part, 'col', across)]
    ppermute x18 -> x24, waiting for transfers between devices: 8.29 us -> 7.03 us  [the longest x1 5.45 us: row_step(): other = lax.ppermute(part, 'col', across)]
  transfers between devices with their start and end apart: 39 -> 51, of which waited for: 14 -> 23; matrix products, arithmetic and copies ran while one was open for 7% -> 0% of each run, Pallas kernels for 17% -> 28%
where the time goes in v2:
time: 133 us
  waiting for transfers between devices  44.4 us (33%)
  Pallas kernels  40.3 us (30%)
  starting transfers between devices  37.5 us (28%)
  local copies, waits for them, and re-layouts  8.91 us (7%)
  between operations  1.62 us (1%)
    pallas_call x85, Pallas kernels, call(): pl.pallas_call(kernel, out_shape=[jax.ShapeDtypeStruct(shape, kind) for _...  40.3 us
    ppermute x26, waiting for transfers between devices, line_columns(): from_outer[k] = lax.ppermute(payload, 'row', outer_pairs)  35.8 us
    ppermute x26, starting transfers between devices, line_columns(): from_outer[k] = lax.ppermute(payload, 'row', outer_pairs)  35.6 us
    unnamed x20, local copies, waits for them, and re-layouts  6.61 us
    ppermute x1, waiting for transfers between devices, row_step(): other = lax.ppermute(part, 'col', across)  5.45 us
  transfers between devices with their start and end apart: 51, of which 23 were waited for; matrix products, arithmetic and copies ran while one was open for 0% of the time, Pallas kernels for 28%

profile of v2, /device:TPU:0, one launch (start us, length us, event | category | flops | bytes accessed | tf_op | source)
XLA Modules:
  0.0 132.8 jit_solution(896861907844312063)
XLA Ops:
  5.2 3.1 %collective-permute-start = (f32[384,128]{1,0:T(8,128)S(1)}, f32[384,128]{1,0:T(8,128)S(1)}, u32[]{:S(2)}, u32[]{:S(2)}) collective-permute-start(f32[384,128]{1,0:T(8,128)S(1)} %merge.26.token_ref), channel_id=1, source_target_pairs={{0,4},{4,0},{8,12},{12,8},{1,5},{5,1},{9,13},{13,9},{2,6},{6,2},{1... | collective-permute-start | bytes 589832 | tf_op jit(solution)/shard_map/ppermute | solution.py:326
  8.3 3.4 %copy-done = bf16[1024,4096]{1,0:T(8,128)(2,1)S(1)} copy-done((bf16[1024,4096]{1,0:T(8,128)(2,1)S(1)}, bf16[1024,4096]{1,0:T(8,128)(2,1)}, u32[]{:S(2)}) %copy-start) | copy-done | bytes 8388632
  13.0 2.1 %copy-done.1 = bf16[1024,4096]{1,0:T(8,128)(2,1)S(1)} copy-done((bf16[1024,4096]{1,0:T(8,128)(2,1)S(1)}, bf16[1024,4096]{1,0:T(8,128)(2,1)}, u32[]{:S(2)}) %copy-start.1) | copy-done | bytes 8388632
  17.7 2.4 %collective-permute-done.1.arrived_ref = f32[384,128]{1,0:T(8,128)S(1)} collective-permute-done((f32[384,128]{1,0:T(8,128)S(1)}, f32[384,128]{1,0:T(8,128)S(1)}, u32[]{:S(2)}, u32[]{:S(2)}) %collective-permute-start.1) | collective-permute-done | bytes 196640 | tf_op jit(solution)/shard_map/ppermute | solution.py:326
  22.5 1.8 %collective-permute-done.2.arrived_ref = f32[384,128]{1,0:T(8,128)S(1)} collective-permute-done((f32[384,128]{1,0:T(8,128)S(1)}, f32[384,128]{1,0:T(8,128)S(1)}, u32[]{:S(2)}, u32[]{:S(2)}) %collective-permute-start.2) | collective-permute-done | bytes 196640 | tf_op jit(solution)/shard_map/ppermute | solution.py:326
  26.3 2.2 %collective-permute-done.4.arrived_ref = f32[384,128]{1,0:T(8,128)S(1)} collective-permute-done((f32[384,128]{1,0:T(8,128)S(1)}, f32[384,128]{1,0:T(8,128)S(1)}, u32[]{:S(2)}, u32[]{:S(2)}) %collective-permute-start.4) | collective-permute-done | bytes 196640 | tf_op jit(solution)/shard_map/ppermute | solution.py:326
  30.9 1.8 %collective-permute-done.6.arrived_ref.far_ref = f32[384,128]{1,0:T(8,128)S(1)} collective-permute-done((f32[384,128]{1,0:T(8,128)S(1)}, f32[384,128]{1,0:T(8,128)S(1)}, u32[]{:S(2)}, u32[]{:S(2)}) %collective-permute-start.6) | collective-permute-done | bytes 196640 | tf_op jit(solution)/shard_map/ppermute | solution.py:326
  35.1 1.8 %collective-permute-done.8.arrived_ref.far_ref = f32[384,128]{1,0:T(8,128)S(1)} collective-permute-done((f32[384,128]{1,0:T(8,128)S(1)}, f32[384,128]{1,0:T(8,128)S(1)}, u32[]{:S(2)}, u32[]{:S(2)}) %collective-permute-start.8) | collective-permute-done | bytes 196640 | tf_op jit(solution)/shard_map/ppermute | solution.py:326
  39.3 1.8 %collective-permute-done.10.arrived_ref.far_ref = f32[384,128]{1,0:T(8,128)S(1)} collective-permute-done((f32[384,128]{1,0:T(8,128)S(1)}, f32[384,128]{1,0:T(8,128)S(1)}, u32[]{:S(2)}, u32[]{:S(2)}) %collective-permute-start.10) | collective-permute-done | bytes 196640 | tf_op jit(solution)/shard_map/ppermute | solution.py:326
  43.5 1.8 %collective-permute-done.12.arrived_ref.far_ref = f32[384,128]{1,0:T(8,128)S(1)} collective-permute-done((f32[384,128]{1,0:T(8,128)S(1)}, f32[384,128]{1,0:T(8,128)S(1)}, u32[]{:S(2)}, u32[]{:S(2)}) %collective-permute-start.12) | collective-permute-done | bytes 196640 | tf_op jit(solution)/shard_map/ppermute | solution.py:326
  47.3 2.2 %collective-permute-done.14.arrived_ref.far_ref = f32[384,128]{1,0:T(8,128)S(1)} collective-permute-done((f32[384,128]{1,0:T(8,128)S(1)}, f32[384,128]{1,0:T(8,128)S(1)}, u32[]{:S(2)}, u32[]{:S(2)}) %collective-permute-start.14) | collective-permute-done | bytes 196640 | tf_op jit(solution)/shard_map/ppermute | solution.py:326
  50.8 1.5 %middle.11 = (f32[384,128]{1,0:T(8,128)S(1)}, f32[384,128]{1,0:T(8,128)S(1)}, f32[384,128]{1,0:T(8,128)S(1)}, f32[384,128]{1,0:T(8,128)S(1)}) custom-call(f32[384,128]{1,0:T(8,128)S(1)} %get-tuple-element.121.token_ref, s32[1]{0:T(128)} %bitcast.1.outer_ref.refs_1_, f32[384,128]{1,0:T(8,128)S(1)} %collective-permute-done.6.arrived_ref.far_ref, ...), custom_call_target="tpu_custom_call" | custom-call | flops 1 | bytes 1 | tf_op jit(solution)/shard_map/middle/pallas_call | solution.py:164
  52.2 1.5 %collective-permute-done.16.arrived_ref.far_ref = f32[384,128]{1,0:T(8,128)S(1)} collective-permute-done((f32[384,128]{1,0:T(8,128)S(1)}, f32[384,128]{1,0:T(8,128)S(1)}, u32[]{:S(2)}, u32[]{:S(2)}) %collective-permute-start.16) | collective-permute-done | bytes 196640 | tf_op jit(solution)/shard_map/ppermute | solution.py:326
  53.9 1.5 %collective-permute-start.20 = (f32[384,128]{1,0:T(8,128)S(1)}, f32[384,128]{1,0:T(8,128)S(1)}, u32[]{:S(2)}, u32[]{:S(2)}) collective-permute-start(f32[384,128]{1,0:T(8,128)S(1)} %get-tuple-element.124.token_ref), channel_id=1, source_target_pairs={{0,4},{4,0},{8,12},{12,8},{1,5},{5,1},{9,13},{13,9},{2,6},{6,2},{1... | collective-permute-start | bytes 589832 | tf_op jit(solution)/shard_map/ppermute | solution.py:326
  60.3 1.9 %collective-permute-done.20.arrived_ref.far_ref = f32[384,128]{1,0:T(8,128)S(1)} collective-permute-done((f32[384,128]{1,0:T(8,128)S(1)}, f32[384,128]{1,0:T(8,128)S(1)}, u32[]{:S(2)}, u32[]{:S(2)}) %collective-permute-start.20) | collective-permute-done | bytes 196640 | tf_op jit(solution)/shard_map/ppermute | solution.py:326
  64.6 1.8 %collective-permute-done.22.arrived_ref.far_ref = f32[384,128]{1,0:T(8,128)S(1)} collective-permute-done((f32[384,128]{1,0:T(8,128)S(1)}, f32[384,128]{1,0:T(8,128)S(1)}, u32[]{:S(2)}, u32[]{:S(2)}) %collective-permute-start.22) | collective-permute-done | bytes 196640 | tf_op jit(solution)/shard_map/ppermute | solution.py:326
  68.7 1.9 %collective-permute-done.24.arrived_ref.far_ref = f32[384,128]{1,0:T(8,128)S(1)} collective-permute-done((f32[384,128]{1,0:T(8,128)S(1)}, f32[384,128]{1,0:T(8,128)S(1)}, u32[]{:S(2)}, u32[]{:S(2)}) %collective-permute-start.24) | collective-permute-done | bytes 196640 | tf_op jit(solution)/shard_map/ppermute | solution.py:326
  72.9 1.9 %collective-permute-done.26.arrived_ref.far_ref = f32[384,128]{1,0:T(8,128)S(1)} collective-permute-done((f32[384,128]{1,0:T(8,128)S(1)}, f32[384,128]{1,0:T(8,128)S(1)}, u32[]{:S(2)}, u32[]{:S(2)}) %collective-permute-start.26) | collective-permute-done | bytes 196640 | tf_op jit(solution)/shard_map/ppermute | solution.py:326
  77.1 1.9 %collective-permute-done.28.arrived_ref.refs_2_ = f32[384,128]{1,0:T(8,128)S(1)} collective-permute-done((f32[384,128]{1,0:T(8,128)S(1)}, f32[384,128]{1,0:T(8,128)S(1)}, u32[]{:S(2)}, u32[]{:S(2)}) %collective-permute-start.28) | collective-permute-done | bytes 196640 | tf_op jit(solution)/shard_map/ppermute | solution.py:326
  83.3 1.8 %collective-permute-start.34 = (f32[384,128]{1,0:T(8,128)S(1)}, f32[384,128]{1,0:T(8,128)S(1)}, u32[]{:S(2)}, u32[]{:S(2)}) collective-permute-start(f32[384,128]{1,0:T(8,128)S(1)} %get-tuple-element.151.token_ref), channel_id=1, source_target_pairs={{0,4},{4,0},{8,12},{12,8},{1,5},{5,1},{9,13},{13,9},{2,6},{6,2},{1... | collective-permute-start | bytes 589832 | tf_op jit(solution)/shard_map/ppermute | solution.py:326
  87.7 1.9 %collective-permute-start.36 = (f32[384,128]{1,0:T(8,128)S(1)}, f32[384,128]{1,0:T(8,128)S(1)}, u32[]{:S(2)}, u32[]{:S(2)}) collective-permute-start(f32[384,128]{1,0:T(8,128)S(1)} %get-tuple-element.159.token_ref), channel_id=1, source_target_pairs={{0,4},{4,0},{8,12},{12,8},{1,5},{5,1},{9,13},{13,9},{2,6},{6,2},{1... | collective-permute-start | bytes 589832 | tf_op jit(solution)/shard_map/ppermute | solution.py:326
  91.9 1.6 %collective-permute-start.38 = (f32[384,128]{1,0:T(8,128)S(1)}, f32[384,128]{1,0:T(8,128)S(1)}, u32[]{:S(2)}, u32[]{:S(2)}) collective-permute-start(f32[384,128]{1,0:T(8,128)S(1)} %get-tuple-element.167.token_ref), channel_id=1, source_target_pairs={{0,4},{4,0},{8,12},{12,8},{1,5},{5,1},{9,13},{13,9},{2,6},{6,2},{1... | collective-permute-start | bytes 589832 | tf_op jit(solution)/shard_map/ppermute | solution.py:326
  95.4 1.7 %collective-permute-start.40 = (f32[384,128]{1,0:T(8,128)S(1)}, f32[384,128]{1,0:T(8,128)S(1)}, u32[]{:S(2)}, u32[]{:S(2)}) collective-permute-start(f32[384,128]{1,0:T(8,128)S(1)} %get-tuple-element.175.refs_0_), channel_id=1, source_target_pairs={{0,4},{4,0},{8,12},{12,8},{1,5},{5,1},{9,13},{13,9},{2,6},{6,2},{1... | collective-permute-start | bytes 589832 | tf_op jit(solution)/shard_map/ppermute | solution.py:326
  98.0 1.7 %collective-permute-done.38.arrived_ref.refs_2_ = f32[384,128]{1,0:T(8,128)S(1)} collective-permute-done((f32[384,128]{1,0:T(8,128)S(1)}, f32[384,128]{1,0:T(8,128)S(1)}, u32[]{:S(2)}, u32[]{:S(2)}) %collective-permute-start.38) | collective-permute-done | bytes 196640 | tf_op jit(solution)/shard_map/ppermute | solution.py:326
  99.8 3.6 %collective-permute-start.43 = (f32[384,128]{1,0:T(8,128)S(1)}, f32[384,128]{1,0:T(8,128)S(1)}, u32[]{:S(2)}, u32[]{:S(2)}) collective-permute-start(f32[384,128]{1,0:T(8,128)S(1)} %merge.48.refs_0_.refs_3_), channel_id=1, source_target_pairs={{0,4},{4,0},{8,12},{12,8},{1,5},{5,1},{9,13},{13,9},{2,6},{6,2},{1... | collective-permute-start | bytes 589832 | tf_op jit(solution)/shard_map/ppermute | solution.py:326
  104.5 3.2 %collective-permute-start.45 = (f32[384,128]{1,0:T(8,128)S(1)}, f32[384,128]{1,0:T(8,128)S(1)}, u32[]{:S(2)}, u32[]{:S(2)}) collective-permute-start(f32[384,128]{1,0:T(8,128)S(1)} %merge.49.refs_0_.refs_3_), channel_id=1, source_target_pairs={{0,4},{4,0},{8,12},{12,8},{1,5},{5,1},{9,13},{13,9},{2,6},{6,2},{1... | collective-permute-start | bytes 589832 | tf_op jit(solution)/shard_map/ppermute | solution.py:326
  108.6 1.7 %collective-permute-start.46 = (f32[384,128]{1,0:T(8,128)S(1)}, f32[384,128]{1,0:T(8,128)S(1)}, u32[]{:S(2)}, u32[]{:S(2)}) collective-permute-start(f32[384,128]{1,0:T(8,128)S(1)} %merge.50.refs_0_.refs_3_), channel_id=1, source_target_pairs={{0,4},{4,0},{8,12},{12,8},{1,5},{5,1},{9,13},{13,9},{2,6},{6,2},{1... | collective-permute-start | bytes 589832 | tf_op jit(solution)/shard_map/ppermute | solution.py:326
  114.4 3.2 %collective-permute-done.46.refs_2_ = f32[384,128]{1,0:T(8,128)S(1)} collective-permute-done((f32[384,128]{1,0:T(8,128)S(1)}, f32[384,128]{1,0:T(8,128)S(1)}, u32[]{:S(2)}, u32[]{:S(2)}) %collective-permute-start.46) | collective-permute-done | bytes 196640 | tf_op jit(solution)/shard_map/ppermute | solution.py:326
  120.0 1.5 %collective-permute-done.48 = f32[512,128]{1,0:T(8,128)S(1)} collective-permute-done((f32[512,128]{1,0:T(8,128)S(1)}, f32[512,128]{1,0:T(8,128)S(1)}, u32[]{:S(2)}, u32[]{:S(2)}) %collective-permute-start.48) | collective-permute-done | bytes 262176 | tf_op jit(solution)/shard_map/ppermute | solution.py:345
  121.6 1.6 %collective-permute-start.49 = (f32[512,128]{1,0:T(8,128)S(1)}, f32[512,128]{1,0:T(8,128)S(1)}, u32[]{:S(2)}, u32[]{:S(2)}) collective-permute-start(f32[512,128]{1,0:T(8,128)S(1)} %add.3.token_ref.part_ref), channel_id=1, source_target_pairs={{0,2},{2,0},{1,3},{3,1},{4,6},{6,4},{5,7},{7,5},{8,10},{10,8},{9,1... | collective-permute-start | bytes 786440 | tf_op jit(solution)/shard_map/ppermute | solution.py:346
  124.5 5.5 %collective-permute-done.49.other_ref = f32[512,128]{1,0:T(8,128)S(1)} collective-permute-done((f32[512,128]{1,0:T(8,128)S(1)}, f32[512,128]{1,0:T(8,128)S(1)}, u32[]{:S(2)}, u32[]{:S(2)}) %collective-permute-start.49) | collective-permute-done | bytes 262176 | tf_op jit(solution)/shard_map/ppermute | solution.py:346
  130.3 1.5 %collective-permute-done.50.other_ref = f32[512,128]{1,0:T(8,128)S(1)} collective-permute-done((f32[512,128]{1,0:T(8,128)S(1)}, f32[512,128]{1,0:T(8,128)S(1)}, u32[]{:S(2)}, u32[]{:S(2)}) %collective-permute-start.50) | collective-permute-done | bytes 262176 | tf_op jit(solution)/shard_map/ppermute | solution.py:352
  (178 shorter events, 62.2 us)
Async XLA Ops:
  5.2 11.0 %collective-permute-start = (f32[384,128]{1,0:T(8,128)S(1)}, f32[384,128]{1,0:T(8,128)S(1)}, u32[]{:S(2)}, u32[]{:S(2)}) collective-permute-start(f32[384,128]{1,0:T(8,128)S(1)} %merge.26.token_ref), channel_id=1, source_target_pairs={{0,4},{4,0},{8,12},{12,8},{1,5},{5,1},{9,13},{13,9},{2,6},{6,2},{1... | collective-permute-start | bytes 589832 | tf_op jit(solution)/shard_map/ppermute | solution.py:326
  16.3 7.9 %collective-permute-start.2 = (f32[384,128]{1,0:T(8,128)S(1)}, f32[384,128]{1,0:T(8,128)S(1)}, u32[]{:S(2)}, u32[]{:S(2)}) collective-permute-start(f32[384,128]{1,0:T(8,128)S(1)} %merge.28.token_ref), channel_id=1, source_target_pairs={{0,4},{4,0},{8,12},{12,8},{1,5},{5,1},{9,13},{13,9},{2,6},{6,2},{1... | collective-permute-start | bytes 589832 | tf_op jit(solution)/shard_map/ppermute | solution.py:326
  16.4 7.9 %collective-permute-start.3 = (f32[384,128]{1,0:T(8,128)S(1)}, f32[384,128]{1,0:T(8,128)S(1)}, u32[]{:S(2)}, u32[]{:S(2)}) collective-permute-start(f32[384,128]{1,0:T(8,128)S(1)} %sum.22.token_ref.refs_0_), channel_id=1, source_target_pairs={{4,8},{8,4},{0,1},{12,13},{5,9},{9,5},{1,0},{13,12},{6,10},{10,6},... | collective-permute-start | bytes 589832 | tf_op jit(solution)/shard_map/ppermute | solution.py:304
  20.1 8.4 %collective-permute-start.4 = (f32[384,128]{1,0:T(8,128)S(1)}, f32[384,128]{1,0:T(8,128)S(1)}, u32[]{:S(2)}, u32[]{:S(2)}) collective-permute-start(f32[384,128]{1,0:T(8,128)S(1)} %merge.29.token_ref), channel_id=1, source_target_pairs={{0,4},{4,0},{8,12},{12,8},{1,5},{5,1},{9,13},{13,9},{2,6},{6,2},{1... | collective-permute-start | bytes 589832 | tf_op jit(solution)/shard_map/ppermute | solution.py:326
  24.4 8.3 %collective-permute-start.6 = (f32[384,128]{1,0:T(8,128)S(1)}, f32[384,128]{1,0:T(8,128)S(1)}, u32[]{:S(2)}, u32[]{:S(2)}) collective-permute-start(f32[384,128]{1,0:T(8,128)S(1)} %get-tuple-element.115.token_ref), channel_id=1, source_target_pairs={{0,4},{4,0},{8,12},{12,8},{1,5},{5,1},{9,13},{13,9},{2,6},{6,2},{1... | collective-permute-start | bytes 589832 | tf_op jit(solution)/shard_map/ppermute | solution.py:326
  25.1 7.6 %collective-permute-start.7 = (f32[384,128]{1,0:T(8,128)S(1)}, f32[384,128]{1,0:T(8,128)S(1)}, u32[]{:S(2)}, u32[]{:S(2)}) collective-permute-start(f32[384,128]{1,0:T(8,128)S(1)} %sum.24.token_ref.refs_0_), channel_id=1, source_target_pairs={{4,8},{8,4},{0,1},{12,13},{5,9},{9,5},{1,0},{13,12},{6,10},{10,6},... | collective-permute-start | bytes 589832 | tf_op jit(solution)/shard_map/ppermute | solution.py:304
  28.6 8.3 %collective-permute-start.8 = (f32[384,128]{1,0:T(8,128)S(1)}, f32[384,128]{1,0:T(8,128)S(1)}, u32[]{:S(2)}, u32[]{:S(2)}) collective-permute-start(f32[384,128]{1,0:T(8,128)S(1)} %get-tuple-element.116.token_ref), channel_id=1, source_target_pairs={{0,4},{4,0},{8,12},{12,8},{1,5},{5,1},{9,13},{13,9},{2,6},{6,2},{1... | collective-permute-start | bytes 589832 | tf_op jit(solution)/shard_map/ppermute | solution.py:326
  32.8 8.3 %collective-permute-start.10 = (f32[384,128]{1,0:T(8,128)S(1)}, f32[384,128]{1,0:T(8,128)S(1)}, u32[]{:S(2)}, u32[]{:S(2)}) collective-permute-start(f32[384,128]{1,0:T(8,128)S(1)} %get-tuple-element.117.token_ref), channel_id=1, source_target_pairs={{0,4},{4,0},{8,12},{12,8},{1,5},{5,1},{9,13},{13,9},{2,6},{6,2},{1... | collective-permute-start | bytes 589832 | tf_op jit(solution)/shard_map/ppermute | solution.py:326
  37.0 8.3 %collective-permute-start.12 = (f32[384,128]{1,0:T(8,128)S(1)}, f32[384,128]{1,0:T(8,128)S(1)}, u32[]{:S(2)}, u32[]{:S(2)}) collective-permute-start(f32[384,128]{1,0:T(8,128)S(1)} %get-tuple-element.118.token_ref), channel_id=1, source_target_pairs={{0,4},{4,0},{8,12},{12,8},{1,5},{5,1},{9,13},{13,9},{2,6},{6,2},{1... | collective-permute-start | bytes 589832 | tf_op jit(solution)/shard_map/ppermute | solution.py:326
  41.2 8.3 %collective-permute-start.14 = (f32[384,128]{1,0:T(8,128)S(1)}, f32[384,128]{1,0:T(8,128)S(1)}, u32[]{:S(2)}, u32[]{:S(2)}) collective-permute-start(f32[384,128]{1,0:T(8,128)S(1)} %get-tuple-element.119.token_ref), channel_id=1, source_target_pairs={{0,4},{4,0},{8,12},{12,8},{1,5},{5,1},{9,13},{13,9},{2,6},{6,2},{1... | collective-permute-start | bytes 589832 | tf_op jit(solution)/shard_map/ppermute | solution.py:326
  45.4 8.3 %collective-permute-start.16 = (f32[384,128]{1,0:T(8,128)S(1)}, f32[384,128]{1,0:T(8,128)S(1)}, u32[]{:S(2)}, u32[]{:S(2)}) collective-permute-start(f32[384,128]{1,0:T(8,128)S(1)} %get-tuple-element.120.token_ref), channel_id=1, source_target_pairs={{0,4},{4,0},{8,12},{12,8},{1,5},{5,1},{9,13},{13,9},{2,6},{6,2},{1... | collective-permute-start | bytes 589832 | tf_op jit(solution)/shard_map/ppermute | solution.py:326
  49.6 8.3 %collective-permute-start.18 = (f32[384,128]{1,0:T(8,128)S(1)}, f32[384,128]{1,0:T(8,128)S(1)}, u32[]{:S(2)}, u32[]{:S(2)}) collective-permute-start(f32[384,128]{1,0:T(8,128)S(1)} %get-tuple-element.121.token_ref), channel_id=1, source_target_pairs={{0,4},{4,0},{8,12},{12,8},{1,5},{5,1},{9,13},{13,9},{2,6},{6,2},{1... | collective-permute-start | bytes 589832 | tf_op jit(solution)/shard_map/ppermute | solution.py:326
  53.9 8.3 %collective-permute-start.20 = (f32[384,128]{1,0:T(8,128)S(1)}, f32[384,128]{1,0:T(8,128)S(1)}, u32[]{:S(2)}, u32[]{:S(2)}) collective-permute-start(f32[384,128]{1,0:T(8,128)S(1)} %get-tuple-element.124.token_ref), channel_id=1, source_target_pairs={{0,4},{4,0},{8,12},{12,8},{1,5},{5,1},{9,13},{13,9},{2,6},{6,2},{1... | collective-permute-start | bytes 589832 | tf_op jit(solution)/shard_map/ppermute | solution.py:326
  58.1 8.4 %collective-permute-start.22 = (f32[384,128]{1,0:T(8,128)S(1)}, f32[384,128]{1,0:T(8,128)S(1)}, u32[]{:S(2)}, u32[]{:S(2)}) collective-permute-start(f32[384,128]{1,0:T(8,128)S(1)} %get-tuple-element.127.token_ref), channel_id=1, source_target_pairs={{0,4},{4,0},{8,12},{12,8},{1,5},{5,1},{9,13},{13,9},{2,6},{6,2},{1... | collective-permute-start | bytes 589832 | tf_op jit(solution)/shard_map/ppermute | solution.py:326
  59.0 7.5 %collective-permute-start.23 = (f32[256,128]{1,0:T(8,128)S(1)}, f32[256,128]{1,0:T(8,128)S(1)}, u32[]{:S(2)}, u32[]{:S(2)}) collective-permute-start(f32[256,128]{1,0:T(8,128)S(1)} %sum.32.token_ref.refs_0_), channel_id=1, source_target_pairs={{4,8},{8,4},{0,1},{12,13},{5,9},{9,5},{1,0},{13,12},{6,10},{10,6},... | collective-permute-start | bytes 393224 | tf_op jit(solution)/shard_map/ppermute | solution.py:304
  62.3 8.3 %collective-permute-start.24 = (f32[384,128]{1,0:T(8,128)S(1)}, f32[384,128]{1,0:T(8,128)S(1)}, u32[]{:S(2)}, u32[]{:S(2)}) collective-permute-start(f32[384,128]{1,0:T(8,128)S(1)} %get-tuple-element.130.token_ref), channel_id=1, source_target_pairs={{0,4},{4,0},{8,12},{12,8},{1,5},{5,1},{9,13},{13,9},{2,6},{6,2},{1... | collective-permute-start | bytes 589832 | tf_op jit(solution)/shard_map/ppermute | solution.py:326
  66.5 8.3 %collective-permute-start.26 = (f32[384,128]{1,0:T(8,128)S(1)}, f32[384,128]{1,0:T(8,128)S(1)}, u32[]{:S(2)}, u32[]{:S(2)}) collective-permute-start(f32[384,128]{1,0:T(8,128)S(1)} %get-tuple-element.133.token_ref), channel_id=1, source_target_pairs={{0,4},{4,0},{8,12},{12,8},{1,5},{5,1},{9,13},{13,9},{2,6},{6,2},{1... | collective-permute-start | bytes 589832 | tf_op jit(solution)/shard_map/ppermute | solution.py:326
  70.7 8.3 %collective-permute-start.28 = (f32[384,128]{1,0:T(8,128)S(1)}, f32[384,128]{1,0:T(8,128)S(1)}, u32[]{:S(2)}, u32[]{:S(2)}) collective-permute-start(f32[384,128]{1,0:T(8,128)S(1)} %get-tuple-element.136.token_ref), channel_id=1, source_target_pairs={{0,4},{4,0},{8,12},{12,8},{1,5},{5,1},{9,13},{13,9},{2,6},{6,2},{1... | collective-permute-start | bytes 589832 | tf_op jit(solution)/shard_map/ppermute | solution.py:326
  71.6 7.5 %collective-permute-start.29 = (f32[384,128]{1,0:T(8,128)S(1)}, f32[384,128]{1,0:T(8,128)S(1)}, u32[]{:S(2)}, u32[]{:S(2)}) collective-permute-start(f32[384,128]{1,0:T(8,128)S(1)} %sum.35.token_ref.refs_0_), channel_id=1, source_target_pairs={{4,8},{8,4},{0,1},{12,13},{5,9},{9,5},{1,0},{13,12},{6,10},{10,6},... | collective-permute-start | bytes 589832 | tf_op jit(solution)/shard_map/ppermute | solution.py:304
  74.9 8.3 %collective-permute-start.30 = (f32[384,128]{1,0:T(8,128)S(1)}, f32[384,128]{1,0:T(8,128)S(1)}, u32[]{:S(2)}, u32[]{:S(2)}) collective-permute-start(f32[384,128]{1,0:T(8,128)S(1)} %get-tuple-element.139.token_ref), channel_id=1, source_target_pairs={{0,4},{4,0},{8,12},{12,8},{1,5},{5,1},{9,13},{13,9},{2,6},{6,2},{1... | collective-permute-start | bytes 589832 | tf_op jit(solution)/shard_map/ppermute | solution.py:326
  79.1 8.4 %collective-permute-start.32 = (f32[384,128]{1,0:T(8,128)S(1)}, f32[384,128]{1,0:T(8,128)S(1)}, u32[]{:S(2)}, u32[]{:S(2)}) collective-permute-start(f32[384,128]{1,0:T(8,128)S(1)} %get-tuple-element.142.token_ref), channel_id=1, source_target_pairs={{0,4},{4,0},{8,12},{12,8},{1,5},{5,1},{9,13},{13,9},{2,6},{6,2},{1... | collective-permute-start | bytes 589832 | tf_op jit(solution)/shard_map/ppermute | solution.py:326
  80.0 7.6 %collective-permute-start.33 = (f32[384,128]{1,0:T(8,128)S(1)}, f32[384,128]{1,0:T(8,128)S(1)}, u32[]{:S(2)}, u32[]{:S(2)}) collective-permute-start(f32[384,128]{1,0:T(8,128)S(1)} %sum.37.token_ref.refs_0_), channel_id=1, source_target_pairs={{4,8},{8,4},{0,1},{12,13},{5,9},{9,5},{1,0},{13,12},{6,10},{10,6},... | collective-permute-start | bytes 589832 | tf_op jit(solution)/shard_map/ppermute | solution.py:304
  83.3 8.5 %collective-permute-start.34 = (f32[384,128]{1,0:T(8,128)S(1)}, f32[384,128]{1,0:T(8,128)S(1)}, u32[]{:S(2)}, u32[]{:S(2)}) collective-permute-start(f32[384,128]{1,0:T(8,128)S(1)} %get-tuple-element.151.token_ref), channel_id=1, source_target_pairs={{0,4},{4,0},{8,12},{12,8},{1,5},{5,1},{9,13},{13,9},{2,6},{6,2},{1... | collective-permute-start | bytes 589832 | tf_op jit(solution)/shard_map/ppermute | solution.py:326
  87.7 7.7 %collective-permute-start.36 = (f32[384,128]{1,0:T(8,128)S(1)}, f32[384,128]{1,0:T(8,128)S(1)}, u32[]{:S(2)}, u32[]{:S(2)}) collective-permute-start(f32[384,128]{1,0:T(8,128)S(1)} %get-tuple-element.159.token_ref), channel_id=1, source_target_pairs={{0,4},{4,0},{8,12},{12,8},{1,5},{5,1},{9,13},{13,9},{2,6},{6,2},{1... | collective-permute-start | bytes 589832 | tf_op jit(solution)/shard_map/ppermute | solution.py:326
  91.9 7.8 %collective-permute-start.38 = (f32[384,128]{1,0:T(8,128)S(1)}, f32[384,128]{1,0:T(8,128)S(1)}, u32[]{:S(2)}, u32[]{:S(2)}) collective-permute-start(f32[384,128]{1,0:T(8,128)S(1)} %get-tuple-element.167.token_ref), channel_id=1, source_target_pairs={{0,4},{4,0},{8,12},{12,8},{1,5},{5,1},{9,13},{13,9},{2,6},{6,2},{1... | collective-permute-start | bytes 589832 | tf_op jit(solution)/shard_map/ppermute | solution.py:326
  95.4 8.9 %collective-permute-start.40 = (f32[384,128]{1,0:T(8,128)S(1)}, f32[384,128]{1,0:T(8,128)S(1)}, u32[]{:S(2)}, u32[]{:S(2)}) collective-permute-start(f32[384,128]{1,0:T(8,128)S(1)} %get-tuple-element.175.refs_0_), channel_id=1, source_target_pairs={{0,4},{4,0},{8,12},{12,8},{1,5},{5,1},{9,13},{13,9},{2,6},{6,2},{1... | collective-permute-start | bytes 589832 | tf_op jit(solution)/shard_map/ppermute | solution.py:326
  99.7 8.8 %collective-permute-start.42 = (f32[384,128]{1,0:T(8,128)S(1)}, f32[384,128]{1,0:T(8,128)S(1)}, u32[]{:S(2)}, u32[]{:S(2)}) collective-permute-start(f32[384,128]{1,0:T(8,128)S(1)} %sum.42.token_ref.refs_0_), channel_id=1, source_target_pairs={{4,8},{8,4},{0,1},{12,13},{5,9},{9,5},{1,0},{13,12},{6,10},{10,6},... | collective-permute-start | bytes 589832 | tf_op jit(solution)/shard_map/ppermute | solution.py:304
  99.8 10.4 %collective-permute-start.43 = (f32[384,128]{1,0:T(8,128)S(1)}, f32[384,128]{1,0:T(8,128)S(1)}, u32[]{:S(2)}, u32[]{:S(2)}) collective-permute-start(f32[384,128]{1,0:T(8,128)S(1)} %merge.48.refs_0_.refs_3_), channel_id=1, source_target_pairs={{0,4},{4,0},{8,12},{12,8},{1,5},{5,1},{9,13},{13,9},{2,6},{6,2},{1... | collective-permute-start | bytes 589832 | tf_op jit(solution)/shard_map/ppermute | solution.py:326
  104.5 9.0 %collective-permute-start.45 = (f32[384,128]{1,0:T(8,128)S(1)}, f32[384,128]{1,0:T(8,128)S(1)}, u32[]{:S(2)}, u32[]{:S(2)}) collective-permute-start(f32[384,128]{1,0:T(8,128)S(1)} %merge.49.refs_0_.refs_3_), channel_id=1, source_target_pairs={{0,4},{4,0},{8,12},{12,8},{1,5},{5,1},{9,13},{13,9},{2,6},{6,2},{1... | collective-permute-start | bytes 589832 | tf_op jit(solution)/shard_map/ppermute | solution.py:326
  108.6 9.1 %collective-permute-start.46 = (f32[384,128]{1,0:T(8,128)S(1)}, f32[384,128]{1,0:T(8,128)S(1)}, u32[]{:S(2)}, u32[]{:S(2)}) collective-permute-start(f32[384,128]{1,0:T(8,128)S(1)} %merge.50.refs_0_.refs_3_), channel_id=1, source_target_pairs={{0,4},{4,0},{8,12},{12,8},{1,5},{5,1},{9,13},{13,9},{2,6},{6,2},{1... | collective-permute-start | bytes 589832 | tf_op jit(solution)/shard_map/ppermute | solution.py:326
  111.2 7.9 %collective-permute-start.47 = (f32[256,128]{1,0:T(8,128)S(1)}, f32[256,128]{1,0:T(8,128)S(1)}, u32[]{:S(2)}, u32[]{:S(2)}) collective-permute-start(f32[256,128]{1,0:T(8,128)S(1)} %merge.51.refs_0_.refs_3_), channel_id=1, source_target_pairs={{0,4},{4,0},{8,12},{12,8},{1,5},{5,1},{9,13},{13,9},{2,6},{6,2},{1... | collective-permute-start | bytes 393224 | tf_op jit(solution)/shard_map/ppermute | solution.py:326
  121.6 8.4 %collective-permute-start.49 = (f32[512,128]{1,0:T(8,128)S(1)}, f32[512,128]{1,0:T(8,128)S(1)}, u32[]{:S(2)}, u32[]{:S(2)}) collective-permute-start(f32[512,128]{1,0:T(8,128)S(1)} %add.3.token_ref.part_ref), channel_id=1, source_target_pairs={{0,2},{2,0},{1,3},{3,1},{4,6},{6,4},{5,7},{7,5},{8,10},{10,8},{9,1... | collective-permute-start | bytes 786440 | tf_op jit(solution)/shard_map/ppermute | solution.py:346
  (28 other events, 177.5 us)

commit v3 on v2

--- a/solution.py
+++ b/solution.py
@@ -17,8 +17,10 @@
 NT = (((1,), (1,)), ((), ()))
 ROW_BLOCK = 256
 UNIT = 128
-TARGET = 384
-LAG = 2
+TARGET = 256
+OUTER_LAG = 3
+INNER_LAG = 2
+BATCH = 3
 
 
 def adam_move(values, gradient, first_moment, square, counter):
@@ -55,13 +57,32 @@
     return (total[:rank] + total[rank:]).T
 
 
-def first_kernel(outer_ref, high_ref, row_ref, col_ref, mat_ref, twice_ref, pair_ref, turned_ref, out_ref):
+def first_kernel(
+    outer_ref, high_ref, row_hbm, col_hbm, mat_hbm, twice_ref, pair_ref, turned_ref, col_ref, mat_ref, out_ref,
+    row_ref, sems,
+):
     del outer_ref, high_ref
+    width, columns = out_ref.shape[0], mat_ref.shape[1]
+    loads = [
+        pltpu.make_async_copy(row_hbm, row_ref, sems.at[0]),
+        pltpu.make_async_copy(mat_hbm.at[:, pl.ds(0, width)], mat_ref.at[:, pl.ds(0, width)], sems.at[1]),
+        pltpu.make_async_copy(col_hbm, col_ref, sems.at[2]),
+    ]
+    if width < columns:
+        rest = pl.ds(width, columns - width)
+        loads.append(pltpu.make_async_copy(mat_hbm.at[:, rest], mat_ref.at[:, rest], sems.at[3]))
+    for load in loads:
+        load.start()
+    loads[0].wait()
     high, low = split(row_ref[...])
     twice_ref[...] = jnp.concatenate([high, high], axis=1)
     pair_ref[...] = jnp.concatenate([high, low], axis=1)
     turned_ref[...] = jnp.concatenate([high.T, low.T], axis=0)
-    out_ref[...] = col_partial(twice_ref, turned_ref, col_ref[: out_ref.shape[0], :], mat_ref, 0)
+    loads[1].wait()
+    loads[2].wait()
+    out_ref[...] = col_partial(twice_ref, turned_ref, col_ref[:width, :], mat_ref, 0)
+    for load in loads[3:]:
+        load.wait()
 
 
 def pick(outer_ref, far_ref, near_ref):
@@ -90,25 +111,25 @@
     out_ref[...] = col_partial(twice_ref, turned_ref, new, mat_ref, at)
 
 
-def last_kernel(at, rows_total, begun, *refs):
-    _, outer_ref, far_ref, near_ref, pair_ref, mat_ref, col_ref, mean_ref, square_ref, *grad_ref = refs[:-2]
-    new_ref, out_ref = refs[-2:]
-    total = pick(outer_ref, far_ref, near_ref)
-    width, rank = total.shape
-    own = pl.ds(at, width)
-    new, _, _ = adam_move(
-        col_ref[...], total / rows_total, mean_ref[...], square_ref[...], START + 2
-    )
-    new_ref[...] = new
-    high, low = split(new)
+def last_kernel(at, rows_total, count, token_ref, outer_ref, pair_ref, mat_ref, *refs):
+    del token_ref
+    out_ref, grad_ref, news = refs[-1], refs[5 * count : -1 - count], []
+    for index in range(count):
+        far_ref, near_ref, col_ref, mean_ref, square_ref = refs[5 * index : 5 * index + 5]
+        gradient = pick(outer_ref, far_ref, near_ref) / rows_total
+        new, _, _ = adam_move(col_ref[...], gradient, mean_ref[...], square_ref[...], START + 2)
+        refs[index - 1 - count][...] = new
+        news.append(new)
+    high, low = split(jnp.concatenate(news, axis=0))
     twice = jnp.concatenate([high, high], axis=1)
     pair = jnp.concatenate([high, low], axis=1)
+    width, rank = high.shape
     for at_row in range(0, mat_ref.shape[0], ROW_BLOCK):
         rows = pl.ds(at_row, ROW_BLOCK)
-        slopes = slopes_of(pair_ref[rows, :], twice, mat_ref[rows, own])
+        slopes = slopes_of(pair_ref[rows, :], twice, mat_ref[rows, pl.ds(at, width)])
         term = jnp.dot(slopes, pair, preferred_element_type=F32)
         term = term[:, :rank] + term[:, rank:]
-        out_ref[rows, :] = grad_ref[0][rows, :] + term if begun else term
+        out_ref[rows, :] = grad_ref[0][rows, :] + term if grad_ref else term
 
 
 def store_kernel(token_ref, *refs):
@@ -160,7 +181,7 @@
 HBM = pl.BlockSpec(memory_space=pltpu.HBM)
 
 
-def call(kernel, name, ins, outs, scratch=(), aliases=None):
+def call(kernel, name, ins, outs, scratch=(), aliases=None, room=4):
     return pl.pallas_call(
         kernel,
         out_shape=[jax.ShapeDtypeStruct(shape, kind) for _, shape, kind in outs],
@@ -168,10 +189,10 @@
         out_specs=[spec for spec, _, _ in outs],
         scratch_shapes=scratch,
         input_output_aliases=aliases or {},
-        compiler_params=pltpu.CompilerParams(vmem_limit_bytes=4 << 20),
+        compiler_params=pltpu.CompilerParams(vmem_limit_bytes=room << 20),
         cost_estimate=pl.CostEstimate(flops=1, bytes_accessed=1, transcendentals=0),
         name=name,
-    )(*[array for _, array in ins])
+    )(*[pltpu.with_memory_space_constraint(array, pltpu.HBM) if spec is HBM else array for spec, array in ins])
 
 
 def chunks_of(columns):
@@ -199,13 +220,15 @@
 
     def first(self):
         rows, rank = self.row.shape
-        width = self.chunks[0][1]
         wide = (VMEM, (rows, 2 * rank), BF16)
-        self.twice, self.pair, self.turned, out = call(
+        col = self.state[0]
+        self.twice, self.pair, self.turned, self.state[0], self.matrix, out = call(
             first_kernel, "first",
-            [(SMEM, self.outer), (SMEM, self.high), (VMEM, self.row)]
-            + [(VMEM, self.state[0][:width]), (VMEM, self.matrix[:, :width])],
-            [wide, wide, (VMEM, (2 * rank, rows), BF16), self.chunk(0)],
+            [(SMEM, self.outer), (SMEM, self.high), (HBM, self.row), (HBM, col), (HBM, self.matrix)],
+            [wide, wide, (VMEM, (2 * rank, rows), BF16)]
+            + [(VMEM, col.shape, F32), (VMEM, self.matrix.shape, BF16), self.chunk(0)],
+            scratch=[pltpu.VMEM(self.row.shape, F32), pltpu.SemaphoreType.DMA((4,))],
+            room=4,
         )
         return out
 
@@ -226,18 +249,21 @@
         )
         return out
 
-    def last(self, index, far, near, token):
-        ins = [(ANY, token), (SMEM, self.outer), (VMEM, far), (VMEM, near), (VMEM, self.pair)]
-        ins += [(VMEM, array) for array in (self.matrix, *self.moved[index])]
-        begun = self.grad is not None
-        if begun:
-            ins += [(VMEM, self.grad)]
-        self.new[index], self.grad = call(
-            functools.partial(last_kernel, self.chunks[index][0], self.rows_total, begun), "last",
+    def last(self, indices, far, near, token):
+        ins = [(ANY, token), (SMEM, self.outer), (VMEM, self.pair), (VMEM, self.matrix)]
+        for index in indices:
+            ins += [(VMEM, array) for array in (far[index], near[index], *self.moved[index])]
+        aliases = None
+        if self.grad is not None:
+            aliases = {len(ins): len(indices)}
+            ins.append((VMEM, self.grad))
+        *new, self.grad = call(
+            functools.partial(last_kernel, self.chunks[indices[0]][0], self.rows_total, len(indices)), "last",
             ins,
-            [self.chunk(index), (VMEM, self.row.shape, F32)],
-            aliases={9: 1} if begun else None,
+            [*map(self.chunk, indices), (VMEM, self.row.shape, F32)],
+            aliases=aliases,
         )
+        self.new.update(zip(indices, new, strict=True))
 
     def new_cols(self, token):
         return call(
@@ -255,7 +281,7 @@
         sums.append(lax.psum(work.fresh(index, sums[0]), "row"))
     sums = [lax.psum(work.middle(index, sums[index], sums[index], sums[index]), "row") for index in every]
     for index in every:
-        work.last(index, sums[index], sums[index], sums[index])
+        work.last([index], sums, sums, sums[index])
 
 
 def join_sums_kernel(token_ref, own_ref, arrived_ref, out_ref):
@@ -290,10 +316,13 @@
     chunks = len(work.chunks)
     slots = 2 * chunks
     own, joined, whole, from_outer, from_inner = {}, {}, {}, {}, {}
+    far, near, pending = {}, {}, []
     own[0] = work.first()
     token = own[0]
-    for k in range(slots + 3 * LAG):
-        here, then, done = k - LAG, k - 2 * LAG, k - 3 * LAG
+    for k in range(slots + 2 * OUTER_LAG + INNER_LAG):
+        here = k - OUTER_LAG
+        then = here - INNER_LAG
+        done = then - OUTER_LAG
         if 0 <= here < slots:
             (joined[here],) = call(
                 join_sums_kernel, "sum",
@@ -304,12 +333,12 @@
             from_inner[k] = lax.ppermute(joined[here], ("row", "col"), inner_pairs)
         ins, outs = {}, {}
         if 0 <= then < slots:
-            ins["joined"], ins["from_inner"] = joined[then], from_inner[here]
+            ins["joined"], ins["from_inner"] = joined[then], from_inner[k - INNER_LAG]
             outs["whole"] = work.chunk(then % chunks)
             if k < slots:
                 ins["own"] = own[k]
                 outs["payload"] = max(work.chunk(then % chunks), work.chunk(k % chunks), key=lambda o: o[1])
-        if k < 2 * LAG:
+        if k < OUTER_LAG + INNER_LAG:
             ins["own"], outs["payload"] = own[k], work.chunk(k)
         if outs:
             got = call(
@@ -321,7 +350,7 @@
             token = got[[*outs][-1]]
             if "whole" in got:
                 whole[then] = got["whole"]
-        if k < slots + 2 * LAG:
+        if k < slots + OUTER_LAG + INNER_LAG:
             payload = got["payload"] if k < slots else whole[then]
             from_outer[k] = lax.ppermute(payload, "row", outer_pairs)
         nxt = k + 1
@@ -329,9 +358,14 @@
             token = own[nxt] = work.fresh(nxt, token)
         elif nxt < slots:
             at = nxt - chunks
-            token = own[nxt] = work.middle(at, from_outer[at + 2 * LAG], whole[at], token)
+            token = own[nxt] = work.middle(at, from_outer[at + OUTER_LAG + INNER_LAG], whole[at], token)
         if done >= chunks:
-            work.last(done - chunks, from_outer[done + 2 * LAG], whole[done], token)
+            at = done - chunks
+            far[at], near[at] = from_outer[done + OUTER_LAG + INNER_LAG], whole[done]
+            pending.append(at)
+        if pending and nxt >= slots:
+            batch, pending = pending[:BATCH], pending[BATCH:]
+            work.last(batch, far, near, token)
             token = work.grad
 
 

time: 133 us -> 129 us (0.970)
  starting transfers between devices: 37.5 us -> 70.8 us
  waiting for transfers between devices: 44.4 us -> 13.2 us
  local copies, waits for them, and re-layouts: 8.91 us -> 0.13 us
  Pallas kernels: 40.3 us -> 42.7 us
    ppermute x26 -> x37, waiting for transfers between devices: 35.8 us -> 4.69 us  [line_columns(): from_outer[k] = lax.ppermute(payload, 'row', outer_pairs)]
    ppermute x26 -> x37, starting transfers between devices: 35.6 us -> 66.3 us  [line_columns(): from_outer[k] = lax.ppermute(payload, 'row', outer_pairs)]
    unnamed x20 -> x13, local copies, waits for them, and re-layouts: 6.61 us -> 0.13 us
    ppermute x22 -> x32, starting transfers between devices: 0.25 us -> 2.75 us  [line_columns(): from_inner[k] = lax.ppermute(joined[here], ('row', 'col'), inner_pairs)]
    pallas_call x85 -> x114, Pallas kernels: 40.3 us -> 42.7 us  [call(): pl.pallas_call(kernel, out_shape=[jax.ShapeDtypeStruct(shape, kind) for _...]
    slice x2 -> x0, local copies, waits for them, and re-layouts: 2.3 us -> none  [the longest x1 1.36 us: first(): self.matrix[:, :width]]
  transfers between devices with their start and end apart: 51 -> 72, of which waited for: 23 -> 6; matrix products, arithmetic and copies ran while one was open for 0% -> 0% of each run, Pallas kernels for 28% -> 28%
where the time goes in v3:
time: 129 us
  starting transfers between devices  70.8 us (55%)
  Pallas kernels  42.7 us (33%)
  waiting for transfers between devices  13.2 us (10%)
  between operations  2.43 us (2%)
    ppermute x37, starting transfers between devices, line_columns(): from_outer[k] = lax.ppermute(payload, 'row', outer_pairs)  66.3 us
    pallas_call x114, Pallas kernels, call(): pl.pallas_call(kernel, out_shape=[jax.ShapeDtypeStruct(shape, kind) for _...  42.7 us
    ppermute x1, waiting for transfers between devices, row_step(): other = lax.ppermute(part, 'col', across)  5.41 us
    ppermute x37, waiting for transfers between devices, line_columns(): from_outer[k] = lax.ppermute(payload, 'row', outer_pairs)  4.69 us
    ppermute x32, starting transfers between devices, line_columns(): from_inner[k] = lax.ppermute(joined[here], ('row', 'col'), inner_pairs)  2.75 us
  transfers between devices with their start and end apart: 72, of which 6 were waited for; matrix products, arithmetic and copies ran while one was open for 0% of the time, Pallas kernels for 28%

profile of v3, /device:TPU:0, one launch (start us, length us, event | category | flops | bytes accessed | tf_op | source)
XLA Modules:
  0.0 129.3 jit_solution(12023887470552372717)
XLA Ops:
  0.6 4.3 %first.1 = (bf16[1024,256]{1,0:T(8,128)(2,1)S(1)}, bf16[1024,256]{1,0:T(8,128)(2,1)S(1)}, bf16[256,1024]{1,0:T(8,128)(2,1)S(1)}, f32[4096,128]{1,0:T(8,128)S(1)}...) custom-call(s32[1]{0:T(128)} %bitcast.1.outer_ref, s32[1]{0:T(128)} %bitcast.high_ref, f32[1024,128]{1,0:T(8,128)} %row_ref.1, ...), custom_call_target="tpu_custom_call" | custom-call | flops 1 | bytes 1 | tf_op jit(solution)/shard_map/first/pallas_call | solution.py:185
  4.9 3.1 %collective-permute-start = (f32[256,128]{1,0:T(8,128)S(1)}, f32[256,128]{1,0:T(8,128)S(1)}, u32[]{:S(2)}, u32[]{:S(2)}) collective-permute-start(f32[256,128]{1,0:T(8,128)S(1)} %merge.37.token_ref), channel_id=1, source_target_pairs={{0,4},{4,0},{8,12},{12,8},{1,5},{5,1},{9,13},{13,9},{2,6},{6,2},{1... | collective-permute-start | bytes 393224 | tf_op jit(solution)/shard_map/ppermute | solution.py:355
  9.7 2.1 %collective-permute-start.2 = (f32[256,128]{1,0:T(8,128)S(1)}, f32[256,128]{1,0:T(8,128)S(1)}, u32[]{:S(2)}, u32[]{:S(2)}) collective-permute-start(f32[256,128]{1,0:T(8,128)S(1)} %merge.39.token_ref), channel_id=1, source_target_pairs={{0,4},{4,0},{8,12},{12,8},{1,5},{5,1},{9,13},{13,9},{2,6},{6,2},{1... | collective-permute-start | bytes 393224 | tf_op jit(solution)/shard_map/ppermute | solution.py:355
  12.7 3.2 %collective-permute-start.4 = (f32[256,128]{1,0:T(8,128)S(1)}, f32[256,128]{1,0:T(8,128)S(1)}, u32[]{:S(2)}, u32[]{:S(2)}) collective-permute-start(f32[256,128]{1,0:T(8,128)S(1)} %merge.40.token_ref), channel_id=1, source_target_pairs={{0,4},{4,0},{8,12},{12,8},{1,5},{5,1},{9,13},{13,9},{2,6},{6,2},{1... | collective-permute-start | bytes 393224 | tf_op jit(solution)/shard_map/ppermute | solution.py:355
  16.8 1.9 %collective-permute-start.6 = (f32[256,128]{1,0:T(8,128)S(1)}, f32[256,128]{1,0:T(8,128)S(1)}, u32[]{:S(2)}, u32[]{:S(2)}) collective-permute-start(f32[256,128]{1,0:T(8,128)S(1)} %merge.41.token_ref), channel_id=1, source_target_pairs={{0,4},{4,0},{8,12},{12,8},{1,5},{5,1},{9,13},{13,9},{2,6},{6,2},{1... | collective-permute-start | bytes 393224 | tf_op jit(solution)/shard_map/ppermute | solution.py:355
  19.6 1.9 %collective-permute-start.8 = (f32[256,128]{1,0:T(8,128)S(1)}, f32[256,128]{1,0:T(8,128)S(1)}, u32[]{:S(2)}, u32[]{:S(2)}) collective-permute-start(f32[256,128]{1,0:T(8,128)S(1)} %get-tuple-element.160.token_ref), channel_id=1, source_target_pairs={{0,4},{4,0},{8,12},{12,8},{1,5},{5,1},{9,13},{13,9},{2,6},{6,2},{1... | collective-permute-start | bytes 393224 | tf_op jit(solution)/shard_map/ppermute | solution.py:355
  22.5 1.9 %collective-permute-start.10 = (f32[256,128]{1,0:T(8,128)S(1)}, f32[256,128]{1,0:T(8,128)S(1)}, u32[]{:S(2)}, u32[]{:S(2)}) collective-permute-start(f32[256,128]{1,0:T(8,128)S(1)} %get-tuple-element.161.token_ref), channel_id=1, source_target_pairs={{0,4},{4,0},{8,12},{12,8},{1,5},{5,1},{9,13},{13,9},{2,6},{6,2},{1... | collective-permute-start | bytes 393224 | tf_op jit(solution)/shard_map/ppermute | solution.py:355
  25.3 1.9 %collective-permute-start.12 = (f32[256,128]{1,0:T(8,128)S(1)}, f32[256,128]{1,0:T(8,128)S(1)}, u32[]{:S(2)}, u32[]{:S(2)}) collective-permute-start(f32[256,128]{1,0:T(8,128)S(1)} %get-tuple-element.162.token_ref), channel_id=1, source_target_pairs={{0,4},{4,0},{8,12},{12,8},{1,5},{5,1},{9,13},{13,9},{2,6},{6,2},{1... | collective-permute-start | bytes 393224 | tf_op jit(solution)/shard_map/ppermute | solution.py:355
  28.1 1.9 %collective-permute-start.14 = (f32[256,128]{1,0:T(8,128)S(1)}, f32[256,128]{1,0:T(8,128)S(1)}, u32[]{:S(2)}, u32[]{:S(2)}) collective-permute-start(f32[256,128]{1,0:T(8,128)S(1)} %get-tuple-element.163.token_ref), channel_id=1, source_target_pairs={{0,4},{4,0},{8,12},{12,8},{1,5},{5,1},{9,13},{13,9},{2,6},{6,2},{1... | collective-permute-start | bytes 393224 | tf_op jit(solution)/shard_map/ppermute | solution.py:355
  30.9 1.9 %collective-permute-start.16 = (f32[256,128]{1,0:T(8,128)S(1)}, f32[256,128]{1,0:T(8,128)S(1)}, u32[]{:S(2)}, u32[]{:S(2)}) collective-permute-start(f32[256,128]{1,0:T(8,128)S(1)} %get-tuple-element.164.token_ref), channel_id=1, source_target_pairs={{0,4},{4,0},{8,12},{12,8},{1,5},{5,1},{9,13},{13,9},{2,6},{6,2},{1... | collective-permute-start | bytes 393224 | tf_op jit(solution)/shard_map/ppermute | solution.py:355
  33.7 1.9 %collective-permute-start.18 = (f32[256,128]{1,0:T(8,128)S(1)}, f32[256,128]{1,0:T(8,128)S(1)}, u32[]{:S(2)}, u32[]{:S(2)}) collective-permute-start(f32[256,128]{1,0:T(8,128)S(1)} %get-tuple-element.165.token_ref), channel_id=1, source_target_pairs={{0,4},{4,0},{8,12},{12,8},{1,5},{5,1},{9,13},{13,9},{2,6},{6,2},{1... | collective-permute-start | bytes 393224 | tf_op jit(solution)/shard_map/ppermute | solution.py:355
  36.5 1.9 %collective-permute-start.20 = (f32[256,128]{1,0:T(8,128)S(1)}, f32[256,128]{1,0:T(8,128)S(1)}, u32[]{:S(2)}, u32[]{:S(2)}) collective-permute-start(f32[256,128]{1,0:T(8,128)S(1)} %get-tuple-element.166.token_ref), channel_id=1, source_target_pairs={{0,4},{4,0},{8,12},{12,8},{1,5},{5,1},{9,13},{13,9},{2,6},{6,2},{1... | collective-permute-start | bytes 393224 | tf_op jit(solution)/shard_map/ppermute | solution.py:355
  39.3 1.9 %collective-permute-start.22 = (f32[256,128]{1,0:T(8,128)S(1)}, f32[256,128]{1,0:T(8,128)S(1)}, u32[]{:S(2)}, u32[]{:S(2)}) collective-permute-start(f32[256,128]{1,0:T(8,128)S(1)} %get-tuple-element.167.token_ref), channel_id=1, source_target_pairs={{0,4},{4,0},{8,12},{12,8},{1,5},{5,1},{9,13},{13,9},{2,6},{6,2},{1... | collective-permute-start | bytes 393224 | tf_op jit(solution)/shard_map/ppermute | solution.py:355
  42.2 1.9 %collective-permute-start.24 = (f32[256,128]{1,0:T(8,128)S(1)}, f32[256,128]{1,0:T(8,128)S(1)}, u32[]{:S(2)}, u32[]{:S(2)}) collective-permute-start(f32[256,128]{1,0:T(8,128)S(1)} %get-tuple-element.168.token_ref), channel_id=1, source_target_pairs={{0,4},{4,0},{8,12},{12,8},{1,5},{5,1},{9,13},{13,9},{2,6},{6,2},{1... | collective-permute-start | bytes 393224 | tf_op jit(solution)/shard_map/ppermute | solution.py:355
  45.0 1.9 %collective-permute-start.26 = (f32[256,128]{1,0:T(8,128)S(1)}, f32[256,128]{1,0:T(8,128)S(1)}, u32[]{:S(2)}, u32[]{:S(2)}) collective-permute-start(f32[256,128]{1,0:T(8,128)S(1)} %get-tuple-element.169.token_ref), channel_id=1, source_target_pairs={{0,4},{4,0},{8,12},{12,8},{1,5},{5,1},{9,13},{13,9},{2,6},{6,2},{1... | collective-permute-start | bytes 393224 | tf_op jit(solution)/shard_map/ppermute | solution.py:355
  47.8 1.9 %collective-permute-start.28 = (f32[256,128]{1,0:T(8,128)S(1)}, f32[256,128]{1,0:T(8,128)S(1)}, u32[]{:S(2)}, u32[]{:S(2)}) collective-permute-start(f32[256,128]{1,0:T(8,128)S(1)} %get-tuple-element.170.token_ref), channel_id=1, source_target_pairs={{0,4},{4,0},{8,12},{12,8},{1,5},{5,1},{9,13},{13,9},{2,6},{6,2},{1... | collective-permute-start | bytes 393224 | tf_op jit(solution)/shard_map/ppermute | solution.py:355
  50.6 1.9 %collective-permute-start.30 = (f32[256,128]{1,0:T(8,128)S(1)}, f32[256,128]{1,0:T(8,128)S(1)}, u32[]{:S(2)}, u32[]{:S(2)}) collective-permute-start(f32[256,128]{1,0:T(8,128)S(1)} %get-tuple-element.173.token_ref), channel_id=1, source_target_pairs={{0,4},{4,0},{8,12},{12,8},{1,5},{5,1},{9,13},{13,9},{2,6},{6,2},{1... | collective-permute-start | bytes 393224 | tf_op jit(solution)/shard_map/ppermute | solution.py:355
  53.7 1.8 %collective-permute-start.32 = (f32[256,128]{1,0:T(8,128)S(1)}, f32[256,128]{1,0:T(8,128)S(1)}, u32[]{:S(2)}, u32[]{:S(2)}) collective-permute-start(f32[256,128]{1,0:T(8,128)S(1)} %get-tuple-element.176.token_ref), channel_id=1, source_target_pairs={{0,4},{4,0},{8,12},{12,8},{1,5},{5,1},{9,13},{13,9},{2,6},{6,2},{1... | collective-permute-start | bytes 393224 | tf_op jit(solution)/shard_map/ppermute | solution.py:355
  61.9 1.8 %collective-permute-start.38 = (f32[256,128]{1,0:T(8,128)S(1)}, f32[256,128]{1,0:T(8,128)S(1)}, u32[]{:S(2)}, u32[]{:S(2)}) collective-permute-start(f32[256,128]{1,0:T(8,128)S(1)} %get-tuple-element.185.token_ref), channel_id=1, source_target_pairs={{0,4},{4,0},{8,12},{12,8},{1,5},{5,1},{9,13},{13,9},{2,6},{6,2},{1... | collective-permute-start | bytes 393224 | tf_op jit(solution)/shard_map/ppermute | solution.py:355
  64.7 1.8 %collective-permute-start.40 = (f32[256,128]{1,0:T(8,128)S(1)}, f32[256,128]{1,0:T(8,128)S(1)}, u32[]{:S(2)}, u32[]{:S(2)}) collective-permute-start(f32[256,128]{1,0:T(8,128)S(1)} %get-tuple-element.188.token_ref), channel_id=1, source_target_pairs={{0,4},{4,0},{8,12},{12,8},{1,5},{5,1},{9,13},{13,9},{2,6},{6,2},{1... | collective-permute-start | bytes 393224 | tf_op jit(solution)/shard_map/ppermute | solution.py:355
  67.6 1.8 %collective-permute-start.42 = (f32[256,128]{1,0:T(8,128)S(1)}, f32[256,128]{1,0:T(8,128)S(1)}, u32[]{:S(2)}, u32[]{:S(2)}) collective-permute-start(f32[256,128]{1,0:T(8,128)S(1)} %get-tuple-element.191.token_ref), channel_id=1, source_target_pairs={{0,4},{4,0},{8,12},{12,8},{1,5},{5,1},{9,13},{13,9},{2,6},{6,2},{1... | collective-permute-start | bytes 393224 | tf_op jit(solution)/shard_map/ppermute | solution.py:355
  70.4 1.8 %collective-permute-start.44 = (f32[256,128]{1,0:T(8,128)S(1)}, f32[256,128]{1,0:T(8,128)S(1)}, u32[]{:S(2)}, u32[]{:S(2)}) collective-permute-start(f32[256,128]{1,0:T(8,128)S(1)} %get-tuple-element.194.token_ref), channel_id=1, source_target_pairs={{0,4},{4,0},{8,12},{12,8},{1,5},{5,1},{9,13},{13,9},{2,6},{6,2},{1... | collective-permute-start | bytes 393224 | tf_op jit(solution)/shard_map/ppermute | solution.py:355
  73.2 1.8 %collective-permute-start.46 = (f32[256,128]{1,0:T(8,128)S(1)}, f32[256,128]{1,0:T(8,128)S(1)}, u32[]{:S(2)}, u32[]{:S(2)}) collective-permute-start(f32[256,128]{1,0:T(8,128)S(1)} %get-tuple-element.197.token_ref), channel_id=1, source_target_pairs={{0,4},{4,0},{8,12},{12,8},{1,5},{5,1},{9,13},{13,9},{2,6},{6,2},{1... | collective-permute-start | bytes 393224 | tf_op jit(solution)/shard_map/ppermute | solution.py:355
  76.0 1.8 %collective-permute-start.48 = (f32[256,128]{1,0:T(8,128)S(1)}, f32[256,128]{1,0:T(8,128)S(1)}, u32[]{:S(2)}, u32[]{:S(2)}) collective-permute-start(f32[256,128]{1,0:T(8,128)S(1)} %get-tuple-element.200.token_ref), channel_id=1, source_target_pairs={{0,4},{4,0},{8,12},{12,8},{1,5},{5,1},{9,13},{13,9},{2,6},{6,2},{1... | collective-permute-start | bytes 393224 | tf_op jit(solution)/shard_map/ppermute | solution.py:355
  78.8 1.8 %collective-permute-start.50 = (f32[256,128]{1,0:T(8,128)S(1)}, f32[256,128]{1,0:T(8,128)S(1)}, u32[]{:S(2)}, u32[]{:S(2)}) collective-permute-start(f32[256,128]{1,0:T(8,128)S(1)} %get-tuple-element.203.token_ref), channel_id=1, source_target_pairs={{0,4},{4,0},{8,12},{12,8},{1,5},{5,1},{9,13},{13,9},{2,6},{6,2},{1... | collective-permute-start | bytes 393224 | tf_op jit(solution)/shard_map/ppermute | solution.py:355
  84.4 1.8 %collective-permute-start.54 = (f32[256,128]{1,0:T(8,128)S(1)}, f32[256,128]{1,0:T(8,128)S(1)}, u32[]{:S(2)}, u32[]{:S(2)}) collective-permute-start(f32[256,128]{1,0:T(8,128)S(1)} %get-tuple-element.209.token_ref), channel_id=1, source_target_pairs={{0,4},{4,0},{8,12},{12,8},{1,5},{5,1},{9,13},{13,9},{2,6},{6,2},{1... | collective-permute-start | bytes 393224 | tf_op jit(solution)/shard_map/ppermute | solution.py:355
  87.2 1.8 %collective-permute-start.56 = (f32[256,128]{1,0:T(8,128)S(1)}, f32[256,128]{1,0:T(8,128)S(1)}, u32[]{:S(2)}, u32[]{:S(2)}) collective-permute-start(f32[256,128]{1,0:T(8,128)S(1)} %get-tuple-element.212.token_ref), channel_id=1, source_target_pairs={{0,4},{4,0},{8,12},{12,8},{1,5},{5,1},{9,13},{13,9},{2,6},{6,2},{1... | collective-permute-start | bytes 393224 | tf_op jit(solution)/shard_map/ppermute | solution.py:355
  92.8 1.8 %collective-permute-start.60 = (f32[256,128]{1,0:T(8,128)S(1)}, f32[256,128]{1,0:T(8,128)S(1)}, u32[]{:S(2)}, u32[]{:S(2)}) collective-permute-start(f32[256,128]{1,0:T(8,128)S(1)} %get-tuple-element.218.token_ref), channel_id=1, source_target_pairs={{0,4},{4,0},{8,12},{12,8},{1,5},{5,1},{9,13},{13,9},{2,6},{6,2},{1... | collective-permute-start | bytes 393224 | tf_op jit(solution)/shard_map/ppermute | solution.py:355
  96.3 1.8 %collective-permute-start.63 = (f32[256,128]{1,0:T(8,128)S(1)}, f32[256,128]{1,0:T(8,128)S(1)}, u32[]{:S(2)}, u32[]{:S(2)}) collective-permute-start(f32[256,128]{1,0:T(8,128)S(1)} %merge.69.token_ref.refs_1_), channel_id=1, source_target_pairs={{0,4},{4,0},{8,12},{12,8},{1,5},{5,1},{9,13},{13,9},{2,6},{6,2},{1... | collective-permute-start | bytes 393224 | tf_op jit(solution)/shard_map/ppermute | solution.py:355
  104.8 1.9 %collective-permute-start.67 = (f32[256,128]{1,0:T(8,128)S(1)}, f32[256,128]{1,0:T(8,128)S(1)}, u32[]{:S(2)}, u32[]{:S(2)}) collective-permute-start(f32[256,128]{1,0:T(8,128)S(1)} %merge.72.token_ref.refs_1_), channel_id=1, source_target_pairs={{0,4},{4,0},{8,12},{12,8},{1,5},{5,1},{9,13},{13,9},{2,6},{6,2},{1... | collective-permute-start | bytes 393224 | tf_op jit(solution)/shard_map/ppermute | solution.py:355
  111.6 2.0 %collective-permute-done.67.refs_0_ = f32[256,128]{1,0:T(8,128)S(1)} collective-permute-done((f32[256,128]{1,0:T(8,128)S(1)}, f32[256,128]{1,0:T(8,128)S(1)}, u32[]{:S(2)}, u32[]{:S(2)}) %collective-permute-start.67) | collective-permute-done | bytes 131104 | tf_op jit(solution)/shard_map/ppermute | solution.py:355
  121.0 5.4 %collective-permute-done.70.other_ref = f32[512,128]{1,0:T(8,128)S(1)} collective-permute-done((f32[512,128]{1,0:T(8,128)S(1)}, f32[512,128]{1,0:T(8,128)S(1)}, u32[]{:S(2)}, u32[]{:S(2)}) %collective-permute-start.70) | collective-permute-done | bytes 262176 | tf_op jit(solution)/shard_map/ppermute | solution.py:380
  (240 shorter events, 59.0 us)
Async XLA Ops:
  9.7 9.8 %collective-permute-start.2 = (f32[256,128]{1,0:T(8,128)S(1)}, f32[256,128]{1,0:T(8,128)S(1)}, u32[]{:S(2)}, u32[]{:S(2)}) collective-permute-start(f32[256,128]{1,0:T(8,128)S(1)} %merge.39.token_ref), channel_id=1, source_target_pairs={{0,4},{4,0},{8,12},{12,8},{1,5},{5,1},{9,13},{13,9},{2,6},{6,2},{1... | collective-permute-start | bytes 393224 | tf_op jit(solution)/shard_map/ppermute | solution.py:355
  12.7 9.6 %collective-permute-start.4 = (f32[256,128]{1,0:T(8,128)S(1)}, f32[256,128]{1,0:T(8,128)S(1)}, u32[]{:S(2)}, u32[]{:S(2)}) collective-permute-start(f32[256,128]{1,0:T(8,128)S(1)} %merge.40.token_ref), channel_id=1, source_target_pairs={{0,4},{4,0},{8,12},{12,8},{1,5},{5,1},{9,13},{13,9},{2,6},{6,2},{1... | collective-permute-start | bytes 393224 | tf_op jit(solution)/shard_map/ppermute | solution.py:355
  16.8 8.3 %collective-permute-start.6 = (f32[256,128]{1,0:T(8,128)S(1)}, f32[256,128]{1,0:T(8,128)S(1)}, u32[]{:S(2)}, u32[]{:S(2)}) collective-permute-start(f32[256,128]{1,0:T(8,128)S(1)} %merge.41.token_ref), channel_id=1, source_target_pairs={{0,4},{4,0},{8,12},{12,8},{1,5},{5,1},{9,13},{13,9},{2,6},{6,2},{1... | collective-permute-start | bytes 393224 | tf_op jit(solution)/shard_map/ppermute | solution.py:355
  19.6 8.3 %collective-permute-start.8 = (f32[256,128]{1,0:T(8,128)S(1)}, f32[256,128]{1,0:T(8,128)S(1)}, u32[]{:S(2)}, u32[]{:S(2)}) collective-permute-start(f32[256,128]{1,0:T(8,128)S(1)} %get-tuple-element.160.token_ref), channel_id=1, source_target_pairs={{0,4},{4,0},{8,12},{12,8},{1,5},{5,1},{9,13},{13,9},{2,6},{6,2},{1... | collective-permute-start | bytes 393224 | tf_op jit(solution)/shard_map/ppermute | solution.py:355
  22.5 8.3 %collective-permute-start.10 = (f32[256,128]{1,0:T(8,128)S(1)}, f32[256,128]{1,0:T(8,128)S(1)}, u32[]{:S(2)}, u32[]{:S(2)}) collective-permute-start(f32[256,128]{1,0:T(8,128)S(1)} %get-tuple-element.161.token_ref), channel_id=1, source_target_pairs={{0,4},{4,0},{8,12},{12,8},{1,5},{5,1},{9,13},{13,9},{2,6},{6,2},{1... | collective-permute-start | bytes 393224 | tf_op jit(solution)/shard_map/ppermute | solution.py:355
  25.3 8.3 %collective-permute-start.12 = (f32[256,128]{1,0:T(8,128)S(1)}, f32[256,128]{1,0:T(8,128)S(1)}, u32[]{:S(2)}, u32[]{:S(2)}) collective-permute-start(f32[256,128]{1,0:T(8,128)S(1)} %get-tuple-element.162.token_ref), channel_id=1, source_target_pairs={{0,4},{4,0},{8,12},{12,8},{1,5},{5,1},{9,13},{13,9},{2,6},{6,2},{1... | collective-permute-start | bytes 393224 | tf_op jit(solution)/shard_map/ppermute | solution.py:355
  28.1 8.3 %collective-permute-start.14 = (f32[256,128]{1,0:T(8,128)S(1)}, f32[256,128]{1,0:T(8,128)S(1)}, u32[]{:S(2)}, u32[]{:S(2)}) collective-permute-start(f32[256,128]{1,0:T(8,128)S(1)} %get-tuple-element.163.token_ref), channel_id=1, source_target_pairs={{0,4},{4,0},{8,12},{12,8},{1,5},{5,1},{9,13},{13,9},{2,6},{6,2},{1... | collective-permute-start | bytes 393224 | tf_op jit(solution)/shard_map/ppermute | solution.py:355
  30.9 8.3 %collective-permute-start.16 = (f32[256,128]{1,0:T(8,128)S(1)}, f32[256,128]{1,0:T(8,128)S(1)}, u32[]{:S(2)}, u32[]{:S(2)}) collective-permute-start(f32[256,128]{1,0:T(8,128)S(1)} %get-tuple-element.164.token_ref), channel_id=1, source_target_pairs={{0,4},{4,0},{8,12},{12,8},{1,5},{5,1},{9,13},{13,9},{2,6},{6,2},{1... | collective-permute-start | bytes 393224 | tf_op jit(solution)/shard_map/ppermute | solution.py:355
  33.7 8.3 %collective-permute-start.18 = (f32[256,128]{1,0:T(8,128)S(1)}, f32[256,128]{1,0:T(8,128)S(1)}, u32[]{:S(2)}, u32[]{:S(2)}) collective-permute-start(f32[256,128]{1,0:T(8,128)S(1)} %get-tuple-element.165.token_ref), channel_id=1, source_target_pairs={{0,4},{4,0},{8,12},{12,8},{1,5},{5,1},{9,13},{13,9},{2,6},{6,2},{1... | collective-permute-start | bytes 393224 | tf_op jit(solution)/shard_map/ppermute | solution.py:355
  36.5 8.3 %collective-permute-start.20 = (f32[256,128]{1,0:T(8,128)S(1)}, f32[256,128]{1,0:T(8,128)S(1)}, u32[]{:S(2)}, u32[]{:S(2)}) collective-permute-start(f32[256,128]{1,0:T(8,128)S(1)} %get-tuple-element.166.token_ref), channel_id=1, source_target_pairs={{0,4},{4,0},{8,12},{12,8},{1,5},{5,1},{9,13},{13,9},{2,6},{6,2},{1... | collective-permute-start | bytes 393224 | tf_op jit(solution)/shard_map/ppermute | solution.py:355
  39.3 8.3 %collective-permute-start.22 = (f32[256,128]{1,0:T(8,128)S(1)}, f32[256,128]{1,0:T(8,128)S(1)}, u32[]{:S(2)}, u32[]{:S(2)}) collective-permute-start(f32[256,128]{1,0:T(8,128)S(1)} %get-tuple-element.167.token_ref), channel_id=1, source_target_pairs={{0,4},{4,0},{8,12},{12,8},{1,5},{5,1},{9,13},{13,9},{2,6},{6,2},{1... | collective-permute-start | bytes 393224 | tf_op jit(solution)/shard_map/ppermute | solution.py:355
  42.2 8.3 %collective-permute-start.24 = (f32[256,128]{1,0:T(8,128)S(1)}, f32[256,128]{1,0:T(8,128)S(1)}, u32[]{:S(2)}, u32[]{:S(2)}) collective-permute-start(f32[256,128]{1,0:T(8,128)S(1)} %get-tuple-element.168.token_ref), channel_id=1, source_target_pairs={{0,4},{4,0},{8,12},{12,8},{1,5},{5,1},{9,13},{13,9},{2,6},{6,2},{1... | collective-permute-start | bytes 393224 | tf_op jit(solution)/shard_map/ppermute | solution.py:355
  45.0 8.6 %collective-permute-start.26 = (f32[256,128]{1,0:T(8,128)S(1)}, f32[256,128]{1,0:T(8,128)S(1)}, u32[]{:S(2)}, u32[]{:S(2)}) collective-permute-start(f32[256,128]{1,0:T(8,128)S(1)} %get-tuple-element.169.token_ref), channel_id=1, source_target_pairs={{0,4},{4,0},{8,12},{12,8},{1,5},{5,1},{9,13},{13,9},{2,6},{6,2},{1... | collective-permute-start | bytes 393224 | tf_op jit(solution)/shard_map/ppermute | solution.py:355
  47.8 8.6 %collective-permute-start.28 = (f32[256,128]{1,0:T(8,128)S(1)}, f32[256,128]{1,0:T(8,128)S(1)}, u32[]{:S(2)}, u32[]{:S(2)}) collective-permute-start(f32[256,128]{1,0:T(8,128)S(1)} %get-tuple-element.170.token_ref), channel_id=1, source_target_pairs={{0,4},{4,0},{8,12},{12,8},{1,5},{5,1},{9,13},{13,9},{2,6},{6,2},{1... | collective-permute-start | bytes 393224 | tf_op jit(solution)/shard_map/ppermute | solution.py:355
  50.6 8.3 %collective-permute-start.30 = (f32[256,128]{1,0:T(8,128)S(1)}, f32[256,128]{1,0:T(8,128)S(1)}, u32[]{:S(2)}, u32[]{:S(2)}) collective-permute-start(f32[256,128]{1,0:T(8,128)S(1)} %get-tuple-element.173.token_ref), channel_id=1, source_target_pairs={{0,4},{4,0},{8,12},{12,8},{1,5},{5,1},{9,13},{13,9},{2,6},{6,2},{1... | collective-permute-start | bytes 393224 | tf_op jit(solution)/shard_map/ppermute | solution.py:355
  53.7 8.1 %collective-permute-start.32 = (f32[256,128]{1,0:T(8,128)S(1)}, f32[256,128]{1,0:T(8,128)S(1)}, u32[]{:S(2)}, u32[]{:S(2)}) collective-permute-start(f32[256,128]{1,0:T(8,128)S(1)} %get-tuple-element.176.token_ref), channel_id=1, source_target_pairs={{0,4},{4,0},{8,12},{12,8},{1,5},{5,1},{9,13},{13,9},{2,6},{6,2},{1... | collective-permute-start | bytes 393224 | tf_op jit(solution)/shard_map/ppermute | solution.py:355
  59.1 8.3 %collective-permute-start.36 = (f32[256,128]{1,0:T(8,128)S(1)}, f32[256,128]{1,0:T(8,128)S(1)}, u32[]{:S(2)}, u32[]{:S(2)}) collective-permute-start(f32[256,128]{1,0:T(8,128)S(1)} %get-tuple-element.182.token_ref), channel_id=1, source_target_pairs={{0,4},{4,0},{8,12},{12,8},{1,5},{5,1},{9,13},{13,9},{2,6},{6,2},{1... | collective-permute-start | bytes 393224 | tf_op jit(solution)/shard_map/ppermute | solution.py:355
  61.9 8.3 %collective-permute-start.38 = (f32[256,128]{1,0:T(8,128)S(1)}, f32[256,128]{1,0:T(8,128)S(1)}, u32[]{:S(2)}, u32[]{:S(2)}) collective-permute-start(f32[256,128]{1,0:T(8,128)S(1)} %get-tuple-element.185.token_ref), channel_id=1, source_target_pairs={{0,4},{4,0},{8,12},{12,8},{1,5},{5,1},{9,13},{13,9},{2,6},{6,2},{1... | collective-permute-start | bytes 393224 | tf_op jit(solution)/shard_map/ppermute | solution.py:355
  64.7 8.3 %collective-permute-start.40 = (f32[256,128]{1,0:T(8,128)S(1)}, f32[256,128]{1,0:T(8,128)S(1)}, u32[]{:S(2)}, u32[]{:S(2)}) collective-permute-start(f32[256,128]{1,0:T(8,128)S(1)} %get-tuple-element.188.token_ref), channel_id=1, source_target_pairs={{0,4},{4,0},{8,12},{12,8},{1,5},{5,1},{9,13},{13,9},{2,6},{6,2},{1... | collective-permute-start | bytes 393224 | tf_op jit(solution)/shard_map/ppermute | solution.py:355
  67.6 8.3 %collective-permute-start.42 = (f32[256,128]{1,0:T(8,128)S(1)}, f32[256,128]{1,0:T(8,128)S(1)}, u32[]{:S(2)}, u32[]{:S(2)}) collective-permute-start(f32[256,128]{1,0:T(8,128)S(1)} %get-tuple-element.191.token_ref), channel_id=1, source_target_pairs={{0,4},{4,0},{8,12},{12,8},{1,5},{5,1},{9,13},{13,9},{2,6},{6,2},{1... | collective-permute-start | bytes 393224 | tf_op jit(solution)/shard_map/ppermute | solution.py:355
  70.4 8.3 %collective-permute-start.44 = (f32[256,128]{1,0:T(8,128)S(1)}, f32[256,128]{1,0:T(8,128)S(1)}, u32[]{:S(2)}, u32[]{:S(2)}) collective-permute-start(f32[256,128]{1,0:T(8,128)S(1)} %get-tuple-element.194.token_ref), channel_id=1, source_target_pairs={{0,4},{4,0},{8,12},{12,8},{1,5},{5,1},{9,13},{13,9},{2,6},{6,2},{1... | collective-permute-start | bytes 393224 | tf_op jit(solution)/shard_map/ppermute | solution.py:355
  73.2 8.3 %collective-permute-start.46 = (f32[256,128]{1,0:T(8,128)S(1)}, f32[256,128]{1,0:T(8,128)S(1)}, u32[]{:S(2)}, u32[]{:S(2)}) collective-permute-start(f32[256,128]{1,0:T(8,128)S(1)} %get-tuple-element.197.token_ref), channel_id=1, source_target_pairs={{0,4},{4,0},{8,12},{12,8},{1,5},{5,1},{9,13},{13,9},{2,6},{6,2},{1... | collective-permute-start | bytes 393224 | tf_op jit(solution)/shard_map/ppermute | solution.py:355
  76.0 8.3 %collective-permute-start.48 = (f32[256,128]{1,0:T(8,128)S(1)}, f32[256,128]{1,0:T(8,128)S(1)}, u32[]{:S(2)}, u32[]{:S(2)}) collective-permute-start(f32[256,128]{1,0:T(8,128)S(1)} %get-tuple-element.200.token_ref), channel_id=1, source_target_pairs={{0,4},{4,0},{8,12},{12,8},{1,5},{5,1},{9,13},{13,9},{2,6},{6,2},{1... | collective-permute-start | bytes 393224 | tf_op jit(solution)/shard_map/ppermute | solution.py:355
  78.8 8.3 %collective-permute-start.50 = (f32[256,128]{1,0:T(8,128)S(1)}, f32[256,128]{1,0:T(8,128)S(1)}, u32[]{:S(2)}, u32[]{:S(2)}) collective-permute-start(f32[256,128]{1,0:T(8,128)S(1)} %get-tuple-element.203.token_ref), channel_id=1, source_target_pairs={{0,4},{4,0},{8,12},{12,8},{1,5},{5,1},{9,13},{13,9},{2,6},{6,2},{1... | collective-permute-start | bytes 393224 | tf_op jit(solution)/shard_map/ppermute | solution.py:355
  81.6 8.3 %collective-permute-start.52 = (f32[256,128]{1,0:T(8,128)S(1)}, f32[256,128]{1,0:T(8,128)S(1)}, u32[]{:S(2)}, u32[]{:S(2)}) collective-permute-start(f32[256,128]{1,0:T(8,128)S(1)} %get-tuple-element.206.token_ref), channel_id=1, source_target_pairs={{0,4},{4,0},{8,12},{12,8},{1,5},{5,1},{9,13},{13,9},{2,6},{6,2},{1... | collective-permute-start | bytes 393224 | tf_op jit(solution)/shard_map/ppermute | solution.py:355
  84.4 8.3 %collective-permute-start.54 = (f32[256,128]{1,0:T(8,128)S(1)}, f32[256,128]{1,0:T(8,128)S(1)}, u32[]{:S(2)}, u32[]{:S(2)}) collective-permute-start(f32[256,128]{1,0:T(8,128)S(1)} %get-tuple-element.209.token_ref), channel_id=1, source_target_pairs={{0,4},{4,0},{8,12},{12,8},{1,5},{5,1},{9,13},{13,9},{2,6},{6,2},{1... | collective-permute-start | bytes 393224 | tf_op jit(solution)/shard_map/ppermute | solution.py:355
  87.2 9.0 %collective-permute-start.56 = (f32[256,128]{1,0:T(8,128)S(1)}, f32[256,128]{1,0:T(8,128)S(1)}, u32[]{:S(2)}, u32[]{:S(2)}) collective-permute-start(f32[256,128]{1,0:T(8,128)S(1)} %get-tuple-element.212.token_ref), channel_id=1, source_target_pairs={{0,4},{4,0},{8,12},{12,8},{1,5},{5,1},{9,13},{13,9},{2,6},{6,2},{1... | collective-permute-start | bytes 393224 | tf_op jit(solution)/shard_map/ppermute | solution.py:355
  90.0 9.5 %collective-permute-start.58 = (f32[256,128]{1,0:T(8,128)S(1)}, f32[256,128]{1,0:T(8,128)S(1)}, u32[]{:S(2)}, u32[]{:S(2)}) collective-permute-start(f32[256,128]{1,0:T(8,128)S(1)} %get-tuple-element.215.token_ref), channel_id=1, source_target_pairs={{0,4},{4,0},{8,12},{12,8},{1,5},{5,1},{9,13},{13,9},{2,6},{6,2},{1... | collective-permute-start | bytes 393224 | tf_op jit(solution)/shard_map/ppermute | solution.py:355
  92.8 8.2 %collective-permute-start.60 = (f32[256,128]{1,0:T(8,128)S(1)}, f32[256,128]{1,0:T(8,128)S(1)}, u32[]{:S(2)}, u32[]{:S(2)}) collective-permute-start(f32[256,128]{1,0:T(8,128)S(1)} %get-tuple-element.218.token_ref), channel_id=1, source_target_pairs={{0,4},{4,0},{8,12},{12,8},{1,5},{5,1},{9,13},{13,9},{2,6},{6,2},{1... | collective-permute-start | bytes 393224 | tf_op jit(solution)/shard_map/ppermute | solution.py:355
  96.3 10.3 %collective-permute-start.63 = (f32[256,128]{1,0:T(8,128)S(1)}, f32[256,128]{1,0:T(8,128)S(1)}, u32[]{:S(2)}, u32[]{:S(2)}) collective-permute-start(f32[256,128]{1,0:T(8,128)S(1)} %merge.69.token_ref.refs_1_), channel_id=1, source_target_pairs={{0,4},{4,0},{8,12},{12,8},{1,5},{5,1},{9,13},{13,9},{2,6},{6,2},{1... | collective-permute-start | bytes 393224 | tf_op jit(solution)/shard_map/ppermute | solution.py:355
  104.8 8.8 %collective-permute-start.67 = (f32[256,128]{1,0:T(8,128)S(1)}, f32[256,128]{1,0:T(8,128)S(1)}, u32[]{:S(2)}, u32[]{:S(2)}) collective-permute-start(f32[256,128]{1,0:T(8,128)S(1)} %merge.72.token_ref.refs_1_), channel_id=1, source_target_pairs={{0,4},{4,0},{8,12},{12,8},{1,5},{5,1},{9,13},{13,9},{2,6},{6,2},{1... | collective-permute-start | bytes 393224 | tf_op jit(solution)/shard_map/ppermute | solution.py:355
  118.0 8.4 %collective-permute-start.70 = (f32[512,128]{1,0:T(8,128)S(1)}, f32[512,128]{1,0:T(8,128)S(1)}, u32[]{:S(2)}, u32[]{:S(2)}) collective-permute-start(f32[512,128]{1,0:T(8,128)S(1)} %add.3.token_ref.part_ref), channel_id=1, source_target_pairs={{0,2},{2,0},{1,3},{3,1},{4,6},{6,4},{5,7},{7,5},{8,10},{10,8},{9,1... | collective-permute-start | bytes 786440 | tf_op jit(solution)/shard_map/ppermute | solution.py:380
  (45 other events, 272.6 us)

commit v4 on v3

--- a/solution.py
+++ b/solution.py
@@ -15,7 +15,7 @@
 EPSILON = 1e-08
 F32, BF16 = jnp.float32, jnp.bfloat16
 NT = (((1,), (1,)), ((), ()))
-ROW_BLOCK = 256
+ROW_BLOCK = 1024
 UNIT = 128
 TARGET = 256
 OUTER_LAG = 3
@@ -58,19 +58,16 @@
 
 
 def first_kernel(
-    outer_ref, high_ref, row_hbm, col_hbm, mat_hbm, twice_ref, pair_ref, turned_ref, col_ref, mat_ref, out_ref,
-    row_ref, sems,
+    outer_ref, high_ref, row_hbm, col_hbm, mat_hbm, twice_ref, pair_ref, turned_ref, one_ref, two_ref,
+    row_ref, col_ref, mat_ref, sems,
 ):
     del outer_ref, high_ref
-    width, columns = out_ref.shape[0], mat_ref.shape[1]
+    width = col_ref.shape[0]
     loads = [
         pltpu.make_async_copy(row_hbm, row_ref, sems.at[0]),
-        pltpu.make_async_copy(mat_hbm.at[:, pl.ds(0, width)], mat_ref.at[:, pl.ds(0, width)], sems.at[1]),
-        pltpu.make_async_copy(col_hbm, col_ref, sems.at[2]),
+        pltpu.make_async_copy(mat_hbm.at[:, pl.ds(0, width)], mat_ref, sems.at[1]),
+        pltpu.make_async_copy(col_hbm.at[pl.ds(0, width), :], col_ref, sems.at[2]),
     ]
-    if width < columns:
-        rest = pl.ds(width, columns - width)
-        loads.append(pltpu.make_async_copy(mat_hbm.at[:, rest], mat_ref.at[:, rest], sems.at[3]))
     for load in loads:
         load.start()
     loads[0].wait()
@@ -80,14 +77,42 @@
     turned_ref[...] = jnp.concatenate([high.T, low.T], axis=0)
     loads[1].wait()
     loads[2].wait()
-    out_ref[...] = col_partial(twice_ref, turned_ref, col_ref[:width, :], mat_ref, 0)
-    for load in loads[3:]:
+    out = col_partial(twice_ref, turned_ref, col_ref[...], mat_ref, 0)
+    one_ref[...] = out[: one_ref.shape[0]]
+    two_ref[...] = out[one_ref.shape[0] :]
+
+
+def third_kernel(
+    at, token_ref, col_hbm, mat_hbm, twice_ref, turned_ref, col_ref, mat_ref, out_ref, sems
+):
+    del token_ref
+    width, columns = out_ref.shape[0], mat_ref.shape[1]
+    soon = at + width
+    loads = [
+        pltpu.make_async_copy(mat_hbm.at[:, pl.ds(0, soon)], mat_ref.at[:, pl.ds(0, soon)], sems.at[0]),
+        pltpu.make_async_copy(col_hbm, col_ref, sems.at[1]),
+    ]
+    if soon < columns:
+        rest = pl.ds(soon, columns - soon)
+        loads.append(pltpu.make_async_copy(mat_hbm.at[:, rest], mat_ref.at[:, rest], sems.at[2]))
+    for load in loads:
+        load.start()
+    loads[0].wait()
+    loads[1].wait()
+    col = col_ref[pl.ds(at, width), :]
+    out_ref[...] = col_partial(twice_ref, turned_ref, col, mat_ref, at)
+    for load in loads[2:]:
         load.wait()
 
 
 def pick(outer_ref, far_ref, near_ref):
     near = near_ref[...]
     return jnp.where(outer_ref[0] == 1, far_ref[: near.shape[0], :], near)
+
+
+def pick_kernel(outer_ref, token_ref, far_ref, near_ref, out_ref):
+    del token_ref
+    out_ref[...] = pick(outer_ref, far_ref, near_ref)
 
 
 def fresh_kernel(at, token_ref, twice_ref, turned_ref, col_ref, mat_ref, out_ref):
@@ -181,7 +206,7 @@
 HBM = pl.BlockSpec(memory_space=pltpu.HBM)
 
 
-def call(kernel, name, ins, outs, scratch=(), aliases=None, room=4):
+def call(kernel, name, ins, outs, scratch=(), aliases=None):
     return pl.pallas_call(
         kernel,
         out_shape=[jax.ShapeDtypeStruct(shape, kind) for _, shape, kind in outs],
@@ -189,15 +214,13 @@
         out_specs=[spec for spec, _, _ in outs],
         scratch_shapes=scratch,
         input_output_aliases=aliases or {},
-        compiler_params=pltpu.CompilerParams(vmem_limit_bytes=room << 20),
+        compiler_params=pltpu.CompilerParams(vmem_limit_bytes=6 << 20),
         cost_estimate=pl.CostEstimate(flops=1, bytes_accessed=1, transcendentals=0),
         name=name,
     )(*[pltpu.with_memory_space_constraint(array, pltpu.HBM) if spec is HBM else array for spec, array in ins])
 
 
 def chunks_of(columns):
-    if columns % UNIT:
-        return [(0, columns)]
     widths = [TARGET] * (columns // TARGET)
     if columns % TARGET:
         widths.append(columns % TARGET)
@@ -220,19 +243,36 @@
 
     def first(self):
         rows, rank = self.row.shape
+        width = sum(self.chunks[1])
         wide = (VMEM, (rows, 2 * rank), BF16)
+        self.twice, self.pair, self.turned, out, self.early = call(
+            first_kernel, "first",
+            [(SMEM, self.outer), (SMEM, self.high), (HBM, self.row), (HBM, self.state[0]), (HBM, self.matrix)],
+            [wide, wide, (VMEM, (2 * rank, rows), BF16), self.chunk(0), self.chunk(1)],
+            scratch=[
+                pltpu.VMEM(self.row.shape, F32),
+                pltpu.VMEM((width, rank), F32),
+                pltpu.VMEM((rows, width), BF16),
+                pltpu.SemaphoreType.DMA((3,)),
+            ],
+        )
+        return out
+
+    def third(self, token):
         col = self.state[0]
-        self.twice, self.pair, self.turned, self.state[0], self.matrix, out = call(
-            first_kernel, "first",
-            [(SMEM, self.outer), (SMEM, self.high), (HBM, self.row), (HBM, col), (HBM, self.matrix)],
-            [wide, wide, (VMEM, (2 * rank, rows), BF16)]
-            + [(VMEM, col.shape, F32), (VMEM, self.matrix.shape, BF16), self.chunk(0)],
-            scratch=[pltpu.VMEM(self.row.shape, F32), pltpu.SemaphoreType.DMA((4,))],
-            room=4,
+        self.state[0], self.matrix, out = call(
+            functools.partial(third_kernel, self.chunks[2][0]), "third",
+            [(ANY, token), (HBM, col), (HBM, self.matrix), (VMEM, self.twice), (VMEM, self.turned)],
+            [(VMEM, col.shape, F32), (VMEM, self.matrix.shape, BF16), self.chunk(2)],
+            scratch=[pltpu.SemaphoreType.DMA((3,))],
         )
         return out
 
     def fresh(self, index, token):
+        if index == 1:
+            return self.early
+        if index == 2:
+            return self.third(token)
         (out,) = call(
             functools.partial(fresh_kernel, self.chunks[index][0]), "fresh",
             [(ANY, token), (VMEM, self.twice), (VMEM, self.turned), (VMEM, self.state[0]), (VMEM, self.matrix)],
@@ -353,6 +393,15 @@
         if k < slots + OUTER_LAG + INNER_LAG:
             payload = got["payload"] if k < slots else whole[then]
             from_outer[k] = lax.ppermute(payload, "row", outer_pairs)
+        early = k - 2 * OUTER_LAG - INNER_LAG + 1
+        if 11 <= early - chunks < chunks:
+            at = early - chunks
+            (token,) = call(
+                pick_kernel, "pick",
+                [(SMEM, work.outer), (ANY, token), (VMEM, from_outer[k - OUTER_LAG + 1]), (VMEM, whole[early])],
+                [work.chunk(at)],
+            )
+            far[at] = near[at] = token
         nxt = k + 1
         if nxt < chunks:
             token = own[nxt] = work.fresh(nxt, token)
@@ -361,10 +410,12 @@
             token = own[nxt] = work.middle(at, from_outer[at + OUTER_LAG + INNER_LAG], whole[at], token)
         if done >= chunks:
             at = done - chunks
-            far[at], near[at] = from_outer[done + OUTER_LAG + INNER_LAG], whole[done]
+            if at not in far:
+                far[at], near[at] = from_outer[done + OUTER_LAG + INNER_LAG], whole[done]
             pending.append(at)
         if pending and nxt >= slots:
-            batch, pending = pending[:BATCH], pending[BATCH:]
+            count = BATCH if done + 1 < slots else len(pending)
+            batch, pending = pending[:count], pending[count:]
             work.last(batch, far, near, token)
             token = work.grad
 

time: 129 us -> 128 us (level)
  Pallas kernels: 42.7 us -> 39.9 us
  starting transfers between devices: 70.8 us -> 72.1 us
    pallas_call x114 -> x118, Pallas kernels: 42.7 us -> 39.9 us  [call(): pl.pallas_call(kernel, out_shape=[jax.ShapeDtypeStruct(shape, kind) for _...]
    ppermute x37, starting transfers between devices: 66.3 us -> 67.9 us  [line_columns(): from_outer[k] = lax.ppermute(payload, 'row', outer_pairs)]
where the time goes in v4:
time: 128 us; the launch traced here: 127 us
  starting transfers between devices  72.1 us (56%)
  Pallas kernels  39.9 us (31%)
  waiting for transfers between devices  12.8 us (10%)
  between operations  2.48 us (2%)
    ppermute x37, starting transfers between devices, line_columns(): from_outer[k] = lax.ppermute(payload, 'row', outer_pairs)  67.9 us
    pallas_call x118, Pallas kernels, call(): pl.pallas_call(kernel, out_shape=[jax.ShapeDtypeStruct(shape, kind) for _...  39.9 us
    ppermute x1, waiting for transfers between devices, row_step(): other = lax.ppermute(part, 'col', across)  5.41 us
    ppermute x37, waiting for transfers between devices, line_columns(): from_outer[k] = lax.ppermute(payload, 'row', outer_pairs)  4.3 us
  transfers between devices with their start and end apart: 72, of which 6 were waited for; matrix products, arithmetic and copies ran while one was open for 0% of the time, Pallas kernels for 28%

profile of v4, /device:TPU:0, one launch (start us, length us, event | category | flops | bytes accessed | tf_op | source)
XLA Modules:
  0.0 127.5 jit_solution(11569938372298668661)
XLA Ops:
  0.6 2.3 %first.1 = (bf16[1024,256]{1,0:T(8,128)(2,1)S(1)}, bf16[1024,256]{1,0:T(8,128)(2,1)S(1)}, bf16[256,1024]{1,0:T(8,128)(2,1)S(1)}, f32[256,128]{1,0:T(8,128)S(1)}, f32[256,128]{1,0:T(8,128)S(1)}) custom-call(s32[1]{0:T(128)} %bitcast.1.outer_ref, s32[1]{0:T(128)} %bitcast.high_ref, f32[1024,128]{1,0:T(8,128)} %row_ref.1, f32[4096,128]{1,0:T(8,128)} %col_hbm.3, ...), custom_call_target="tpu_custom_call" | custom-call | flops 1 | bytes 1 | tf_op jit(solution)/shard_map/first/pallas_call | solution.py:210
  3.0 3.1 %collective-permute-start = (f32[256,128]{1,0:T(8,128)S(1)}, f32[256,128]{1,0:T(8,128)S(1)}, u32[]{:S(2)}, u32[]{:S(2)}) collective-permute-start(f32[256,128]{1,0:T(8,128)S(1)} %merge.39), channel_id=1, source_target_pairs={{0,4},{4,0},{8,12},{12,8},{1,5},{5,1},{9,13},{13,9},{2,6},{6,2},{1... | collective-permute-start | bytes 393224 | tf_op jit(solution)/shard_map/ppermute | solution.py:395
  6.2 4.1 %third.1 = (f32[4096,128]{1,0:T(8,128)S(1)}, bf16[1024,4096]{1,0:T(8,128)(2,1)S(1)}, f32[256,128]{1,0:T(8,128)S(1)}) custom-call(f32[256,128]{1,0:T(8,128)S(1)} %merge.37.token_ref, f32[4096,128]{1,0:T(8,128)} %col_hbm.3, bf16[1024,4096]{1,0:T(8,128)(2,1)} %mat_hbm.3, bf16[1024,256]{1,0:T(8,128)(2,1)S(1)} %get-tuple-element.158.twice_ref, ...), custom_call_target="tpu_custom_call" | custom-call | flops 1 | bytes 1 | tf_op jit(solution)/shard_map/third/pallas_call | solution.py:210
  10.3 2.1 %collective-permute-start.2 = (f32[256,128]{1,0:T(8,128)S(1)}, f32[256,128]{1,0:T(8,128)S(1)}, u32[]{:S(2)}, u32[]{:S(2)}) collective-permute-start(f32[256,128]{1,0:T(8,128)S(1)} %merge.38.token_ref), channel_id=1, source_target_pairs={{0,4},{4,0},{8,12},{12,8},{1,5},{5,1},{9,13},{13,9},{2,6},{6,2},{1... | collective-permute-start | bytes 393224 | tf_op jit(solution)/shard_map/ppermute | solution.py:395
  13.2 3.2 %collective-permute-start.4 = (f32[256,128]{1,0:T(8,128)S(1)}, f32[256,128]{1,0:T(8,128)S(1)}, u32[]{:S(2)}, u32[]{:S(2)}) collective-permute-start(f32[256,128]{1,0:T(8,128)S(1)} %merge.40.token_ref), channel_id=1, source_target_pairs={{0,4},{4,0},{8,12},{12,8},{1,5},{5,1},{9,13},{13,9},{2,6},{6,2},{1... | collective-permute-start | bytes 393224 | tf_op jit(solution)/shard_map/ppermute | solution.py:395
  21.2 2.1 %collective-permute-start.10 = (f32[256,128]{1,0:T(8,128)S(1)}, f32[256,128]{1,0:T(8,128)S(1)}, u32[]{:S(2)}, u32[]{:S(2)}) collective-permute-start(f32[256,128]{1,0:T(8,128)S(1)} %get-tuple-element.165.token_ref), channel_id=1, source_target_pairs={{0,4},{4,0},{8,12},{12,8},{1,5},{5,1},{9,13},{13,9},{2,6},{6,2},{1... | collective-permute-start | bytes 393224 | tf_op jit(solution)/shard_map/ppermute | solution.py:395
  24.1 2.5 %collective-permute-start.12 = (f32[256,128]{1,0:T(8,128)S(1)}, f32[256,128]{1,0:T(8,128)S(1)}, u32[]{:S(2)}, u32[]{:S(2)}) collective-permute-start(f32[256,128]{1,0:T(8,128)S(1)} %get-tuple-element.166.token_ref), channel_id=1, source_target_pairs={{0,4},{4,0},{8,12},{12,8},{1,5},{5,1},{9,13},{13,9},{2,6},{6,2},{1... | collective-permute-start | bytes 393224 | tf_op jit(solution)/shard_map/ppermute | solution.py:395
  27.5 1.9 %collective-permute-start.14 = (f32[256,128]{1,0:T(8,128)S(1)}, f32[256,128]{1,0:T(8,128)S(1)}, u32[]{:S(2)}, u32[]{:S(2)}) collective-permute-start(f32[256,128]{1,0:T(8,128)S(1)} %get-tuple-element.167.token_ref), channel_id=1, source_target_pairs={{0,4},{4,0},{8,12},{12,8},{1,5},{5,1},{9,13},{13,9},{2,6},{6,2},{1... | collective-permute-start | bytes 393224 | tf_op jit(solution)/shard_map/ppermute | solution.py:395
  30.3 1.9 %collective-permute-start.16 = (f32[256,128]{1,0:T(8,128)S(1)}, f32[256,128]{1,0:T(8,128)S(1)}, u32[]{:S(2)}, u32[]{:S(2)}) collective-permute-start(f32[256,128]{1,0:T(8,128)S(1)} %get-tuple-element.168.token_ref), channel_id=1, source_target_pairs={{0,4},{4,0},{8,12},{12,8},{1,5},{5,1},{9,13},{13,9},{2,6},{6,2},{1... | collective-permute-start | bytes 393224 | tf_op jit(solution)/shard_map/ppermute | solution.py:395
  33.1 1.9 %collective-permute-start.18 = (f32[256,128]{1,0:T(8,128)S(1)}, f32[256,128]{1,0:T(8,128)S(1)}, u32[]{:S(2)}, u32[]{:S(2)}) collective-permute-start(f32[256,128]{1,0:T(8,128)S(1)} %get-tuple-element.169.token_ref), channel_id=1, source_target_pairs={{0,4},{4,0},{8,12},{12,8},{1,5},{5,1},{9,13},{13,9},{2,6},{6,2},{1... | collective-permute-start | bytes 393224 | tf_op jit(solution)/shard_map/ppermute | solution.py:395
  35.9 1.9 %collective-permute-start.20 = (f32[256,128]{1,0:T(8,128)S(1)}, f32[256,128]{1,0:T(8,128)S(1)}, u32[]{:S(2)}, u32[]{:S(2)}) collective-permute-start(f32[256,128]{1,0:T(8,128)S(1)} %get-tuple-element.170.token_ref), channel_id=1, source_target_pairs={{0,4},{4,0},{8,12},{12,8},{1,5},{5,1},{9,13},{13,9},{2,6},{6,2},{1... | collective-permute-start | bytes 393224 | tf_op jit(solution)/shard_map/ppermute | solution.py:395
  38.7 1.9 %collective-permute-start.22 = (f32[256,128]{1,0:T(8,128)S(1)}, f32[256,128]{1,0:T(8,128)S(1)}, u32[]{:S(2)}, u32[]{:S(2)}) collective-permute-start(f32[256,128]{1,0:T(8,128)S(1)} %get-tuple-element.171.token_ref), channel_id=1, source_target_pairs={{0,4},{4,0},{8,12},{12,8},{1,5},{5,1},{9,13},{13,9},{2,6},{6,2},{1... | collective-permute-start | bytes 393224 | tf_op jit(solution)/shard_map/ppermute | solution.py:395
  41.5 1.9 %collective-permute-start.24 = (f32[256,128]{1,0:T(8,128)S(1)}, f32[256,128]{1,0:T(8,128)S(1)}, u32[]{:S(2)}, u32[]{:S(2)}) collective-permute-start(f32[256,128]{1,0:T(8,128)S(1)} %get-tuple-element.172.token_ref), channel_id=1, source_target_pairs={{0,4},{4,0},{8,12},{12,8},{1,5},{5,1},{9,13},{13,9},{2,6},{6,2},{1... | collective-permute-start | bytes 393224 | tf_op jit(solution)/shard_map/ppermute | solution.py:395
  44.3 1.9 %collective-permute-start.26 = (f32[256,128]{1,0:T(8,128)S(1)}, f32[256,128]{1,0:T(8,128)S(1)}, u32[]{:S(2)}, u32[]{:S(2)}) collective-permute-start(f32[256,128]{1,0:T(8,128)S(1)} %get-tuple-element.173.token_ref), channel_id=1, source_target_pairs={{0,4},{4,0},{8,12},{12,8},{1,5},{5,1},{9,13},{13,9},{2,6},{6,2},{1... | collective-permute-start | bytes 393224 | tf_op jit(solution)/shard_map/ppermute | solution.py:395
  47.1 1.9 %collective-permute-start.28 = (f32[256,128]{1,0:T(8,128)S(1)}, f32[256,128]{1,0:T(8,128)S(1)}, u32[]{:S(2)}, u32[]{:S(2)}) collective-permute-start(f32[256,128]{1,0:T(8,128)S(1)} %get-tuple-element.174.token_ref), channel_id=1, source_target_pairs={{0,4},{4,0},{8,12},{12,8},{1,5},{5,1},{9,13},{13,9},{2,6},{6,2},{1... | collective-permute-start | bytes 393224 | tf_op jit(solution)/shard_map/ppermute | solution.py:395
  52.8 1.9 %collective-permute-start.32 = (f32[256,128]{1,0:T(8,128)S(1)}, f32[256,128]{1,0:T(8,128)S(1)}, u32[]{:S(2)}, u32[]{:S(2)}) collective-permute-start(f32[256,128]{1,0:T(8,128)S(1)} %get-tuple-element.180.token_ref), channel_id=1, source_target_pairs={{0,4},{4,0},{8,12},{12,8},{1,5},{5,1},{9,13},{13,9},{2,6},{6,2},{1... | collective-permute-start | bytes 393224 | tf_op jit(solution)/shard_map/ppermute | solution.py:395
  58.4 1.9 %collective-permute-start.36 = (f32[256,128]{1,0:T(8,128)S(1)}, f32[256,128]{1,0:T(8,128)S(1)}, u32[]{:S(2)}, u32[]{:S(2)}) collective-permute-start(f32[256,128]{1,0:T(8,128)S(1)} %get-tuple-element.186.token_ref), channel_id=1, source_target_pairs={{0,4},{4,0},{8,12},{12,8},{1,5},{5,1},{9,13},{13,9},{2,6},{6,2},{1... | collective-permute-start | bytes 393224 | tf_op jit(solution)/shard_map/ppermute | solution.py:395
  61.2 1.9 %collective-permute-start.38 = (f32[256,128]{1,0:T(8,128)S(1)}, f32[256,128]{1,0:T(8,128)S(1)}, u32[]{:S(2)}, u32[]{:S(2)}) collective-permute-start(f32[256,128]{1,0:T(8,128)S(1)} %get-tuple-element.189.token_ref), channel_id=1, source_target_pairs={{0,4},{4,0},{8,12},{12,8},{1,5},{5,1},{9,13},{13,9},{2,6},{6,2},{1... | collective-permute-start | bytes 393224 | tf_op jit(solution)/shard_map/ppermute | solution.py:395
  64.0 1.9 %collective-permute-start.40 = (f32[256,128]{1,0:T(8,128)S(1)}, f32[256,128]{1,0:T(8,128)S(1)}, u32[]{:S(2)}, u32[]{:S(2)}) collective-permute-start(f32[256,128]{1,0:T(8,128)S(1)} %get-tuple-element.192.token_ref), channel_id=1, source_target_pairs={{0,4},{4,0},{8,12},{12,8},{1,5},{5,1},{9,13},{13,9},{2,6},{6,2},{1... | collective-permute-start | bytes 393224 | tf_op jit(solution)/shard_map/ppermute | solution.py:395
  66.8 1.9 %collective-permute-start.42 = (f32[256,128]{1,0:T(8,128)S(1)}, f32[256,128]{1,0:T(8,128)S(1)}, u32[]{:S(2)}, u32[]{:S(2)}) collective-permute-start(f32[256,128]{1,0:T(8,128)S(1)} %get-tuple-element.195.token_ref), channel_id=1, source_target_pairs={{0,4},{4,0},{8,12},{12,8},{1,5},{5,1},{9,13},{13,9},{2,6},{6,2},{1... | collective-permute-start | bytes 393224 | tf_op jit(solution)/shard_map/ppermute | solution.py:395
  69.6 1.9 %collective-permute-start.44 = (f32[256,128]{1,0:T(8,128)S(1)}, f32[256,128]{1,0:T(8,128)S(1)}, u32[]{:S(2)}, u32[]{:S(2)}) collective-permute-start(f32[256,128]{1,0:T(8,128)S(1)} %get-tuple-element.198.token_ref), channel_id=1, source_target_pairs={{0,4},{4,0},{8,12},{12,8},{1,5},{5,1},{9,13},{13,9},{2,6},{6,2},{1... | collective-permute-start | bytes 393224 | tf_op jit(solution)/shard_map/ppermute | solution.py:395
  72.5 1.9 %collective-permute-start.46 = (f32[256,128]{1,0:T(8,128)S(1)}, f32[256,128]{1,0:T(8,128)S(1)}, u32[]{:S(2)}, u32[]{:S(2)}) collective-permute-start(f32[256,128]{1,0:T(8,128)S(1)} %get-tuple-element.201.token_ref), channel_id=1, source_target_pairs={{0,4},{4,0},{8,12},{12,8},{1,5},{5,1},{9,13},{13,9},{2,6},{6,2},{1... | collective-permute-start | bytes 393224 | tf_op jit(solution)/shard_map/ppermute | solution.py:395
  75.3 1.9 %collective-permute-start.48 = (f32[256,128]{1,0:T(8,128)S(1)}, f32[256,128]{1,0:T(8,128)S(1)}, u32[]{:S(2)}, u32[]{:S(2)}) collective-permute-start(f32[256,128]{1,0:T(8,128)S(1)} %get-tuple-element.204.token_ref), channel_id=1, source_target_pairs={{0,4},{4,0},{8,12},{12,8},{1,5},{5,1},{9,13},{13,9},{2,6},{6,2},{1... | collective-permute-start | bytes 393224 | tf_op jit(solution)/shard_map/ppermute | solution.py:395
  78.1 1.9 %collective-permute-start.50 = (f32[256,128]{1,0:T(8,128)S(1)}, f32[256,128]{1,0:T(8,128)S(1)}, u32[]{:S(2)}, u32[]{:S(2)}) collective-permute-start(f32[256,128]{1,0:T(8,128)S(1)} %get-tuple-element.207.token_ref), channel_id=1, source_target_pairs={{0,4},{4,0},{8,12},{12,8},{1,5},{5,1},{9,13},{13,9},{2,6},{6,2},{1... | collective-permute-start | bytes 393224 | tf_op jit(solution)/shard_map/ppermute | solution.py:395
  80.9 1.9 %collective-permute-start.52 = (f32[256,128]{1,0:T(8,128)S(1)}, f32[256,128]{1,0:T(8,128)S(1)}, u32[]{:S(2)}, u32[]{:S(2)}) collective-permute-start(f32[256,128]{1,0:T(8,128)S(1)} %get-tuple-element.210.token_ref), channel_id=1, source_target_pairs={{0,4},{4,0},{8,12},{12,8},{1,5},{5,1},{9,13},{13,9},{2,6},{6,2},{1... | collective-permute-start | bytes 393224 | tf_op jit(solution)/shard_map/ppermute | solution.py:395
  83.7 1.9 %collective-permute-start.54 = (f32[256,128]{1,0:T(8,128)S(1)}, f32[256,128]{1,0:T(8,128)S(1)}, u32[]{:S(2)}, u32[]{:S(2)}) collective-permute-start(f32[256,128]{1,0:T(8,128)S(1)} %get-tuple-element.213.token_ref), channel_id=1, source_target_pairs={{0,4},{4,0},{8,12},{12,8},{1,5},{5,1},{9,13},{13,9},{2,6},{6,2},{1... | collective-permute-start | bytes 393224 | tf_op jit(solution)/shard_map/ppermute | solution.py:395
  86.5 1.9 %collective-permute-start.56 = (f32[256,128]{1,0:T(8,128)S(1)}, f32[256,128]{1,0:T(8,128)S(1)}, u32[]{:S(2)}, u32[]{:S(2)}) collective-permute-start(f32[256,128]{1,0:T(8,128)S(1)} %get-tuple-element.216.token_ref), channel_id=1, source_target_pairs={{0,4},{4,0},{8,12},{12,8},{1,5},{5,1},{9,13},{13,9},{2,6},{6,2},{1... | collective-permute-start | bytes 393224 | tf_op jit(solution)/shard_map/ppermute | solution.py:395
  89.3 1.9 %collective-permute-start.58 = (f32[256,128]{1,0:T(8,128)S(1)}, f32[256,128]{1,0:T(8,128)S(1)}, u32[]{:S(2)}, u32[]{:S(2)}) collective-permute-start(f32[256,128]{1,0:T(8,128)S(1)} %get-tuple-element.219.token_ref), channel_id=1, source_target_pairs={{0,4},{4,0},{8,12},{12,8},{1,5},{5,1},{9,13},{13,9},{2,6},{6,2},{1... | collective-permute-start | bytes 393224 | tf_op jit(solution)/shard_map/ppermute | solution.py:395
  92.1 1.9 %collective-permute-start.60 = (f32[256,128]{1,0:T(8,128)S(1)}, f32[256,128]{1,0:T(8,128)S(1)}, u32[]{:S(2)}, u32[]{:S(2)}) collective-permute-start(f32[256,128]{1,0:T(8,128)S(1)} %get-tuple-element.222.token_ref), channel_id=1, source_target_pairs={{0,4},{4,0},{8,12},{12,8},{1,5},{5,1},{9,13},{13,9},{2,6},{6,2},{1... | collective-permute-start | bytes 393224 | tf_op jit(solution)/shard_map/ppermute | solution.py:395
  105.4 2.1 %collective-permute-start.68 = (f32[256,128]{1,0:T(8,128)S(1)}, f32[256,128]{1,0:T(8,128)S(1)}, u32[]{:S(2)}, u32[]{:S(2)}) collective-permute-start(f32[256,128]{1,0:T(8,128)S(1)} %merge.73.token_ref.near_ref), channel_id=1, source_target_pairs={{0,4},{4,0},{8,12},{12,8},{1,5},{5,1},{9,13},{13,9},{2,6},{6,2},{1... | collective-permute-start | bytes 393224 | tf_op jit(solution)/shard_map/ppermute | solution.py:395
  108.5 2.1 %collective-permute-done.67.far_ref = f32[256,128]{1,0:T(8,128)S(1)} collective-permute-done((f32[256,128]{1,0:T(8,128)S(1)}, f32[256,128]{1,0:T(8,128)S(1)}, u32[]{:S(2)}, u32[]{:S(2)}) %collective-permute-start.67) | collective-permute-done | bytes 131104 | tf_op jit(solution)/shard_map/ppermute | solution.py:395
  119.2 5.4 %collective-permute-done.70.other_ref = f32[512,128]{1,0:T(8,128)S(1)} collective-permute-done((f32[512,128]{1,0:T(8,128)S(1)}, f32[512,128]{1,0:T(8,128)S(1)}, u32[]{:S(2)}, u32[]{:S(2)}) %collective-permute-start.70) | collective-permute-done | bytes 262176 | tf_op jit(solution)/shard_map/ppermute | solution.py:431
  (242 shorter events, 54.2 us)
Async XLA Ops:
  3.0 10.1 %collective-permute-start = (f32[256,128]{1,0:T(8,128)S(1)}, f32[256,128]{1,0:T(8,128)S(1)}, u32[]{:S(2)}, u32[]{:S(2)}) collective-permute-start(f32[256,128]{1,0:T(8,128)S(1)} %merge.39), channel_id=1, source_target_pairs={{0,4},{4,0},{8,12},{12,8},{1,5},{5,1},{9,13},{13,9},{2,6},{6,2},{1... | collective-permute-start | bytes 393224 | tf_op jit(solution)/shard_map/ppermute | solution.py:395
  6.1 11.0 %collective-permute-start.1 = (f32[256,128]{1,0:T(8,128)S(1)}, f32[256,128]{1,0:T(8,128)S(1)}, u32[]{:S(2)}, u32[]{:S(2)}) collective-permute-start(f32[256,128]{1,0:T(8,128)S(1)} %merge.37.token_ref), channel_id=1, source_target_pairs={{0,4},{4,0},{8,12},{12,8},{1,5},{5,1},{9,13},{13,9},{2,6},{6,2},{1... | collective-permute-start | bytes 393224 | tf_op jit(solution)/shard_map/ppermute | solution.py:395
  10.3 8.2 %collective-permute-start.2 = (f32[256,128]{1,0:T(8,128)S(1)}, f32[256,128]{1,0:T(8,128)S(1)}, u32[]{:S(2)}, u32[]{:S(2)}) collective-permute-start(f32[256,128]{1,0:T(8,128)S(1)} %merge.38.token_ref), channel_id=1, source_target_pairs={{0,4},{4,0},{8,12},{12,8},{1,5},{5,1},{9,13},{13,9},{2,6},{6,2},{1... | collective-permute-start | bytes 393224 | tf_op jit(solution)/shard_map/ppermute | solution.py:395
  13.2 7.8 %collective-permute-start.4 = (f32[256,128]{1,0:T(8,128)S(1)}, f32[256,128]{1,0:T(8,128)S(1)}, u32[]{:S(2)}, u32[]{:S(2)}) collective-permute-start(f32[256,128]{1,0:T(8,128)S(1)} %merge.40.token_ref), channel_id=1, source_target_pairs={{0,4},{4,0},{8,12},{12,8},{1,5},{5,1},{9,13},{13,9},{2,6},{6,2},{1... | collective-permute-start | bytes 393224 | tf_op jit(solution)/shard_map/ppermute | solution.py:395
  18.7 8.6 %collective-permute-start.8 = (f32[256,128]{1,0:T(8,128)S(1)}, f32[256,128]{1,0:T(8,128)S(1)}, u32[]{:S(2)}, u32[]{:S(2)}) collective-permute-start(f32[256,128]{1,0:T(8,128)S(1)} %get-tuple-element.164.token_ref), channel_id=1, source_target_pairs={{0,4},{4,0},{8,12},{12,8},{1,5},{5,1},{9,13},{13,9},{2,6},{6,2},{1... | collective-permute-start | bytes 393224 | tf_op jit(solution)/shard_map/ppermute | solution.py:395
  21.2 9.0 %collective-permute-start.10 = (f32[256,128]{1,0:T(8,128)S(1)}, f32[256,128]{1,0:T(8,128)S(1)}, u32[]{:S(2)}, u32[]{:S(2)}) collective-permute-start(f32[256,128]{1,0:T(8,128)S(1)} %get-tuple-element.165.token_ref), channel_id=1, source_target_pairs={{0,4},{4,0},{8,12},{12,8},{1,5},{5,1},{9,13},{13,9},{2,6},{6,2},{1... | collective-permute-start | bytes 393224 | tf_op jit(solution)/shard_map/ppermute | solution.py:395
  24.1 8.8 %collective-permute-start.12 = (f32[256,128]{1,0:T(8,128)S(1)}, f32[256,128]{1,0:T(8,128)S(1)}, u32[]{:S(2)}, u32[]{:S(2)}) collective-permute-start(f32[256,128]{1,0:T(8,128)S(1)} %get-tuple-element.166.token_ref), channel_id=1, source_target_pairs={{0,4},{4,0},{8,12},{12,8},{1,5},{5,1},{9,13},{13,9},{2,6},{6,2},{1... | collective-permute-start | bytes 393224 | tf_op jit(solution)/shard_map/ppermute | solution.py:395
  27.5 8.3 %collective-permute-start.14 = (f32[256,128]{1,0:T(8,128)S(1)}, f32[256,128]{1,0:T(8,128)S(1)}, u32[]{:S(2)}, u32[]{:S(2)}) collective-permute-start(f32[256,128]{1,0:T(8,128)S(1)} %get-tuple-element.167.token_ref), channel_id=1, source_target_pairs={{0,4},{4,0},{8,12},{12,8},{1,5},{5,1},{9,13},{13,9},{2,6},{6,2},{1... | collective-permute-start | bytes 393224 | tf_op jit(solution)/shard_map/ppermute | solution.py:395
  30.3 8.3 %collective-permute-start.16 = (f32[256,128]{1,0:T(8,128)S(1)}, f32[256,128]{1,0:T(8,128)S(1)}, u32[]{:S(2)}, u32[]{:S(2)}) collective-permute-start(f32[256,128]{1,0:T(8,128)S(1)} %get-tuple-element.168.token_ref), channel_id=1, source_target_pairs={{0,4},{4,0},{8,12},{12,8},{1,5},{5,1},{9,13},{13,9},{2,6},{6,2},{1... | collective-permute-start | bytes 393224 | tf_op jit(solution)/shard_map/ppermute | solution.py:395
  33.1 8.3 %collective-permute-start.18 = (f32[256,128]{1,0:T(8,128)S(1)}, f32[256,128]{1,0:T(8,128)S(1)}, u32[]{:S(2)}, u32[]{:S(2)}) collective-permute-start(f32[256,128]{1,0:T(8,128)S(1)} %get-tuple-element.169.token_ref), channel_id=1, source_target_pairs={{0,4},{4,0},{8,12},{12,8},{1,5},{5,1},{9,13},{13,9},{2,6},{6,2},{1... | collective-permute-start | bytes 393224 | tf_op jit(solution)/shard_map/ppermute | solution.py:395
  35.9 8.3 %collective-permute-start.20 = (f32[256,128]{1,0:T(8,128)S(1)}, f32[256,128]{1,0:T(8,128)S(1)}, u32[]{:S(2)}, u32[]{:S(2)}) collective-permute-start(f32[256,128]{1,0:T(8,128)S(1)} %get-tuple-element.170.token_ref), channel_id=1, source_target_pairs={{0,4},{4,0},{8,12},{12,8},{1,5},{5,1},{9,13},{13,9},{2,6},{6,2},{1... | collective-permute-start | bytes 393224 | tf_op jit(solution)/shard_map/ppermute | solution.py:395
  38.7 8.3 %collective-permute-start.22 = (f32[256,128]{1,0:T(8,128)S(1)}, f32[256,128]{1,0:T(8,128)S(1)}, u32[]{:S(2)}, u32[]{:S(2)}) collective-permute-start(f32[256,128]{1,0:T(8,128)S(1)} %get-tuple-element.171.token_ref), channel_id=1, source_target_pairs={{0,4},{4,0},{8,12},{12,8},{1,5},{5,1},{9,13},{13,9},{2,6},{6,2},{1... | collective-permute-start | bytes 393224 | tf_op jit(solution)/shard_map/ppermute | solution.py:395
  41.5 8.3 %collective-permute-start.24 = (f32[256,128]{1,0:T(8,128)S(1)}, f32[256,128]{1,0:T(8,128)S(1)}, u32[]{:S(2)}, u32[]{:S(2)}) collective-permute-start(f32[256,128]{1,0:T(8,128)S(1)} %get-tuple-element.172.token_ref), channel_id=1, source_target_pairs={{0,4},{4,0},{8,12},{12,8},{1,5},{5,1},{9,13},{13,9},{2,6},{6,2},{1... | collective-permute-start | bytes 393224 | tf_op jit(solution)/shard_map/ppermute | solution.py:395
  44.3 8.3 %collective-permute-start.26 = (f32[256,128]{1,0:T(8,128)S(1)}, f32[256,128]{1,0:T(8,128)S(1)}, u32[]{:S(2)}, u32[]{:S(2)}) collective-permute-start(f32[256,128]{1,0:T(8,128)S(1)} %get-tuple-element.173.token_ref), channel_id=1, source_target_pairs={{0,4},{4,0},{8,12},{12,8},{1,5},{5,1},{9,13},{13,9},{2,6},{6,2},{1... | collective-permute-start | bytes 393224 | tf_op jit(solution)/shard_map/ppermute | solution.py:395
  47.1 8.3 %collective-permute-start.28 = (f32[256,128]{1,0:T(8,128)S(1)}, f32[256,128]{1,0:T(8,128)S(1)}, u32[]{:S(2)}, u32[]{:S(2)}) collective-permute-start(f32[256,128]{1,0:T(8,128)S(1)} %get-tuple-element.174.token_ref), channel_id=1, source_target_pairs={{0,4},{4,0},{8,12},{12,8},{1,5},{5,1},{9,13},{13,9},{2,6},{6,2},{1... | collective-permute-start | bytes 393224 | tf_op jit(solution)/shard_map/ppermute | solution.py:395
  50.0 8.3 %collective-permute-start.30 = (f32[256,128]{1,0:T(8,128)S(1)}, f32[256,128]{1,0:T(8,128)S(1)}, u32[]{:S(2)}, u32[]{:S(2)}) collective-permute-start(f32[256,128]{1,0:T(8,128)S(1)} %get-tuple-element.177.token_ref), channel_id=1, source_target_pairs={{0,4},{4,0},{8,12},{12,8},{1,5},{5,1},{9,13},{13,9},{2,6},{6,2},{1... | collective-permute-start | bytes 393224 | tf_op jit(solution)/shard_map/ppermute | solution.py:395
  52.8 8.3 %collective-permute-start.32 = (f32[256,128]{1,0:T(8,128)S(1)}, f32[256,128]{1,0:T(8,128)S(1)}, u32[]{:S(2)}, u32[]{:S(2)}) collective-permute-start(f32[256,128]{1,0:T(8,128)S(1)} %get-tuple-element.180.token_ref), channel_id=1, source_target_pairs={{0,4},{4,0},{8,12},{12,8},{1,5},{5,1},{9,13},{13,9},{2,6},{6,2},{1... | collective-permute-start | bytes 393224 | tf_op jit(solution)/shard_map/ppermute | solution.py:395
  55.8 8.1 %collective-permute-start.34 = (f32[256,128]{1,0:T(8,128)S(1)}, f32[256,128]{1,0:T(8,128)S(1)}, u32[]{:S(2)}, u32[]{:S(2)}) collective-permute-start(f32[256,128]{1,0:T(8,128)S(1)} %get-tuple-element.183.token_ref), channel_id=1, source_target_pairs={{0,4},{4,0},{8,12},{12,8},{1,5},{5,1},{9,13},{13,9},{2,6},{6,2},{1... | collective-permute-start | bytes 393224 | tf_op jit(solution)/shard_map/ppermute | solution.py:395
  58.4 8.3 %collective-permute-start.36 = (f32[256,128]{1,0:T(8,128)S(1)}, f32[256,128]{1,0:T(8,128)S(1)}, u32[]{:S(2)}, u32[]{:S(2)}) collective-permute-start(f32[256,128]{1,0:T(8,128)S(1)} %get-tuple-element.186.token_ref), channel_id=1, source_target_pairs={{0,4},{4,0},{8,12},{12,8},{1,5},{5,1},{9,13},{13,9},{2,6},{6,2},{1... | collective-permute-start | bytes 393224 | tf_op jit(solution)/shard_map/ppermute | solution.py:395
  61.2 8.3 %collective-permute-start.38 = (f32[256,128]{1,0:T(8,128)S(1)}, f32[256,128]{1,0:T(8,128)S(1)}, u32[]{:S(2)}, u32[]{:S(2)}) collective-permute-start(f32[256,128]{1,0:T(8,128)S(1)} %get-tuple-element.189.token_ref), channel_id=1, source_target_pairs={{0,4},{4,0},{8,12},{12,8},{1,5},{5,1},{9,13},{13,9},{2,6},{6,2},{1... | collective-permute-start | bytes 393224 | tf_op jit(solution)/shard_map/ppermute | solution.py:395
  64.0 8.3 %collective-permute-start.40 = (f32[256,128]{1,0:T(8,128)S(1)}, f32[256,128]{1,0:T(8,128)S(1)}, u32[]{:S(2)}, u32[]{:S(2)}) collective-permute-start(f32[256,128]{1,0:T(8,128)S(1)} %get-tuple-element.192.token_ref), channel_id=1, source_target_pairs={{0,4},{4,0},{8,12},{12,8},{1,5},{5,1},{9,13},{13,9},{2,6},{6,2},{1... | collective-permute-start | bytes 393224 | tf_op jit(solution)/shard_map/ppermute | solution.py:395
  66.8 8.3 %collective-permute-start.42 = (f32[256,128]{1,0:T(8,128)S(1)}, f32[256,128]{1,0:T(8,128)S(1)}, u32[]{:S(2)}, u32[]{:S(2)}) collective-permute-start(f32[256,128]{1,0:T(8,128)S(1)} %get-tuple-element.195.token_ref), channel_id=1, source_target_pairs={{0,4},{4,0},{8,12},{12,8},{1,5},{5,1},{9,13},{13,9},{2,6},{6,2},{1... | collective-permute-start | bytes 393224 | tf_op jit(solution)/shard_map/ppermute | solution.py:395
  69.6 8.3 %collective-permute-start.44 = (f32[256,128]{1,0:T(8,128)S(1)}, f32[256,128]{1,0:T(8,128)S(1)}, u32[]{:S(2)}, u32[]{:S(2)}) collective-permute-start(f32[256,128]{1,0:T(8,128)S(1)} %get-tuple-element.198.token_ref), channel_id=1, source_target_pairs={{0,4},{4,0},{8,12},{12,8},{1,5},{5,1},{9,13},{13,9},{2,6},{6,2},{1... | collective-permute-start | bytes 393224 | tf_op jit(solution)/shard_map/ppermute | solution.py:395
  72.5 8.3 %collective-permute-start.46 = (f32[256,128]{1,0:T(8,128)S(1)}, f32[256,128]{1,0:T(8,128)S(1)}, u32[]{:S(2)}, u32[]{:S(2)}) collective-permute-start(f32[256,128]{1,0:T(8,128)S(1)} %get-tuple-element.201.token_ref), channel_id=1, source_target_pairs={{0,4},{4,0},{8,12},{12,8},{1,5},{5,1},{9,13},{13,9},{2,6},{6,2},{1... | collective-permute-start | bytes 393224 | tf_op jit(solution)/shard_map/ppermute | solution.py:395
  75.3 8.3 %collective-permute-start.48 = (f32[256,128]{1,0:T(8,128)S(1)}, f32[256,128]{1,0:T(8,128)S(1)}, u32[]{:S(2)}, u32[]{:S(2)}) collective-permute-start(f32[256,128]{1,0:T(8,128)S(1)} %get-tuple-element.204.token_ref), channel_id=1, source_target_pairs={{0,4},{4,0},{8,12},{12,8},{1,5},{5,1},{9,13},{13,9},{2,6},{6,2},{1... | collective-permute-start | bytes 393224 | tf_op jit(solution)/shard_map/ppermute | solution.py:395
  78.1 8.3 %collective-permute-start.50 = (f32[256,128]{1,0:T(8,128)S(1)}, f32[256,128]{1,0:T(8,128)S(1)}, u32[]{:S(2)}, u32[]{:S(2)}) collective-permute-start(f32[256,128]{1,0:T(8,128)S(1)} %get-tuple-element.207.token_ref), channel_id=1, source_target_pairs={{0,4},{4,0},{8,12},{12,8},{1,5},{5,1},{9,13},{13,9},{2,6},{6,2},{1... | collective-permute-start | bytes 393224 | tf_op jit(solution)/shard_map/ppermute | solution.py:395
  80.9 8.3 %collective-permute-start.52 = (f32[256,128]{1,0:T(8,128)S(1)}, f32[256,128]{1,0:T(8,128)S(1)}, u32[]{:S(2)}, u32[]{:S(2)}) collective-permute-start(f32[256,128]{1,0:T(8,128)S(1)} %get-tuple-element.210.token_ref), channel_id=1, source_target_pairs={{0,4},{4,0},{8,12},{12,8},{1,5},{5,1},{9,13},{13,9},{2,6},{6,2},{1... | collective-permute-start | bytes 393224 | tf_op jit(solution)/shard_map/ppermute | solution.py:395
  83.7 8.3 %collective-permute-start.54 = (f32[256,128]{1,0:T(8,128)S(1)}, f32[256,128]{1,0:T(8,128)S(1)}, u32[]{:S(2)}, u32[]{:S(2)}) collective-permute-start(f32[256,128]{1,0:T(8,128)S(1)} %get-tuple-element.213.token_ref), channel_id=1, source_target_pairs={{0,4},{4,0},{8,12},{12,8},{1,5},{5,1},{9,13},{13,9},{2,6},{6,2},{1... | collective-permute-start | bytes 393224 | tf_op jit(solution)/shard_map/ppermute | solution.py:395
  86.5 8.7 %collective-permute-start.56 = (f32[256,128]{1,0:T(8,128)S(1)}, f32[256,128]{1,0:T(8,128)S(1)}, u32[]{:S(2)}, u32[]{:S(2)}) collective-permute-start(f32[256,128]{1,0:T(8,128)S(1)} %get-tuple-element.216.token_ref), channel_id=1, source_target_pairs={{0,4},{4,0},{8,12},{12,8},{1,5},{5,1},{9,13},{13,9},{2,6},{6,2},{1... | collective-permute-start | bytes 393224 | tf_op jit(solution)/shard_map/ppermute | solution.py:395
  89.3 8.9 %collective-permute-start.58 = (f32[256,128]{1,0:T(8,128)S(1)}, f32[256,128]{1,0:T(8,128)S(1)}, u32[]{:S(2)}, u32[]{:S(2)}) collective-permute-start(f32[256,128]{1,0:T(8,128)S(1)} %get-tuple-element.219.token_ref), channel_id=1, source_target_pairs={{0,4},{4,0},{8,12},{12,8},{1,5},{5,1},{9,13},{13,9},{2,6},{6,2},{1... | collective-permute-start | bytes 393224 | tf_op jit(solution)/shard_map/ppermute | solution.py:395
  92.1 9.2 %collective-permute-start.60 = (f32[256,128]{1,0:T(8,128)S(1)}, f32[256,128]{1,0:T(8,128)S(1)}, u32[]{:S(2)}, u32[]{:S(2)}) collective-permute-start(f32[256,128]{1,0:T(8,128)S(1)} %get-tuple-element.222.token_ref), channel_id=1, source_target_pairs={{0,4},{4,0},{8,12},{12,8},{1,5},{5,1},{9,13},{13,9},{2,6},{6,2},{1... | collective-permute-start | bytes 393224 | tf_op jit(solution)/shard_map/ppermute | solution.py:395
  116.2 8.4 %collective-permute-start.70 = (f32[512,128]{1,0:T(8,128)S(1)}, f32[512,128]{1,0:T(8,128)S(1)}, u32[]{:S(2)}, u32[]{:S(2)}) collective-permute-start(f32[512,128]{1,0:T(8,128)S(1)} %add.3.token_ref.part_ref), channel_id=1, source_target_pairs={{0,2},{2,0},{1,3},{3,1},{4,6},{6,4},{5,7},{7,5},{8,10},{10,8},{9,1... | collective-permute-start | bytes 786440 | tf_op jit(solution)/shard_map/ppermute | solution.py:431
  (45 other events, 262.2 us)

commit v5 on v4

--- a/solution.py
+++ b/solution.py
@@ -394,7 +394,7 @@
             payload = got["payload"] if k < slots else whole[then]
             from_outer[k] = lax.ppermute(payload, "row", outer_pairs)
         early = k - 2 * OUTER_LAG - INNER_LAG + 1
-        if 11 <= early - chunks < chunks:
+        if k >= slots + INNER_LAG and early < slots:
             at = early - chunks
             (token,) = call(
                 pick_kernel, "pick",
@@ -402,17 +402,18 @@
                 [work.chunk(at)],
             )
             far[at] = near[at] = token
+            pending.append(at)
         nxt = k + 1
         if nxt < chunks:
             token = own[nxt] = work.fresh(nxt, token)
         elif nxt < slots:
             at = nxt - chunks
             token = own[nxt] = work.middle(at, from_outer[at + OUTER_LAG + INNER_LAG], whole[at], token)
-        if done >= chunks:
-            at = done - chunks
-            if at not in far:
-                far[at], near[at] = from_outer[done + OUTER_LAG + INNER_LAG], whole[done]
+        at = done - chunks
+        if at >= 0 and at not in far:
+            far[at], near[at] = from_outer[done + OUTER_LAG + INNER_LAG], whole[done]
             pending.append(at)
+        pending.sort()
         if pending and nxt >= slots:
             count = BATCH if done + 1 < slots else len(pending)
             batch, pending = pending[:count], pending[count:]

time: 128 us -> 127 us (level)
    pallas_call x118 -> x117, Pallas kernels: 39.9 us -> 39.5 us  [call(): pl.pallas_call(kernel, out_shape=[jax.ShapeDtypeStruct(shape, kind) for _...]
where the time goes in v5:
time: 127 us
  starting transfers between devices  71.9 us (57%)
  Pallas kernels  39.5 us (31%)
  waiting for transfers between devices  12.8 us (10%)
  between operations  2.47 us (2%)
    ppermute x37, starting transfers between devices, line_columns(): from_outer[k] = lax.ppermute(payload, 'row', outer_pairs)  67.7 us
    pallas_call x117, Pallas kernels, call(): pl.pallas_call(kernel, out_shape=[jax.ShapeDtypeStruct(shape, kind) for _...  39.5 us
    ppermute x1, waiting for transfers between devices, row_step(): other = lax.ppermute(part, 'col', across)  5.41 us
    ppermute x37, waiting for transfers between devices, line_columns(): from_outer[k] = lax.ppermute(payload, 'row', outer_pairs)  4.29 us
  transfers between devices with their start and end apart: 72, of which 6 were waited for; matrix products, arithmetic and copies ran while one was open for 0% of the time, Pallas kernels for 28%

profile of v5, /device:TPU:0, one launch (start us, length us, event | category | flops | bytes accessed | tf_op | source)
XLA Modules:
  0.0 126.7 jit_solution(17635456361879046840)
XLA Ops:
  0.6 2.3 %first.1 = (bf16[1024,256]{1,0:T(8,128)(2,1)S(1)}, bf16[1024,256]{1,0:T(8,128)(2,1)S(1)}, bf16[256,1024]{1,0:T(8,128)(2,1)S(1)}, f32[256,128]{1,0:T(8,128)S(1)}, f32[256,128]{1,0:T(8,128)S(1)}) custom-call(s32[1]{0:T(128)} %bitcast.1.outer_ref, s32[1]{0:T(128)} %bitcast.high_ref, f32[1024,128]{1,0:T(8,128)} %row_ref.1, f32[4096,128]{1,0:T(8,128)} %col_hbm.3, ...), custom_call_target="tpu_custom_call" | custom-call | flops 1 | bytes 1 | tf_op jit(solution)/shard_map/first/pallas_call | solution.py:210
  3.0 3.1 %collective-permute-start = (f32[256,128]{1,0:T(8,128)S(1)}, f32[256,128]{1,0:T(8,128)S(1)}, u32[]{:S(2)}, u32[]{:S(2)}) collective-permute-start(f32[256,128]{1,0:T(8,128)S(1)} %merge.39), channel_id=1, source_target_pairs={{0,4},{4,0},{8,12},{12,8},{1,5},{5,1},{9,13},{13,9},{2,6},{6,2},{1... | collective-permute-start | bytes 393224 | tf_op jit(solution)/shard_map/ppermute | solution.py:395
  6.2 4.1 %third.1 = (f32[4096,128]{1,0:T(8,128)S(1)}, bf16[1024,4096]{1,0:T(8,128)(2,1)S(1)}, f32[256,128]{1,0:T(8,128)S(1)}) custom-call(f32[256,128]{1,0:T(8,128)S(1)} %merge.37.token_ref, f32[4096,128]{1,0:T(8,128)} %col_hbm.3, bf16[1024,4096]{1,0:T(8,128)(2,1)} %mat_hbm.3, bf16[1024,256]{1,0:T(8,128)(2,1)S(1)} %get-tuple-element.157.twice_ref, ...), custom_call_target="tpu_custom_call" | custom-call | flops 1 | bytes 1 | tf_op jit(solution)/shard_map/third/pallas_call | solution.py:210
  10.3 2.1 %collective-permute-start.2 = (f32[256,128]{1,0:T(8,128)S(1)}, f32[256,128]{1,0:T(8,128)S(1)}, u32[]{:S(2)}, u32[]{:S(2)}) collective-permute-start(f32[256,128]{1,0:T(8,128)S(1)} %merge.38.token_ref), channel_id=1, source_target_pairs={{0,4},{4,0},{8,12},{12,8},{1,5},{5,1},{9,13},{13,9},{2,6},{6,2},{1... | collective-permute-start | bytes 393224 | tf_op jit(solution)/shard_map/ppermute | solution.py:395
  13.2 3.2 %collective-permute-start.4 = (f32[256,128]{1,0:T(8,128)S(1)}, f32[256,128]{1,0:T(8,128)S(1)}, u32[]{:S(2)}, u32[]{:S(2)}) collective-permute-start(f32[256,128]{1,0:T(8,128)S(1)} %merge.40.token_ref), channel_id=1, source_target_pairs={{0,4},{4,0},{8,12},{12,8},{1,5},{5,1},{9,13},{13,9},{2,6},{6,2},{1... | collective-permute-start | bytes 393224 | tf_op jit(solution)/shard_map/ppermute | solution.py:395
  21.2 2.1 %collective-permute-start.10 = (f32[256,128]{1,0:T(8,128)S(1)}, f32[256,128]{1,0:T(8,128)S(1)}, u32[]{:S(2)}, u32[]{:S(2)}) collective-permute-start(f32[256,128]{1,0:T(8,128)S(1)} %get-tuple-element.164.token_ref), channel_id=1, source_target_pairs={{0,4},{4,0},{8,12},{12,8},{1,5},{5,1},{9,13},{13,9},{2,6},{6,2},{1... | collective-permute-start | bytes 393224 | tf_op jit(solution)/shard_map/ppermute | solution.py:395
  24.1 2.5 %collective-permute-start.12 = (f32[256,128]{1,0:T(8,128)S(1)}, f32[256,128]{1,0:T(8,128)S(1)}, u32[]{:S(2)}, u32[]{:S(2)}) collective-permute-start(f32[256,128]{1,0:T(8,128)S(1)} %get-tuple-element.165.token_ref), channel_id=1, source_target_pairs={{0,4},{4,0},{8,12},{12,8},{1,5},{5,1},{9,13},{13,9},{2,6},{6,2},{1... | collective-permute-start | bytes 393224 | tf_op jit(solution)/shard_map/ppermute | solution.py:395
  27.5 1.9 %collective-permute-start.14 = (f32[256,128]{1,0:T(8,128)S(1)}, f32[256,128]{1,0:T(8,128)S(1)}, u32[]{:S(2)}, u32[]{:S(2)}) collective-permute-start(f32[256,128]{1,0:T(8,128)S(1)} %get-tuple-element.166.token_ref), channel_id=1, source_target_pairs={{0,4},{4,0},{8,12},{12,8},{1,5},{5,1},{9,13},{13,9},{2,6},{6,2},{1... | collective-permute-start | bytes 393224 | tf_op jit(solution)/shard_map/ppermute | solution.py:395
  30.3 1.9 %collective-permute-start.16 = (f32[256,128]{1,0:T(8,128)S(1)}, f32[256,128]{1,0:T(8,128)S(1)}, u32[]{:S(2)}, u32[]{:S(2)}) collective-permute-start(f32[256,128]{1,0:T(8,128)S(1)} %get-tuple-element.167.token_ref), channel_id=1, source_target_pairs={{0,4},{4,0},{8,12},{12,8},{1,5},{5,1},{9,13},{13,9},{2,6},{6,2},{1... | collective-permute-start | bytes 393224 | tf_op jit(solution)/shard_map/ppermute | solution.py:395
  33.1 1.9 %collective-permute-start.18 = (f32[256,128]{1,0:T(8,128)S(1)}, f32[256,128]{1,0:T(8,128)S(1)}, u32[]{:S(2)}, u32[]{:S(2)}) collective-permute-start(f32[256,128]{1,0:T(8,128)S(1)} %get-tuple-element.168.token_ref), channel_id=1, source_target_pairs={{0,4},{4,0},{8,12},{12,8},{1,5},{5,1},{9,13},{13,9},{2,6},{6,2},{1... | collective-permute-start | bytes 393224 | tf_op jit(solution)/shard_map/ppermute | solution.py:395
  35.9 1.9 %collective-permute-start.20 = (f32[256,128]{1,0:T(8,128)S(1)}, f32[256,128]{1,0:T(8,128)S(1)}, u32[]{:S(2)}, u32[]{:S(2)}) collective-permute-start(f32[256,128]{1,0:T(8,128)S(1)} %get-tuple-element.169.token_ref), channel_id=1, source_target_pairs={{0,4},{4,0},{8,12},{12,8},{1,5},{5,1},{9,13},{13,9},{2,6},{6,2},{1... | collective-permute-start | bytes 393224 | tf_op jit(solution)/shard_map/ppermute | solution.py:395
  38.7 1.9 %collective-permute-start.22 = (f32[256,128]{1,0:T(8,128)S(1)}, f32[256,128]{1,0:T(8,128)S(1)}, u32[]{:S(2)}, u32[]{:S(2)}) collective-permute-start(f32[256,128]{1,0:T(8,128)S(1)} %get-tuple-element.170.token_ref), channel_id=1, source_target_pairs={{0,4},{4,0},{8,12},{12,8},{1,5},{5,1},{9,13},{13,9},{2,6},{6,2},{1... | collective-permute-start | bytes 393224 | tf_op jit(solution)/shard_map/ppermute | solution.py:395
  41.5 1.9 %collective-permute-start.24 = (f32[256,128]{1,0:T(8,128)S(1)}, f32[256,128]{1,0:T(8,128)S(1)}, u32[]{:S(2)}, u32[]{:S(2)}) collective-permute-start(f32[256,128]{1,0:T(8,128)S(1)} %get-tuple-element.171.token_ref), channel_id=1, source_target_pairs={{0,4},{4,0},{8,12},{12,8},{1,5},{5,1},{9,13},{13,9},{2,6},{6,2},{1... | collective-permute-start | bytes 393224 | tf_op jit(solution)/shard_map/ppermute | solution.py:395
  44.3 1.9 %collective-permute-start.26 = (f32[256,128]{1,0:T(8,128)S(1)}, f32[256,128]{1,0:T(8,128)S(1)}, u32[]{:S(2)}, u32[]{:S(2)}) collective-permute-start(f32[256,128]{1,0:T(8,128)S(1)} %get-tuple-element.172.token_ref), channel_id=1, source_target_pairs={{0,4},{4,0},{8,12},{12,8},{1,5},{5,1},{9,13},{13,9},{2,6},{6,2},{1... | collective-permute-start | bytes 393224 | tf_op jit(solution)/shard_map/ppermute | solution.py:395
  47.1 1.9 %collective-permute-start.28 = (f32[256,128]{1,0:T(8,128)S(1)}, f32[256,128]{1,0:T(8,128)S(1)}, u32[]{:S(2)}, u32[]{:S(2)}) collective-permute-start(f32[256,128]{1,0:T(8,128)S(1)} %get-tuple-element.173.token_ref), channel_id=1, source_target_pairs={{0,4},{4,0},{8,12},{12,8},{1,5},{5,1},{9,13},{13,9},{2,6},{6,2},{1... | collective-permute-start | bytes 393224 | tf_op jit(solution)/shard_map/ppermute | solution.py:395
  52.8 1.9 %collective-permute-start.32 = (f32[256,128]{1,0:T(8,128)S(1)}, f32[256,128]{1,0:T(8,128)S(1)}, u32[]{:S(2)}, u32[]{:S(2)}) collective-permute-start(f32[256,128]{1,0:T(8,128)S(1)} %get-tuple-element.179.token_ref), channel_id=1, source_target_pairs={{0,4},{4,0},{8,12},{12,8},{1,5},{5,1},{9,13},{13,9},{2,6},{6,2},{1... | collective-permute-start | bytes 393224 | tf_op jit(solution)/shard_map/ppermute | solution.py:395
  58.4 1.9 %collective-permute-start.36 = (f32[256,128]{1,0:T(8,128)S(1)}, f32[256,128]{1,0:T(8,128)S(1)}, u32[]{:S(2)}, u32[]{:S(2)}) collective-permute-start(f32[256,128]{1,0:T(8,128)S(1)} %get-tuple-element.185.token_ref), channel_id=1, source_target_pairs={{0,4},{4,0},{8,12},{12,8},{1,5},{5,1},{9,13},{13,9},{2,6},{6,2},{1... | collective-permute-start | bytes 393224 | tf_op jit(solution)/shard_map/ppermute | solution.py:395
  61.2 1.9 %collective-permute-start.38 = (f32[256,128]{1,0:T(8,128)S(1)}, f32[256,128]{1,0:T(8,128)S(1)}, u32[]{:S(2)}, u32[]{:S(2)}) collective-permute-start(f32[256,128]{1,0:T(8,128)S(1)} %get-tuple-element.188.token_ref), channel_id=1, source_target_pairs={{0,4},{4,0},{8,12},{12,8},{1,5},{5,1},{9,13},{13,9},{2,6},{6,2},{1... | collective-permute-start | bytes 393224 | tf_op jit(solution)/shard_map/ppermute | solution.py:395
  64.0 1.9 %collective-permute-start.40 = (f32[256,128]{1,0:T(8,128)S(1)}, f32[256,128]{1,0:T(8,128)S(1)}, u32[]{:S(2)}, u32[]{:S(2)}) collective-permute-start(f32[256,128]{1,0:T(8,128)S(1)} %get-tuple-element.191.token_ref), channel_id=1, source_target_pairs={{0,4},{4,0},{8,12},{12,8},{1,5},{5,1},{9,13},{13,9},{2,6},{6,2},{1... | collective-permute-start | bytes 393224 | tf_op jit(solution)/shard_map/ppermute | solution.py:395
  66.8 1.9 %collective-permute-start.42 = (f32[256,128]{1,0:T(8,128)S(1)}, f32[256,128]{1,0:T(8,128)S(1)}, u32[]{:S(2)}, u32[]{:S(2)}) collective-permute-start(f32[256,128]{1,0:T(8,128)S(1)} %get-tuple-element.194.token_ref), channel_id=1, source_target_pairs={{0,4},{4,0},{8,12},{12,8},{1,5},{5,1},{9,13},{13,9},{2,6},{6,2},{1... | collective-permute-start | bytes 393224 | tf_op jit(solution)/shard_map/ppermute | solution.py:395
  69.6 1.9 %collective-permute-start.44 = (f32[256,128]{1,0:T(8,128)S(1)}, f32[256,128]{1,0:T(8,128)S(1)}, u32[]{:S(2)}, u32[]{:S(2)}) collective-permute-start(f32[256,128]{1,0:T(8,128)S(1)} %get-tuple-element.197.token_ref), channel_id=1, source_target_pairs={{0,4},{4,0},{8,12},{12,8},{1,5},{5,1},{9,13},{13,9},{2,6},{6,2},{1... | collective-permute-start | bytes 393224 | tf_op jit(solution)/shard_map/ppermute | solution.py:395
  72.5 1.9 %collective-permute-start.46 = (f32[256,128]{1,0:T(8,128)S(1)}, f32[256,128]{1,0:T(8,128)S(1)}, u32[]{:S(2)}, u32[]{:S(2)}) collective-permute-start(f32[256,128]{1,0:T(8,128)S(1)} %get-tuple-element.200.token_ref), channel_id=1, source_target_pairs={{0,4},{4,0},{8,12},{12,8},{1,5},{5,1},{9,13},{13,9},{2,6},{6,2},{1... | collective-permute-start | bytes 393224 | tf_op jit(solution)/shard_map/ppermute | solution.py:395
  75.3 1.9 %collective-permute-start.48 = (f32[256,128]{1,0:T(8,128)S(1)}, f32[256,128]{1,0:T(8,128)S(1)}, u32[]{:S(2)}, u32[]{:S(2)}) collective-permute-start(f32[256,128]{1,0:T(8,128)S(1)} %get-tuple-element.203.token_ref), channel_id=1, source_target_pairs={{0,4},{4,0},{8,12},{12,8},{1,5},{5,1},{9,13},{13,9},{2,6},{6,2},{1... | collective-permute-start | bytes 393224 | tf_op jit(solution)/shard_map/ppermute | solution.py:395
  78.1 1.9 %collective-permute-start.50 = (f32[256,128]{1,0:T(8,128)S(1)}, f32[256,128]{1,0:T(8,128)S(1)}, u32[]{:S(2)}, u32[]{:S(2)}) collective-permute-start(f32[256,128]{1,0:T(8,128)S(1)} %get-tuple-element.206.token_ref), channel_id=1, source_target_pairs={{0,4},{4,0},{8,12},{12,8},{1,5},{5,1},{9,13},{13,9},{2,6},{6,2},{1... | collective-permute-start | bytes 393224 | tf_op jit(solution)/shard_map/ppermute | solution.py:395
  80.9 1.9 %collective-permute-start.52 = (f32[256,128]{1,0:T(8,128)S(1)}, f32[256,128]{1,0:T(8,128)S(1)}, u32[]{:S(2)}, u32[]{:S(2)}) collective-permute-start(f32[256,128]{1,0:T(8,128)S(1)} %get-tuple-element.209.token_ref), channel_id=1, source_target_pairs={{0,4},{4,0},{8,12},{12,8},{1,5},{5,1},{9,13},{13,9},{2,6},{6,2},{1... | collective-permute-start | bytes 393224 | tf_op jit(solution)/shard_map/ppermute | solution.py:395
  83.7 1.9 %collective-permute-start.54 = (f32[256,128]{1,0:T(8,128)S(1)}, f32[256,128]{1,0:T(8,128)S(1)}, u32[]{:S(2)}, u32[]{:S(2)}) collective-permute-start(f32[256,128]{1,0:T(8,128)S(1)} %get-tuple-element.212.token_ref), channel_id=1, source_target_pairs={{0,4},{4,0},{8,12},{12,8},{1,5},{5,1},{9,13},{13,9},{2,6},{6,2},{1... | collective-permute-start | bytes 393224 | tf_op jit(solution)/shard_map/ppermute | solution.py:395
  86.5 1.9 %collective-permute-start.56 = (f32[256,128]{1,0:T(8,128)S(1)}, f32[256,128]{1,0:T(8,128)S(1)}, u32[]{:S(2)}, u32[]{:S(2)}) collective-permute-start(f32[256,128]{1,0:T(8,128)S(1)} %get-tuple-element.215.token_ref), channel_id=1, source_target_pairs={{0,4},{4,0},{8,12},{12,8},{1,5},{5,1},{9,13},{13,9},{2,6},{6,2},{1... | collective-permute-start | bytes 393224 | tf_op jit(solution)/shard_map/ppermute | solution.py:395
  89.3 1.9 %collective-permute-start.58 = (f32[256,128]{1,0:T(8,128)S(1)}, f32[256,128]{1,0:T(8,128)S(1)}, u32[]{:S(2)}, u32[]{:S(2)}) collective-permute-start(f32[256,128]{1,0:T(8,128)S(1)} %get-tuple-element.218.token_ref), channel_id=1, source_target_pairs={{0,4},{4,0},{8,12},{12,8},{1,5},{5,1},{9,13},{13,9},{2,6},{6,2},{1... | collective-permute-start | bytes 393224 | tf_op jit(solution)/shard_map/ppermute | solution.py:395
  92.1 1.9 %collective-permute-start.60 = (f32[256,128]{1,0:T(8,128)S(1)}, f32[256,128]{1,0:T(8,128)S(1)}, u32[]{:S(2)}, u32[]{:S(2)}) collective-permute-start(f32[256,128]{1,0:T(8,128)S(1)} %get-tuple-element.221.token_ref), channel_id=1, source_target_pairs={{0,4},{4,0},{8,12},{12,8},{1,5},{5,1},{9,13},{13,9},{2,6},{6,2},{1... | collective-permute-start | bytes 393224 | tf_op jit(solution)/shard_map/ppermute | solution.py:395
  105.6 1.9 %collective-permute-start.68 = (f32[256,128]{1,0:T(8,128)S(1)}, f32[256,128]{1,0:T(8,128)S(1)}, u32[]{:S(2)}, u32[]{:S(2)}) collective-permute-start(f32[256,128]{1,0:T(8,128)S(1)} %merge.73.token_ref.near_ref), channel_id=1, source_target_pairs={{0,4},{4,0},{8,12},{12,8},{1,5},{5,1},{9,13},{13,9},{2,6},{6,2},{1... | collective-permute-start | bytes 393224 | tf_op jit(solution)/shard_map/ppermute | solution.py:395
  108.5 2.2 %collective-permute-done.67.far_ref = f32[256,128]{1,0:T(8,128)S(1)} collective-permute-done((f32[256,128]{1,0:T(8,128)S(1)}, f32[256,128]{1,0:T(8,128)S(1)}, u32[]{:S(2)}, u32[]{:S(2)}) %collective-permute-start.67) | collective-permute-done | bytes 131104 | tf_op jit(solution)/shard_map/ppermute | solution.py:395
  118.5 5.4 %collective-permute-done.70.other_ref = f32[512,128]{1,0:T(8,128)S(1)} collective-permute-done((f32[512,128]{1,0:T(8,128)S(1)}, f32[512,128]{1,0:T(8,128)S(1)}, u32[]{:S(2)}, u32[]{:S(2)}) %collective-permute-start.70) | collective-permute-done | bytes 262176 | tf_op jit(solution)/shard_map/ppermute | solution.py:432
  (240 shorter events, 53.6 us)
Async XLA Ops:
  3.0 10.1 %collective-permute-start = (f32[256,128]{1,0:T(8,128)S(1)}, f32[256,128]{1,0:T(8,128)S(1)}, u32[]{:S(2)}, u32[]{:S(2)}) collective-permute-start(f32[256,128]{1,0:T(8,128)S(1)} %merge.39), channel_id=1, source_target_pairs={{0,4},{4,0},{8,12},{12,8},{1,5},{5,1},{9,13},{13,9},{2,6},{6,2},{1... | collective-permute-start | bytes 393224 | tf_op jit(solution)/shard_map/ppermute | solution.py:395
  6.1 11.0 %collective-permute-start.1 = (f32[256,128]{1,0:T(8,128)S(1)}, f32[256,128]{1,0:T(8,128)S(1)}, u32[]{:S(2)}, u32[]{:S(2)}) collective-permute-start(f32[256,128]{1,0:T(8,128)S(1)} %merge.37.token_ref), channel_id=1, source_target_pairs={{0,4},{4,0},{8,12},{12,8},{1,5},{5,1},{9,13},{13,9},{2,6},{6,2},{1... | collective-permute-start | bytes 393224 | tf_op jit(solution)/shard_map/ppermute | solution.py:395
  10.3 8.2 %collective-permute-start.2 = (f32[256,128]{1,0:T(8,128)S(1)}, f32[256,128]{1,0:T(8,128)S(1)}, u32[]{:S(2)}, u32[]{:S(2)}) collective-permute-start(f32[256,128]{1,0:T(8,128)S(1)} %merge.38.token_ref), channel_id=1, source_target_pairs={{0,4},{4,0},{8,12},{12,8},{1,5},{5,1},{9,13},{13,9},{2,6},{6,2},{1... | collective-permute-start | bytes 393224 | tf_op jit(solution)/shard_map/ppermute | solution.py:395
  13.2 7.8 %collective-permute-start.4 = (f32[256,128]{1,0:T(8,128)S(1)}, f32[256,128]{1,0:T(8,128)S(1)}, u32[]{:S(2)}, u32[]{:S(2)}) collective-permute-start(f32[256,128]{1,0:T(8,128)S(1)} %merge.40.token_ref), channel_id=1, source_target_pairs={{0,4},{4,0},{8,12},{12,8},{1,5},{5,1},{9,13},{13,9},{2,6},{6,2},{1... | collective-permute-start | bytes 393224 | tf_op jit(solution)/shard_map/ppermute | solution.py:395
  18.7 8.6 %collective-permute-start.8 = (f32[256,128]{1,0:T(8,128)S(1)}, f32[256,128]{1,0:T(8,128)S(1)}, u32[]{:S(2)}, u32[]{:S(2)}) collective-permute-start(f32[256,128]{1,0:T(8,128)S(1)} %get-tuple-element.163.token_ref), channel_id=1, source_target_pairs={{0,4},{4,0},{8,12},{12,8},{1,5},{5,1},{9,13},{13,9},{2,6},{6,2},{1... | collective-permute-start | bytes 393224 | tf_op jit(solution)/shard_map/ppermute | solution.py:395
  21.2 9.0 %collective-permute-start.10 = (f32[256,128]{1,0:T(8,128)S(1)}, f32[256,128]{1,0:T(8,128)S(1)}, u32[]{:S(2)}, u32[]{:S(2)}) collective-permute-start(f32[256,128]{1,0:T(8,128)S(1)} %get-tuple-element.164.token_ref), channel_id=1, source_target_pairs={{0,4},{4,0},{8,12},{12,8},{1,5},{5,1},{9,13},{13,9},{2,6},{6,2},{1... | collective-permute-start | bytes 393224 | tf_op jit(solution)/shard_map/ppermute | solution.py:395
  24.1 8.8 %collective-permute-start.12 = (f32[256,128]{1,0:T(8,128)S(1)}, f32[256,128]{1,0:T(8,128)S(1)}, u32[]{:S(2)}, u32[]{:S(2)}) collective-permute-start(f32[256,128]{1,0:T(8,128)S(1)} %get-tuple-element.165.token_ref), channel_id=1, source_target_pairs={{0,4},{4,0},{8,12},{12,8},{1,5},{5,1},{9,13},{13,9},{2,6},{6,2},{1... | collective-permute-start | bytes 393224 | tf_op jit(solution)/shard_map/ppermute | solution.py:395
  27.5 8.3 %collective-permute-start.14 = (f32[256,128]{1,0:T(8,128)S(1)}, f32[256,128]{1,0:T(8,128)S(1)}, u32[]{:S(2)}, u32[]{:S(2)}) collective-permute-start(f32[256,128]{1,0:T(8,128)S(1)} %get-tuple-element.166.token_ref), channel_id=1, source_target_pairs={{0,4},{4,0},{8,12},{12,8},{1,5},{5,1},{9,13},{13,9},{2,6},{6,2},{1... | collective-permute-start | bytes 393224 | tf_op jit(solution)/shard_map/ppermute | solution.py:395
  30.3 8.3 %collective-permute-start.16 = (f32[256,128]{1,0:T(8,128)S(1)}, f32[256,128]{1,0:T(8,128)S(1)}, u32[]{:S(2)}, u32[]{:S(2)}) collective-permute-start(f32[256,128]{1,0:T(8,128)S(1)} %get-tuple-element.167.token_ref), channel_id=1, source_target_pairs={{0,4},{4,0},{8,12},{12,8},{1,5},{5,1},{9,13},{13,9},{2,6},{6,2},{1... | collective-permute-start | bytes 393224 | tf_op jit(solution)/shard_map/ppermute | solution.py:395
  33.1 8.3 %collective-permute-start.18 = (f32[256,128]{1,0:T(8,128)S(1)}, f32[256,128]{1,0:T(8,128)S(1)}, u32[]{:S(2)}, u32[]{:S(2)}) collective-permute-start(f32[256,128]{1,0:T(8,128)S(1)} %get-tuple-element.168.token_ref), channel_id=1, source_target_pairs={{0,4},{4,0},{8,12},{12,8},{1,5},{5,1},{9,13},{13,9},{2,6},{6,2},{1... | collective-permute-start | bytes 393224 | tf_op jit(solution)/shard_map/ppermute | solution.py:395
  35.9 8.3 %collective-permute-start.20 = (f32[256,128]{1,0:T(8,128)S(1)}, f32[256,128]{1,0:T(8,128)S(1)}, u32[]{:S(2)}, u32[]{:S(2)}) collective-permute-start(f32[256,128]{1,0:T(8,128)S(1)} %get-tuple-element.169.token_ref), channel_id=1, source_target_pairs={{0,4},{4,0},{8,12},{12,8},{1,5},{5,1},{9,13},{13,9},{2,6},{6,2},{1... | collective-permute-start | bytes 393224 | tf_op jit(solution)/shard_map/ppermute | solution.py:395
  38.7 8.3 %collective-permute-start.22 = (f32[256,128]{1,0:T(8,128)S(1)}, f32[256,128]{1,0:T(8,128)S(1)}, u32[]{:S(2)}, u32[]{:S(2)}) collective-permute-start(f32[256,128]{1,0:T(8,128)S(1)} %get-tuple-element.170.token_ref), channel_id=1, source_target_pairs={{0,4},{4,0},{8,12},{12,8},{1,5},{5,1},{9,13},{13,9},{2,6},{6,2},{1... | collective-permute-start | bytes 393224 | tf_op jit(solution)/shard_map/ppermute | solution.py:395
  41.5 8.3 %collective-permute-start.24 = (f32[256,128]{1,0:T(8,128)S(1)}, f32[256,128]{1,0:T(8,128)S(1)}, u32[]{:S(2)}, u32[]{:S(2)}) collective-permute-start(f32[256,128]{1,0:T(8,128)S(1)} %get-tuple-element.171.token_ref), channel_id=1, source_target_pairs={{0,4},{4,0},{8,12},{12,8},{1,5},{5,1},{9,13},{13,9},{2,6},{6,2},{1... | collective-permute-start | bytes 393224 | tf_op jit(solution)/shard_map/ppermute | solution.py:395
  44.3 8.3 %collective-permute-start.26 = (f32[256,128]{1,0:T(8,128)S(1)}, f32[256,128]{1,0:T(8,128)S(1)}, u32[]{:S(2)}, u32[]{:S(2)}) collective-permute-start(f32[256,128]{1,0:T(8,128)S(1)} %get-tuple-element.172.token_ref), channel_id=1, source_target_pairs={{0,4},{4,0},{8,12},{12,8},{1,5},{5,1},{9,13},{13,9},{2,6},{6,2},{1... | collective-permute-start | bytes 393224 | tf_op jit(solution)/shard_map/ppermute | solution.py:395
  47.1 8.3 %collective-permute-start.28 = (f32[256,128]{1,0:T(8,128)S(1)}, f32[256,128]{1,0:T(8,128)S(1)}, u32[]{:S(2)}, u32[]{:S(2)}) collective-permute-start(f32[256,128]{1,0:T(8,128)S(1)} %get-tuple-element.173.token_ref), channel_id=1, source_target_pairs={{0,4},{4,0},{8,12},{12,8},{1,5},{5,1},{9,13},{13,9},{2,6},{6,2},{1... | collective-permute-start | bytes 393224 | tf_op jit(solution)/shard_map/ppermute | solution.py:395
  50.0 8.3 %collective-permute-start.30 = (f32[256,128]{1,0:T(8,128)S(1)}, f32[256,128]{1,0:T(8,128)S(1)}, u32[]{:S(2)}, u32[]{:S(2)}) collective-permute-start(f32[256,128]{1,0:T(8,128)S(1)} %get-tuple-element.176.token_ref), channel_id=1, source_target_pairs={{0,4},{4,0},{8,12},{12,8},{1,5},{5,1},{9,13},{13,9},{2,6},{6,2},{1... | collective-permute-start | bytes 393224 | tf_op jit(solution)/shard_map/ppermute | solution.py:395
  52.8 8.3 %collective-permute-start.32 = (f32[256,128]{1,0:T(8,128)S(1)}, f32[256,128]{1,0:T(8,128)S(1)}, u32[]{:S(2)}, u32[]{:S(2)}) collective-permute-start(f32[256,128]{1,0:T(8,128)S(1)} %get-tuple-element.179.token_ref), channel_id=1, source_target_pairs={{0,4},{4,0},{8,12},{12,8},{1,5},{5,1},{9,13},{13,9},{2,6},{6,2},{1... | collective-permute-start | bytes 393224 | tf_op jit(solution)/shard_map/ppermute | solution.py:395
  55.8 8.1 %collective-permute-start.34 = (f32[256,128]{1,0:T(8,128)S(1)}, f32[256,128]{1,0:T(8,128)S(1)}, u32[]{:S(2)}, u32[]{:S(2)}) collective-permute-start(f32[256,128]{1,0:T(8,128)S(1)} %get-tuple-element.182.token_ref), channel_id=1, source_target_pairs={{0,4},{4,0},{8,12},{12,8},{1,5},{5,1},{9,13},{13,9},{2,6},{6,2},{1... | collective-permute-start | bytes 393224 | tf_op jit(solution)/shard_map/ppermute | solution.py:395
  58.4 8.3 %collective-permute-start.36 = (f32[256,128]{1,0:T(8,128)S(1)}, f32[256,128]{1,0:T(8,128)S(1)}, u32[]{:S(2)}, u32[]{:S(2)}) collective-permute-start(f32[256,128]{1,0:T(8,128)S(1)} %get-tuple-element.185.token_ref), channel_id=1, source_target_pairs={{0,4},{4,0},{8,12},{12,8},{1,5},{5,1},{9,13},{13,9},{2,6},{6,2},{1... | collective-permute-start | bytes 393224 | tf_op jit(solution)/shard_map/ppermute | solution.py:395
  61.2 8.3 %collective-permute-start.38 = (f32[256,128]{1,0:T(8,128)S(1)}, f32[256,128]{1,0:T(8,128)S(1)}, u32[]{:S(2)}, u32[]{:S(2)}) collective-permute-start(f32[256,128]{1,0:T(8,128)S(1)} %get-tuple-element.188.token_ref), channel_id=1, source_target_pairs={{0,4},{4,0},{8,12},{12,8},{1,5},{5,1},{9,13},{13,9},{2,6},{6,2},{1... | collective-permute-start | bytes 393224 | tf_op jit(solution)/shard_map/ppermute | solution.py:395
  64.0 8.3 %collective-permute-start.40 = (f32[256,128]{1,0:T(8,128)S(1)}, f32[256,128]{1,0:T(8,128)S(1)}, u32[]{:S(2)}, u32[]{:S(2)}) collective-permute-start(f32[256,128]{1,0:T(8,128)S(1)} %get-tuple-element.191.token_ref), channel_id=1, source_target_pairs={{0,4},{4,0},{8,12},{12,8},{1,5},{5,1},{9,13},{13,9},{2,6},{6,2},{1... | collective-permute-start | bytes 393224 | tf_op jit(solution)/shard_map/ppermute | solution.py:395
  66.8 8.3 %collective-permute-start.42 = (f32[256,128]{1,0:T(8,128)S(1)}, f32[256,128]{1,0:T(8,128)S(1)}, u32[]{:S(2)}, u32[]{:S(2)}) collective-permute-start(f32[256,128]{1,0:T(8,128)S(1)} %get-tuple-element.194.token_ref), channel_id=1, source_target_pairs={{0,4},{4,0},{8,12},{12,8},{1,5},{5,1},{9,13},{13,9},{2,6},{6,2},{1... | collective-permute-start | bytes 393224 | tf_op jit(solution)/shard_map/ppermute | solution.py:395
  69.6 8.3 %collective-permute-start.44 = (f32[256,128]{1,0:T(8,128)S(1)}, f32[256,128]{1,0:T(8,128)S(1)}, u32[]{:S(2)}, u32[]{:S(2)}) collective-permute-start(f32[256,128]{1,0:T(8,128)S(1)} %get-tuple-element.197.token_ref), channel_id=1, source_target_pairs={{0,4},{4,0},{8,12},{12,8},{1,5},{5,1},{9,13},{13,9},{2,6},{6,2},{1... | collective-permute-start | bytes 393224 | tf_op jit(solution)/shard_map/ppermute | solution.py:395
  72.5 8.3 %collective-permute-start.46 = (f32[256,128]{1,0:T(8,128)S(1)}, f32[256,128]{1,0:T(8,128)S(1)}, u32[]{:S(2)}, u32[]{:S(2)}) collective-permute-start(f32[256,128]{1,0:T(8,128)S(1)} %get-tuple-element.200.token_ref), channel_id=1, source_target_pairs={{0,4},{4,0},{8,12},{12,8},{1,5},{5,1},{9,13},{13,9},{2,6},{6,2},{1... | collective-permute-start | bytes 393224 | tf_op jit(solution)/shard_map/ppermute | solution.py:395
  75.3 8.3 %collective-permute-start.48 = (f32[256,128]{1,0:T(8,128)S(1)}, f32[256,128]{1,0:T(8,128)S(1)}, u32[]{:S(2)}, u32[]{:S(2)}) collective-permute-start(f32[256,128]{1,0:T(8,128)S(1)} %get-tuple-element.203.token_ref), channel_id=1, source_target_pairs={{0,4},{4,0},{8,12},{12,8},{1,5},{5,1},{9,13},{13,9},{2,6},{6,2},{1... | collective-permute-start | bytes 393224 | tf_op jit(solution)/shard_map/ppermute | solution.py:395
  78.1 8.3 %collective-permute-start.50 = (f32[256,128]{1,0:T(8,128)S(1)}, f32[256,128]{1,0:T(8,128)S(1)}, u32[]{:S(2)}, u32[]{:S(2)}) collective-permute-start(f32[256,128]{1,0:T(8,128)S(1)} %get-tuple-element.206.token_ref), channel_id=1, source_target_pairs={{0,4},{4,0},{8,12},{12,8},{1,5},{5,1},{9,13},{13,9},{2,6},{6,2},{1... | collective-permute-start | bytes 393224 | tf_op jit(solution)/shard_map/ppermute | solution.py:395
  80.9 8.3 %collective-permute-start.52 = (f32[256,128]{1,0:T(8,128)S(1)}, f32[256,128]{1,0:T(8,128)S(1)}, u32[]{:S(2)}, u32[]{:S(2)}) collective-permute-start(f32[256,128]{1,0:T(8,128)S(1)} %get-tuple-element.209.token_ref), channel_id=1, source_target_pairs={{0,4},{4,0},{8,12},{12,8},{1,5},{5,1},{9,13},{13,9},{2,6},{6,2},{1... | collective-permute-start | bytes 393224 | tf_op jit(solution)/shard_map/ppermute | solution.py:395
  83.7 8.3 %collective-permute-start.54 = (f32[256,128]{1,0:T(8,128)S(1)}, f32[256,128]{1,0:T(8,128)S(1)}, u32[]{:S(2)}, u32[]{:S(2)}) collective-permute-start(f32[256,128]{1,0:T(8,128)S(1)} %get-tuple-element.212.token_ref), channel_id=1, source_target_pairs={{0,4},{4,0},{8,12},{12,8},{1,5},{5,1},{9,13},{13,9},{2,6},{6,2},{1... | collective-permute-start | bytes 393224 | tf_op jit(solution)/shard_map/ppermute | solution.py:395
  86.5 8.7 %collective-permute-start.56 = (f32[256,128]{1,0:T(8,128)S(1)}, f32[256,128]{1,0:T(8,128)S(1)}, u32[]{:S(2)}, u32[]{:S(2)}) collective-permute-start(f32[256,128]{1,0:T(8,128)S(1)} %get-tuple-element.215.token_ref), channel_id=1, source_target_pairs={{0,4},{4,0},{8,12},{12,8},{1,5},{5,1},{9,13},{13,9},{2,6},{6,2},{1... | collective-permute-start | bytes 393224 | tf_op jit(solution)/shard_map/ppermute | solution.py:395
  89.3 8.9 %collective-permute-start.58 = (f32[256,128]{1,0:T(8,128)S(1)}, f32[256,128]{1,0:T(8,128)S(1)}, u32[]{:S(2)}, u32[]{:S(2)}) collective-permute-start(f32[256,128]{1,0:T(8,128)S(1)} %get-tuple-element.218.token_ref), channel_id=1, source_target_pairs={{0,4},{4,0},{8,12},{12,8},{1,5},{5,1},{9,13},{13,9},{2,6},{6,2},{1... | collective-permute-start | bytes 393224 | tf_op jit(solution)/shard_map/ppermute | solution.py:395
  92.1 9.2 %collective-permute-start.60 = (f32[256,128]{1,0:T(8,128)S(1)}, f32[256,128]{1,0:T(8,128)S(1)}, u32[]{:S(2)}, u32[]{:S(2)}) collective-permute-start(f32[256,128]{1,0:T(8,128)S(1)} %get-tuple-element.221.token_ref), channel_id=1, source_target_pairs={{0,4},{4,0},{8,12},{12,8},{1,5},{5,1},{9,13},{13,9},{2,6},{6,2},{1... | collective-permute-start | bytes 393224 | tf_op jit(solution)/shard_map/ppermute | solution.py:395
  115.5 8.4 %collective-permute-start.70 = (f32[512,128]{1,0:T(8,128)S(1)}, f32[512,128]{1,0:T(8,128)S(1)}, u32[]{:S(2)}, u32[]{:S(2)}) collective-permute-start(f32[512,128]{1,0:T(8,128)S(1)} %add.3.token_ref.part_ref), channel_id=1, source_target_pairs={{0,2},{2,0},{1,3},{3,1},{4,6},{6,4},{5,7},{7,5},{8,10},{10,8},{9,1... | collective-permute-start | bytes 786440 | tf_op jit(solution)/shard_map/ppermute | solution.py:432
  (45 other events, 262.5 us)

commit v6 on v5

--- a/solution.py
+++ b/solution.py
@@ -172,10 +172,31 @@
         store.wait()
 
 
-def halves_kernel(high_ref, grad_ref, keep_ref, send_ref):
-    half = keep_ref.shape[0]
-    keep_ref[...] = grad_ref[pl.ds(pl.multiple_of(high_ref[0] * half, half), half), :]
-    send_ref[...] = grad_ref[pl.ds(pl.multiple_of((1 - high_ref[0]) * half, half), half), :]
+def half_share(start, at, width, pair_ref, new, mat_ref, grad_ref, out_ref):
+    high, low = split(new)
+    twice = jnp.concatenate([high, high], axis=1)
+    pair = jnp.concatenate([high, low], axis=1)
+    rank, half = new.shape[1], out_ref.shape[0]
+    rows = pl.ds(pl.multiple_of(start * half, half), half)
+    slopes = slopes_of(pair_ref[rows, :], twice, mat_ref[rows, pl.ds(at, width)])
+    term = jnp.dot(slopes, pair, preferred_element_type=F32)
+    out_ref[...] = grad_ref[rows, :] + term[:, :rank] + term[:, rank:]
+
+
+def send_kernel(
+    at, rows_total, token_ref, outer_ref, high_ref, pair_ref, mat_ref, far_ref, near_ref, col_ref, mean_ref,
+    square_ref, grad_ref, new_ref, out_ref,
+):
+    del token_ref
+    gradient = pick(outer_ref, far_ref, near_ref) / rows_total
+    new, _, _ = adam_move(col_ref[...], gradient, mean_ref[...], square_ref[...], START + 2)
+    new_ref[...] = new
+    half_share(1 - high_ref[0], at, new.shape[0], pair_ref, new, mat_ref, grad_ref, out_ref)
+
+
+def keep_kernel(at, token_ref, high_ref, pair_ref, mat_ref, new_ref, grad_ref, out_ref):
+    del token_ref
+    half_share(high_ref[0], at, new_ref.shape[0], pair_ref, new_ref[...], mat_ref, grad_ref, out_ref)
 
 
 def row_kernel(cols_total, token_ref, high_ref, part_ref, other_ref, row_ref, mean_ref, square_ref, new_ref):
@@ -228,7 +249,7 @@
 
 
 class Work:
-    def __init__(self, outer, high, matrix, row_factor, col_factor, col_mean, col_square, rows_total):
+    def __init__(self, outer, high, halved, matrix, row_factor, col_factor, col_mean, col_square, rows_total):
         self.outer, self.high, self.rows_total = outer, high, rows_total
         self.matrix, self.row = matrix, row_factor
         self.state = [col_factor, col_mean, col_square]
@@ -236,7 +257,7 @@
         self.chunks = chunks_of(col_factor.shape[0])
         self.moved = {}
         self.new = {}
-        self.grad = None
+        self.grad, self.halved = None, halved
 
     def chunk(self, index):
         return (VMEM, (self.chunks[index][1], self.rank), F32)
@@ -290,6 +311,12 @@
         return out
 
     def last(self, indices, far, near, token):
+        final = len(self.chunks) - 1
+        if self.halved and final in indices:
+            if len(indices) > 1:
+                self.last(indices[:-1], far, near, token)
+                token = self.grad
+            return self.halves(final, far[final], near[final], token)
         ins = [(ANY, token), (SMEM, self.outer), (VMEM, self.pair), (VMEM, self.matrix)]
         for index in indices:
             ins += [(VMEM, array) for array in (far[index], near[index], *self.moved[index])]
@@ -304,6 +331,24 @@
             aliases=aliases,
         )
         self.new.update(zip(indices, new, strict=True))
+
+    def halves(self, index, far, near, token):
+        at = self.chunks[index][0]
+        rows, rank = self.row.shape
+        half = (VMEM, (rows // 2, rank), F32)
+        ins = [(VMEM, array) for array in (far, near, *self.moved[index], self.grad)]
+        self.new[index], send = call(
+            functools.partial(send_kernel, at, self.rows_total), "send",
+            [(ANY, token), (SMEM, self.outer), (SMEM, self.high), (VMEM, self.pair), (VMEM, self.matrix), *ins],
+            [self.chunk(index), half],
+        )
+        (keep,) = call(
+            functools.partial(keep_kernel, at), "keep",
+            [(ANY, send), (SMEM, self.high)]
+            + [(VMEM, array) for array in (self.pair, self.matrix, self.new[index], self.grad)],
+            [half],
+        )
+        self.ends = keep, send
 
     def new_cols(self, token):
         return call(
@@ -422,12 +467,12 @@
 
 
 def row_step(work, row_mean, row_square, cols_total):
-    high, grad = work.high, work.grad
-    rows, rank = grad.shape
+    high = work.high
+    rows, rank = work.row.shape
     half = (VMEM, (rows // 2, rank), F32)
     swap = [(0, 1), (1, 0), (2, 3), (3, 2)]
     across = [(0, 2), (2, 0), (1, 3), (3, 1)]
-    keep, send = call(halves_kernel, "halves", [(SMEM, high), (VMEM, grad)], [half, half])
+    keep, send = work.ends
     part = keep + lax.ppermute(send, "col", swap)
     other = lax.ppermute(part, "col", across)
     new_cols, stored = work.new_cols(part)
@@ -439,7 +484,7 @@
     (out,) = call(
         join_kernel, "join",
         [(SMEM, high), (VMEM, new), (VMEM, other)],
-        [(HBM, grad.shape, F32)],
+        [(HBM, work.row.shape, F32)],
         scratch=[pltpu.SemaphoreType.DMA((2,))],
     )
     return out, new_cols
@@ -451,7 +496,7 @@
     row, col = lax.axis_index("row"), lax.axis_index("col")
     outer = ((row == 0) | (row == n_row - 1)).astype(jnp.int32).reshape(1)
     high = (col & 1).astype(jnp.int32).reshape(1)
-    work = Work(outer, high, matrix, row_factor, col_factor, col_mean, col_square, matrix.shape[0] * n_row)
+    work = Work(outer, high, n_col == 4, matrix, row_factor, col_factor, col_mean, col_square, matrix.shape[0] * n_row)
     if n_row == 4 and n_col % 2 == 0:
         line_columns(work)
     else:

time: 127 us -> 127 us (level)
  no operation moved by 1% of the time
where the time goes in v6:
time: 127 us; the launch traced here: 126 us
  starting transfers between devices  71.9 us (57%)
  Pallas kernels  39.7 us (31%)
  waiting for transfers between devices  12.3 us (10%)
  between operations  2.46 us (2%)
    ppermute x37, starting transfers between devices, line_columns(): from_outer[k] = lax.ppermute(payload, 'row', outer_pairs)  67.7 us
    pallas_call x117, Pallas kernels, call(): pl.pallas_call(kernel, out_shape=[jax.ShapeDtypeStruct(shape, kind) for _...  39.7 us
    ppermute x1, waiting for transfers between devices, row_step(): other = lax.ppermute(part, 'col', across)  5.41 us
    ppermute x37, waiting for transfers between devices, line_columns(): from_outer[k] = lax.ppermute(payload, 'row', outer_pairs)  4.29 us
  transfers between devices with their start and end apart: 72, of which 6 were waited for; matrix products, arithmetic and copies ran while one was open for 0% of the time, Pallas kernels for 28%

profile of v6, /device:TPU:0, one launch (start us, length us, event | category | flops | bytes accessed | tf_op | source)
XLA Modules:
  0.0 126.5 jit_solution(16361076976273668746)
XLA Ops:
  0.6 2.3 %first.1 = (bf16[1024,256]{1,0:T(8,128)(2,1)S(1)}, bf16[1024,256]{1,0:T(8,128)(2,1)S(1)}, bf16[256,1024]{1,0:T(8,128)(2,1)S(1)}, f32[256,128]{1,0:T(8,128)S(1)}, f32[256,128]{1,0:T(8,128)S(1)}) custom-call(s32[1]{0:T(128)} %bitcast.1.outer_ref, s32[1]{0:T(128)} %bitcast.high_ref, f32[1024,128]{1,0:T(8,128)} %row_ref.1, f32[4096,128]{1,0:T(8,128)} %col_hbm.3, ...), custom_call_target="tpu_custom_call" | custom-call | flops 1 | bytes 1 | tf_op jit(solution)/shard_map/first/pallas_call | solution.py:231
  3.0 3.1 %collective-permute-start = (f32[256,128]{1,0:T(8,128)S(1)}, f32[256,128]{1,0:T(8,128)S(1)}, u32[]{:S(2)}, u32[]{:S(2)}) collective-permute-start(f32[256,128]{1,0:T(8,128)S(1)} %merge.39), channel_id=1, source_target_pairs={{0,4},{4,0},{8,12},{12,8},{1,5},{5,1},{9,13},{13,9},{2,6},{6,2},{1... | collective-permute-start | bytes 393224 | tf_op jit(solution)/shard_map/ppermute | solution.py:440
  6.2 4.1 %third.1 = (f32[4096,128]{1,0:T(8,128)S(1)}, bf16[1024,4096]{1,0:T(8,128)(2,1)S(1)}, f32[256,128]{1,0:T(8,128)S(1)}) custom-call(f32[256,128]{1,0:T(8,128)S(1)} %merge.37.token_ref, f32[4096,128]{1,0:T(8,128)} %col_hbm.3, bf16[1024,4096]{1,0:T(8,128)(2,1)} %mat_hbm.3, bf16[1024,256]{1,0:T(8,128)(2,1)S(1)} %get-tuple-element.155.twice_ref, ...), custom_call_target="tpu_custom_call" | custom-call | flops 1 | bytes 1 | tf_op jit(solution)/shard_map/third/pallas_call | solution.py:231
  10.3 2.1 %collective-permute-start.2 = (f32[256,128]{1,0:T(8,128)S(1)}, f32[256,128]{1,0:T(8,128)S(1)}, u32[]{:S(2)}, u32[]{:S(2)}) collective-permute-start(f32[256,128]{1,0:T(8,128)S(1)} %merge.38.token_ref), channel_id=1, source_target_pairs={{0,4},{4,0},{8,12},{12,8},{1,5},{5,1},{9,13},{13,9},{2,6},{6,2},{1... | collective-permute-start | bytes 393224 | tf_op jit(solution)/shard_map/ppermute | solution.py:440
  13.2 3.2 %collective-permute-start.4 = (f32[256,128]{1,0:T(8,128)S(1)}, f32[256,128]{1,0:T(8,128)S(1)}, u32[]{:S(2)}, u32[]{:S(2)}) collective-permute-start(f32[256,128]{1,0:T(8,128)S(1)} %merge.40.token_ref), channel_id=1, source_target_pairs={{0,4},{4,0},{8,12},{12,8},{1,5},{5,1},{9,13},{13,9},{2,6},{6,2},{1... | collective-permute-start | bytes 393224 | tf_op jit(solution)/shard_map/ppermute | solution.py:440
  21.2 2.1 %collective-permute-start.10 = (f32[256,128]{1,0:T(8,128)S(1)}, f32[256,128]{1,0:T(8,128)S(1)}, u32[]{:S(2)}, u32[]{:S(2)}) collective-permute-start(f32[256,128]{1,0:T(8,128)S(1)} %get-tuple-element.162.token_ref), channel_id=1, source_target_pairs={{0,4},{4,0},{8,12},{12,8},{1,5},{5,1},{9,13},{13,9},{2,6},{6,2},{1... | collective-permute-start | bytes 393224 | tf_op jit(solution)/shard_map/ppermute | solution.py:440
  24.1 2.5 %collective-permute-start.12 = (f32[256,128]{1,0:T(8,128)S(1)}, f32[256,128]{1,0:T(8,128)S(1)}, u32[]{:S(2)}, u32[]{:S(2)}) collective-permute-start(f32[256,128]{1,0:T(8,128)S(1)} %get-tuple-element.163.token_ref), channel_id=1, source_target_pairs={{0,4},{4,0},{8,12},{12,8},{1,5},{5,1},{9,13},{13,9},{2,6},{6,2},{1... | collective-permute-start | bytes 393224 | tf_op jit(solution)/shard_map/ppermute | solution.py:440
  27.5 1.9 %collective-permute-start.14 = (f32[256,128]{1,0:T(8,128)S(1)}, f32[256,128]{1,0:T(8,128)S(1)}, u32[]{:S(2)}, u32[]{:S(2)}) collective-permute-start(f32[256,128]{1,0:T(8,128)S(1)} %get-tuple-element.164.token_ref), channel_id=1, source_target_pairs={{0,4},{4,0},{8,12},{12,8},{1,5},{5,1},{9,13},{13,9},{2,6},{6,2},{1... | collective-permute-start | bytes 393224 | tf_op jit(solution)/shard_map/ppermute | solution.py:440
  30.3 1.9 %collective-permute-start.16 = (f32[256,128]{1,0:T(8,128)S(1)}, f32[256,128]{1,0:T(8,128)S(1)}, u32[]{:S(2)}, u32[]{:S(2)}) collective-permute-start(f32[256,128]{1,0:T(8,128)S(1)} %get-tuple-element.165.token_ref), channel_id=1, source_target_pairs={{0,4},{4,0},{8,12},{12,8},{1,5},{5,1},{9,13},{13,9},{2,6},{6,2},{1... | collective-permute-start | bytes 393224 | tf_op jit(solution)/shard_map/ppermute | solution.py:440
  33.1 1.9 %collective-permute-start.18 = (f32[256,128]{1,0:T(8,128)S(1)}, f32[256,128]{1,0:T(8,128)S(1)}, u32[]{:S(2)}, u32[]{:S(2)}) collective-permute-start(f32[256,128]{1,0:T(8,128)S(1)} %get-tuple-element.166.token_ref), channel_id=1, source_target_pairs={{0,4},{4,0},{8,12},{12,8},{1,5},{5,1},{9,13},{13,9},{2,6},{6,2},{1... | collective-permute-start | bytes 393224 | tf_op jit(solution)/shard_map/ppermute | solution.py:440
  35.9 1.9 %collective-permute-start.20 = (f32[256,128]{1,0:T(8,128)S(1)}, f32[256,128]{1,0:T(8,128)S(1)}, u32[]{:S(2)}, u32[]{:S(2)}) collective-permute-start(f32[256,128]{1,0:T(8,128)S(1)} %get-tuple-element.167.token_ref), channel_id=1, source_target_pairs={{0,4},{4,0},{8,12},{12,8},{1,5},{5,1},{9,13},{13,9},{2,6},{6,2},{1... | collective-permute-start | bytes 393224 | tf_op jit(solution)/shard_map/ppermute | solution.py:440
  38.7 1.9 %collective-permute-start.22 = (f32[256,128]{1,0:T(8,128)S(1)}, f32[256,128]{1,0:T(8,128)S(1)}, u32[]{:S(2)}, u32[]{:S(2)}) collective-permute-start(f32[256,128]{1,0:T(8,128)S(1)} %get-tuple-element.168.token_ref), channel_id=1, source_target_pairs={{0,4},{4,0},{8,12},{12,8},{1,5},{5,1},{9,13},{13,9},{2,6},{6,2},{1... | collective-permute-start | bytes 393224 | tf_op jit(solution)/shard_map/ppermute | solution.py:440
  41.5 1.9 %collective-permute-start.24 = (f32[256,128]{1,0:T(8,128)S(1)}, f32[256,128]{1,0:T(8,128)S(1)}, u32[]{:S(2)}, u32[]{:S(2)}) collective-permute-start(f32[256,128]{1,0:T(8,128)S(1)} %get-tuple-element.169.token_ref), channel_id=1, source_target_pairs={{0,4},{4,0},{8,12},{12,8},{1,5},{5,1},{9,13},{13,9},{2,6},{6,2},{1... | collective-permute-start | bytes 393224 | tf_op jit(solution)/shard_map/ppermute | solution.py:440
  44.3 1.9 %collective-permute-start.26 = (f32[256,128]{1,0:T(8,128)S(1)}, f32[256,128]{1,0:T(8,128)S(1)}, u32[]{:S(2)}, u32[]{:S(2)}) collective-permute-start(f32[256,128]{1,0:T(8,128)S(1)} %get-tuple-element.170.token_ref), channel_id=1, source_target_pairs={{0,4},{4,0},{8,12},{12,8},{1,5},{5,1},{9,13},{13,9},{2,6},{6,2},{1... | collective-permute-start | bytes 393224 | tf_op jit(solution)/shard_map/ppermute | solution.py:440
  47.1 1.9 %collective-permute-start.28 = (f32[256,128]{1,0:T(8,128)S(1)}, f32[256,128]{1,0:T(8,128)S(1)}, u32[]{:S(2)}, u32[]{:S(2)}) collective-permute-start(f32[256,128]{1,0:T(8,128)S(1)} %get-tuple-element.171.token_ref), channel_id=1, source_target_pairs={{0,4},{4,0},{8,12},{12,8},{1,5},{5,1},{9,13},{13,9},{2,6},{6,2},{1... | collective-permute-start | bytes 393224 | tf_op jit(solution)/shard_map/ppermute | solution.py:440
  52.8 1.9 %collective-permute-start.32 = (f32[256,128]{1,0:T(8,128)S(1)}, f32[256,128]{1,0:T(8,128)S(1)}, u32[]{:S(2)}, u32[]{:S(2)}) collective-permute-start(f32[256,128]{1,0:T(8,128)S(1)} %get-tuple-element.177.token_ref), channel_id=1, source_target_pairs={{0,4},{4,0},{8,12},{12,8},{1,5},{5,1},{9,13},{13,9},{2,6},{6,2},{1... | collective-permute-start | bytes 393224 | tf_op jit(solution)/shard_map/ppermute | solution.py:440
  58.4 1.9 %collective-permute-start.36 = (f32[256,128]{1,0:T(8,128)S(1)}, f32[256,128]{1,0:T(8,128)S(1)}, u32[]{:S(2)}, u32[]{:S(2)}) collective-permute-start(f32[256,128]{1,0:T(8,128)S(1)} %get-tuple-element.183.token_ref), channel_id=1, source_target_pairs={{0,4},{4,0},{8,12},{12,8},{1,5},{5,1},{9,13},{13,9},{2,6},{6,2},{1... | collective-permute-start | bytes 393224 | tf_op jit(solution)/shard_map/ppermute | solution.py:440
  61.2 1.9 %collective-permute-start.38 = (f32[256,128]{1,0:T(8,128)S(1)}, f32[256,128]{1,0:T(8,128)S(1)}, u32[]{:S(2)}, u32[]{:S(2)}) collective-permute-start(f32[256,128]{1,0:T(8,128)S(1)} %get-tuple-element.186.token_ref), channel_id=1, source_target_pairs={{0,4},{4,0},{8,12},{12,8},{1,5},{5,1},{9,13},{13,9},{2,6},{6,2},{1... | collective-permute-start | bytes 393224 | tf_op jit(solution)/shard_map/ppermute | solution.py:440
  64.0 1.9 %collective-permute-start.40 = (f32[256,128]{1,0:T(8,128)S(1)}, f32[256,128]{1,0:T(8,128)S(1)}, u32[]{:S(2)}, u32[]{:S(2)}) collective-permute-start(f32[256,128]{1,0:T(8,128)S(1)} %get-tuple-element.189.token_ref), channel_id=1, source_target_pairs={{0,4},{4,0},{8,12},{12,8},{1,5},{5,1},{9,13},{13,9},{2,6},{6,2},{1... | collective-permute-start | bytes 393224 | tf_op jit(solution)/shard_map/ppermute | solution.py:440
  66.8 1.9 %collective-permute-start.42 = (f32[256,128]{1,0:T(8,128)S(1)}, f32[256,128]{1,0:T(8,128)S(1)}, u32[]{:S(2)}, u32[]{:S(2)}) collective-permute-start(f32[256,128]{1,0:T(8,128)S(1)} %get-tuple-element.192.token_ref), channel_id=1, source_target_pairs={{0,4},{4,0},{8,12},{12,8},{1,5},{5,1},{9,13},{13,9},{2,6},{6,2},{1... | collective-permute-start | bytes 393224 | tf_op jit(solution)/shard_map/ppermute | solution.py:440
  69.6 1.9 %collective-permute-start.44 = (f32[256,128]{1,0:T(8,128)S(1)}, f32[256,128]{1,0:T(8,128)S(1)}, u32[]{:S(2)}, u32[]{:S(2)}) collective-permute-start(f32[256,128]{1,0:T(8,128)S(1)} %get-tuple-element.195.token_ref), channel_id=1, source_target_pairs={{0,4},{4,0},{8,12},{12,8},{1,5},{5,1},{9,13},{13,9},{2,6},{6,2},{1... | collective-permute-start | bytes 393224 | tf_op jit(solution)/shard_map/ppermute | solution.py:440
  72.5 1.9 %collective-permute-start.46 = (f32[256,128]{1,0:T(8,128)S(1)}, f32[256,128]{1,0:T(8,128)S(1)}, u32[]{:S(2)}, u32[]{:S(2)}) collective-permute-start(f32[256,128]{1,0:T(8,128)S(1)} %get-tuple-element.198.token_ref), channel_id=1, source_target_pairs={{0,4},{4,0},{8,12},{12,8},{1,5},{5,1},{9,13},{13,9},{2,6},{6,2},{1... | collective-permute-start | bytes 393224 | tf_op jit(solution)/shard_map/ppermute | solution.py:440
  75.3 1.9 %collective-permute-start.48 = (f32[256,128]{1,0:T(8,128)S(1)}, f32[256,128]{1,0:T(8,128)S(1)}, u32[]{:S(2)}, u32[]{:S(2)}) collective-permute-start(f32[256,128]{1,0:T(8,128)S(1)} %get-tuple-element.201.token_ref), channel_id=1, source_target_pairs={{0,4},{4,0},{8,12},{12,8},{1,5},{5,1},{9,13},{13,9},{2,6},{6,2},{1... | collective-permute-start | bytes 393224 | tf_op jit(solution)/shard_map/ppermute | solution.py:440
  78.1 1.9 %collective-permute-start.50 = (f32[256,128]{1,0:T(8,128)S(1)}, f32[256,128]{1,0:T(8,128)S(1)}, u32[]{:S(2)}, u32[]{:S(2)}) collective-permute-start(f32[256,128]{1,0:T(8,128)S(1)} %get-tuple-element.204.token_ref), channel_id=1, source_target_pairs={{0,4},{4,0},{8,12},{12,8},{1,5},{5,1},{9,13},{13,9},{2,6},{6,2},{1... | collective-permute-start | bytes 393224 | tf_op jit(solution)/shard_map/ppermute | solution.py:440
  80.9 1.9 %collective-permute-start.52 = (f32[256,128]{1,0:T(8,128)S(1)}, f32[256,128]{1,0:T(8,128)S(1)}, u32[]{:S(2)}, u32[]{:S(2)}) collective-permute-start(f32[256,128]{1,0:T(8,128)S(1)} %get-tuple-element.207.token_ref), channel_id=1, source_target_pairs={{0,4},{4,0},{8,12},{12,8},{1,5},{5,1},{9,13},{13,9},{2,6},{6,2},{1... | collective-permute-start | bytes 393224 | tf_op jit(solution)/shard_map/ppermute | solution.py:440
  83.7 1.9 %collective-permute-start.54 = (f32[256,128]{1,0:T(8,128)S(1)}, f32[256,128]{1,0:T(8,128)S(1)}, u32[]{:S(2)}, u32[]{:S(2)}) collective-permute-start(f32[256,128]{1,0:T(8,128)S(1)} %get-tuple-element.210.token_ref), channel_id=1, source_target_pairs={{0,4},{4,0},{8,12},{12,8},{1,5},{5,1},{9,13},{13,9},{2,6},{6,2},{1... | collective-permute-start | bytes 393224 | tf_op jit(solution)/shard_map/ppermute | solution.py:440
  86.5 1.9 %collective-permute-start.56 = (f32[256,128]{1,0:T(8,128)S(1)}, f32[256,128]{1,0:T(8,128)S(1)}, u32[]{:S(2)}, u32[]{:S(2)}) collective-permute-start(f32[256,128]{1,0:T(8,128)S(1)} %get-tuple-element.213.token_ref), channel_id=1, source_target_pairs={{0,4},{4,0},{8,12},{12,8},{1,5},{5,1},{9,13},{13,9},{2,6},{6,2},{1... | collective-permute-start | bytes 393224 | tf_op jit(solution)/shard_map/ppermute | solution.py:440
  89.3 1.9 %collective-permute-start.58 = (f32[256,128]{1,0:T(8,128)S(1)}, f32[256,128]{1,0:T(8,128)S(1)}, u32[]{:S(2)}, u32[]{:S(2)}) collective-permute-start(f32[256,128]{1,0:T(8,128)S(1)} %get-tuple-element.216.token_ref), channel_id=1, source_target_pairs={{0,4},{4,0},{8,12},{12,8},{1,5},{5,1},{9,13},{13,9},{2,6},{6,2},{1... | collective-permute-start | bytes 393224 | tf_op jit(solution)/shard_map/ppermute | solution.py:440
  92.1 1.9 %collective-permute-start.60 = (f32[256,128]{1,0:T(8,128)S(1)}, f32[256,128]{1,0:T(8,128)S(1)}, u32[]{:S(2)}, u32[]{:S(2)}) collective-permute-start(f32[256,128]{1,0:T(8,128)S(1)} %get-tuple-element.219.token_ref), channel_id=1, source_target_pairs={{0,4},{4,0},{8,12},{12,8},{1,5},{5,1},{9,13},{13,9},{2,6},{6,2},{1... | collective-permute-start | bytes 393224 | tf_op jit(solution)/shard_map/ppermute | solution.py:440
  105.6 1.9 %collective-permute-start.68 = (f32[256,128]{1,0:T(8,128)S(1)}, f32[256,128]{1,0:T(8,128)S(1)}, u32[]{:S(2)}, u32[]{:S(2)}) collective-permute-start(f32[256,128]{1,0:T(8,128)S(1)} %merge.73.token_ref.near_ref), channel_id=1, source_target_pairs={{0,4},{4,0},{8,12},{12,8},{1,5},{5,1},{9,13},{13,9},{2,6},{6,2},{1... | collective-permute-start | bytes 393224 | tf_op jit(solution)/shard_map/ppermute | solution.py:440
  108.5 2.2 %collective-permute-done.67.far_ref = f32[256,128]{1,0:T(8,128)S(1)} collective-permute-done((f32[256,128]{1,0:T(8,128)S(1)}, f32[256,128]{1,0:T(8,128)S(1)}, u32[]{:S(2)}, u32[]{:S(2)}) %collective-permute-start.67) | collective-permute-done | bytes 131104 | tf_op jit(solution)/shard_map/ppermute | solution.py:440
  118.3 5.4 %collective-permute-done.70.other_ref = f32[512,128]{1,0:T(8,128)S(1)} collective-permute-done((f32[512,128]{1,0:T(8,128)S(1)}, f32[512,128]{1,0:T(8,128)S(1)}, u32[]{:S(2)}, u32[]{:S(2)}) %collective-permute-start.70) | collective-permute-done | bytes 262176 | tf_op jit(solution)/shard_map/ppermute | solution.py:477
  (240 shorter events, 53.4 us)
Async XLA Ops:
  3.0 10.1 %collective-permute-start = (f32[256,128]{1,0:T(8,128)S(1)}, f32[256,128]{1,0:T(8,128)S(1)}, u32[]{:S(2)}, u32[]{:S(2)}) collective-permute-start(f32[256,128]{1,0:T(8,128)S(1)} %merge.39), channel_id=1, source_target_pairs={{0,4},{4,0},{8,12},{12,8},{1,5},{5,1},{9,13},{13,9},{2,6},{6,2},{1... | collective-permute-start | bytes 393224 | tf_op jit(solution)/shard_map/ppermute | solution.py:440
  6.1 11.0 %collective-permute-start.1 = (f32[256,128]{1,0:T(8,128)S(1)}, f32[256,128]{1,0:T(8,128)S(1)}, u32[]{:S(2)}, u32[]{:S(2)}) collective-permute-start(f32[256,128]{1,0:T(8,128)S(1)} %merge.37.token_ref), channel_id=1, source_target_pairs={{0,4},{4,0},{8,12},{12,8},{1,5},{5,1},{9,13},{13,9},{2,6},{6,2},{1... | collective-permute-start | bytes 393224 | tf_op jit(solution)/shard_map/ppermute | solution.py:440
  10.3 8.2 %collective-permute-start.2 = (f32[256,128]{1,0:T(8,128)S(1)}, f32[256,128]{1,0:T(8,128)S(1)}, u32[]{:S(2)}, u32[]{:S(2)}) collective-permute-start(f32[256,128]{1,0:T(8,128)S(1)} %merge.38.token_ref), channel_id=1, source_target_pairs={{0,4},{4,0},{8,12},{12,8},{1,5},{5,1},{9,13},{13,9},{2,6},{6,2},{1... | collective-permute-start | bytes 393224 | tf_op jit(solution)/shard_map/ppermute | solution.py:440
  13.2 7.8 %collective-permute-start.4 = (f32[256,128]{1,0:T(8,128)S(1)}, f32[256,128]{1,0:T(8,128)S(1)}, u32[]{:S(2)}, u32[]{:S(2)}) collective-permute-start(f32[256,128]{1,0:T(8,128)S(1)} %merge.40.token_ref), channel_id=1, source_target_pairs={{0,4},{4,0},{8,12},{12,8},{1,5},{5,1},{9,13},{13,9},{2,6},{6,2},{1... | collective-permute-start | bytes 393224 | tf_op jit(solution)/shard_map/ppermute | solution.py:440
  18.7 8.6 %collective-permute-start.8 = (f32[256,128]{1,0:T(8,128)S(1)}, f32[256,128]{1,0:T(8,128)S(1)}, u32[]{:S(2)}, u32[]{:S(2)}) collective-permute-start(f32[256,128]{1,0:T(8,128)S(1)} %get-tuple-element.161.token_ref), channel_id=1, source_target_pairs={{0,4},{4,0},{8,12},{12,8},{1,5},{5,1},{9,13},{13,9},{2,6},{6,2},{1... | collective-permute-start | bytes 393224 | tf_op jit(solution)/shard_map/ppermute | solution.py:440
  21.2 9.0 %collective-permute-start.10 = (f32[256,128]{1,0:T(8,128)S(1)}, f32[256,128]{1,0:T(8,128)S(1)}, u32[]{:S(2)}, u32[]{:S(2)}) collective-permute-start(f32[256,128]{1,0:T(8,128)S(1)} %get-tuple-element.162.token_ref), channel_id=1, source_target_pairs={{0,4},{4,0},{8,12},{12,8},{1,5},{5,1},{9,13},{13,9},{2,6},{6,2},{1... | collective-permute-start | bytes 393224 | tf_op jit(solution)/shard_map/ppermute | solution.py:440
  24.1 8.8 %collective-permute-start.12 = (f32[256,128]{1,0:T(8,128)S(1)}, f32[256,128]{1,0:T(8,128)S(1)}, u32[]{:S(2)}, u32[]{:S(2)}) collective-permute-start(f32[256,128]{1,0:T(8,128)S(1)} %get-tuple-element.163.token_ref), channel_id=1, source_target_pairs={{0,4},{4,0},{8,12},{12,8},{1,5},{5,1},{9,13},{13,9},{2,6},{6,2},{1... | collective-permute-start | bytes 393224 | tf_op jit(solution)/shard_map/ppermute | solution.py:440
  27.5 8.3 %collective-permute-start.14 = (f32[256,128]{1,0:T(8,128)S(1)}, f32[256,128]{1,0:T(8,128)S(1)}, u32[]{:S(2)}, u32[]{:S(2)}) collective-permute-start(f32[256,128]{1,0:T(8,128)S(1)} %get-tuple-element.164.token_ref), channel_id=1, source_target_pairs={{0,4},{4,0},{8,12},{12,8},{1,5},{5,1},{9,13},{13,9},{2,6},{6,2},{1... | collective-permute-start | bytes 393224 | tf_op jit(solution)/shard_map/ppermute | solution.py:440
  30.3 8.3 %collective-permute-start.16 = (f32[256,128]{1,0:T(8,128)S(1)}, f32[256,128]{1,0:T(8,128)S(1)}, u32[]{:S(2)}, u32[]{:S(2)}) collective-permute-start(f32[256,128]{1,0:T(8,128)S(1)} %get-tuple-element.165.token_ref), channel_id=1, source_target_pairs={{0,4},{4,0},{8,12},{12,8},{1,5},{5,1},{9,13},{13,9},{2,6},{6,2},{1... | collective-permute-start | bytes 393224 | tf_op jit(solution)/shard_map/ppermute | solution.py:440
  33.1 8.3 %collective-permute-start.18 = (f32[256,128]{1,0:T(8,128)S(1)}, f32[256,128]{1,0:T(8,128)S(1)}, u32[]{:S(2)}, u32[]{:S(2)}) collective-permute-start(f32[256,128]{1,0:T(8,128)S(1)} %get-tuple-element.166.token_ref), channel_id=1, source_target_pairs={{0,4},{4,0},{8,12},{12,8},{1,5},{5,1},{9,13},{13,9},{2,6},{6,2},{1... | collective-permute-start | bytes 393224 | tf_op jit(solution)/shard_map/ppermute | solution.py:440
  35.9 8.3 %collective-permute-start.20 = (f32[256,128]{1,0:T(8,128)S(1)}, f32[256,128]{1,0:T(8,128)S(1)}, u32[]{:S(2)}, u32[]{:S(2)}) collective-permute-start(f32[256,128]{1,0:T(8,128)S(1)} %get-tuple-element.167.token_ref), channel_id=1, source_target_pairs={{0,4},{4,0},{8,12},{12,8},{1,5},{5,1},{9,13},{13,9},{2,6},{6,2},{1... | collective-permute-start | bytes 393224 | tf_op jit(solution)/shard_map/ppermute | solution.py:440
  38.7 8.3 %collective-permute-start.22 = (f32[256,128]{1,0:T(8,128)S(1)}, f32[256,128]{1,0:T(8,128)S(1)}, u32[]{:S(2)}, u32[]{:S(2)}) collective-permute-start(f32[256,128]{1,0:T(8,128)S(1)} %get-tuple-element.168.token_ref), channel_id=1, source_target_pairs={{0,4},{4,0},{8,12},{12,8},{1,5},{5,1},{9,13},{13,9},{2,6},{6,2},{1... | collective-permute-start | bytes 393224 | tf_op jit(solution)/shard_map/ppermute | solution.py:440
  41.5 8.3 %collective-permute-start.24 = (f32[256,128]{1,0:T(8,128)S(1)}, f32[256,128]{1,0:T(8,128)S(1)}, u32[]{:S(2)}, u32[]{:S(2)}) collective-permute-start(f32[256,128]{1,0:T(8,128)S(1)} %get-tuple-element.169.token_ref), channel_id=1, source_target_pairs={{0,4},{4,0},{8,12},{12,8},{1,5},{5,1},{9,13},{13,9},{2,6},{6,2},{1... | collective-permute-start | bytes 393224 | tf_op jit(solution)/shard_map/ppermute | solution.py:440
  44.3 8.3 %collective-permute-start.26 = (f32[256,128]{1,0:T(8,128)S(1)}, f32[256,128]{1,0:T(8,128)S(1)}, u32[]{:S(2)}, u32[]{:S(2)}) collective-permute-start(f32[256,128]{1,0:T(8,128)S(1)} %get-tuple-element.170.token_ref), channel_id=1, source_target_pairs={{0,4},{4,0},{8,12},{12,8},{1,5},{5,1},{9,13},{13,9},{2,6},{6,2},{1... | collective-permute-start | bytes 393224 | tf_op jit(solution)/shard_map/ppermute | solution.py:440
  47.1 8.3 %collective-permute-start.28 = (f32[256,128]{1,0:T(8,128)S(1)}, f32[256,128]{1,0:T(8,128)S(1)}, u32[]{:S(2)}, u32[]{:S(2)}) collective-permute-start(f32[256,128]{1,0:T(8,128)S(1)} %get-tuple-element.171.token_ref), channel_id=1, source_target_pairs={{0,4},{4,0},{8,12},{12,8},{1,5},{5,1},{9,13},{13,9},{2,6},{6,2},{1... | collective-permute-start | bytes 393224 | tf_op jit(solution)/shard_map/ppermute | solution.py:440
  50.0 8.3 %collective-permute-start.30 = (f32[256,128]{1,0:T(8,128)S(1)}, f32[256,128]{1,0:T(8,128)S(1)}, u32[]{:S(2)}, u32[]{:S(2)}) collective-permute-start(f32[256,128]{1,0:T(8,128)S(1)} %get-tuple-element.174.token_ref), channel_id=1, source_target_pairs={{0,4},{4,0},{8,12},{12,8},{1,5},{5,1},{9,13},{13,9},{2,6},{6,2},{1... | collective-permute-start | bytes 393224 | tf_op jit(solution)/shard_map/ppermute | solution.py:440
  52.8 8.3 %collective-permute-start.32 = (f32[256,128]{1,0:T(8,128)S(1)}, f32[256,128]{1,0:T(8,128)S(1)}, u32[]{:S(2)}, u32[]{:S(2)}) collective-permute-start(f32[256,128]{1,0:T(8,128)S(1)} %get-tuple-element.177.token_ref), channel_id=1, source_target_pairs={{0,4},{4,0},{8,12},{12,8},{1,5},{5,1},{9,13},{13,9},{2,6},{6,2},{1... | collective-permute-start | bytes 393224 | tf_op jit(solution)/shard_map/ppermute | solution.py:440
  55.8 8.1 %collective-permute-start.34 = (f32[256,128]{1,0:T(8,128)S(1)}, f32[256,128]{1,0:T(8,128)S(1)}, u32[]{:S(2)}, u32[]{:S(2)}) collective-permute-start(f32[256,128]{1,0:T(8,128)S(1)} %get-tuple-element.180.token_ref), channel_id=1, source_target_pairs={{0,4},{4,0},{8,12},{12,8},{1,5},{5,1},{9,13},{13,9},{2,6},{6,2},{1... | collective-permute-start | bytes 393224 | tf_op jit(solution)/shard_map/ppermute | solution.py:440
  58.4 8.3 %collective-permute-start.36 = (f32[256,128]{1,0:T(8,128)S(1)}, f32[256,128]{1,0:T(8,128)S(1)}, u32[]{:S(2)}, u32[]{:S(2)}) collective-permute-start(f32[256,128]{1,0:T(8,128)S(1)} %get-tuple-element.183.token_ref), channel_id=1, source_target_pairs={{0,4},{4,0},{8,12},{12,8},{1,5},{5,1},{9,13},{13,9},{2,6},{6,2},{1... | collective-permute-start | bytes 393224 | tf_op jit(solution)/shard_map/ppermute | solution.py:440
  61.2 8.3 %collective-permute-start.38 = (f32[256,128]{1,0:T(8,128)S(1)}, f32[256,128]{1,0:T(8,128)S(1)}, u32[]{:S(2)}, u32[]{:S(2)}) collective-permute-start(f32[256,128]{1,0:T(8,128)S(1)} %get-tuple-element.186.token_ref), channel_id=1, source_target_pairs={{0,4},{4,0},{8,12},{12,8},{1,5},{5,1},{9,13},{13,9},{2,6},{6,2},{1... | collective-permute-start | bytes 393224 | tf_op jit(solution)/shard_map/ppermute | solution.py:440
  64.0 8.3 %collective-permute-start.40 = (f32[256,128]{1,0:T(8,128)S(1)}, f32[256,128]{1,0:T(8,128)S(1)}, u32[]{:S(2)}, u32[]{:S(2)}) collective-permute-start(f32[256,128]{1,0:T(8,128)S(1)} %get-tuple-element.189.token_ref), channel_id=1, source_target_pairs={{0,4},{4,0},{8,12},{12,8},{1,5},{5,1},{9,13},{13,9},{2,6},{6,2},{1... | collective-permute-start | bytes 393224 | tf_op jit(solution)/shard_map/ppermute | solution.py:440
  66.8 8.3 %collective-permute-start.42 = (f32[256,128]{1,0:T(8,128)S(1)}, f32[256,128]{1,0:T(8,128)S(1)}, u32[]{:S(2)}, u32[]{:S(2)}) collective-permute-start(f32[256,128]{1,0:T(8,128)S(1)} %get-tuple-element.192.token_ref), channel_id=1, source_target_pairs={{0,4},{4,0},{8,12},{12,8},{1,5},{5,1},{9,13},{13,9},{2,6},{6,2},{1... | collective-permute-start | bytes 393224 | tf_op jit(solution)/shard_map/ppermute | solution.py:440
  69.6 8.3 %collective-permute-start.44 = (f32[256,128]{1,0:T(8,128)S(1)}, f32[256,128]{1,0:T(8,128)S(1)}, u32[]{:S(2)}, u32[]{:S(2)}) collective-permute-start(f32[256,128]{1,0:T(8,128)S(1)} %get-tuple-element.195.token_ref), channel_id=1, source_target_pairs={{0,4},{4,0},{8,12},{12,8},{1,5},{5,1},{9,13},{13,9},{2,6},{6,2},{1... | collective-permute-start | bytes 393224 | tf_op jit(solution)/shard_map/ppermute | solution.py:440
  72.5 8.3 %collective-permute-start.46 = (f32[256,128]{1,0:T(8,128)S(1)}, f32[256,128]{1,0:T(8,128)S(1)}, u32[]{:S(2)}, u32[]{:S(2)}) collective-permute-start(f32[256,128]{1,0:T(8,128)S(1)} %get-tuple-element.198.token_ref), channel_id=1, source_target_pairs={{0,4},{4,0},{8,12},{12,8},{1,5},{5,1},{9,13},{13,9},{2,6},{6,2},{1... | collective-permute-start | bytes 393224 | tf_op jit(solution)/shard_map/ppermute | solution.py:440
  75.3 8.3 %collective-permute-start.48 = (f32[256,128]{1,0:T(8,128)S(1)}, f32[256,128]{1,0:T(8,128)S(1)}, u32[]{:S(2)}, u32[]{:S(2)}) collective-permute-start(f32[256,128]{1,0:T(8,128)S(1)} %get-tuple-element.201.token_ref), channel_id=1, source_target_pairs={{0,4},{4,0},{8,12},{12,8},{1,5},{5,1},{9,13},{13,9},{2,6},{6,2},{1... | collective-permute-start | bytes 393224 | tf_op jit(solution)/shard_map/ppermute | solution.py:440
  78.1 8.3 %collective-permute-start.50 = (f32[256,128]{1,0:T(8,128)S(1)}, f32[256,128]{1,0:T(8,128)S(1)}, u32[]{:S(2)}, u32[]{:S(2)}) collective-permute-start(f32[256,128]{1,0:T(8,128)S(1)} %get-tuple-element.204.token_ref), channel_id=1, source_target_pairs={{0,4},{4,0},{8,12},{12,8},{1,5},{5,1},{9,13},{13,9},{2,6},{6,2},{1... | collective-permute-start | bytes 393224 | tf_op jit(solution)/shard_map/ppermute | solution.py:440
  80.9 8.3 %collective-permute-start.52 = (f32[256,128]{1,0:T(8,128)S(1)}, f32[256,128]{1,0:T(8,128)S(1)}, u32[]{:S(2)}, u32[]{:S(2)}) collective-permute-start(f32[256,128]{1,0:T(8,128)S(1)} %get-tuple-element.207.token_ref), channel_id=1, source_target_pairs={{0,4},{4,0},{8,12},{12,8},{1,5},{5,1},{9,13},{13,9},{2,6},{6,2},{1... | collective-permute-start | bytes 393224 | tf_op jit(solution)/shard_map/ppermute | solution.py:440
  83.7 8.3 %collective-permute-start.54 = (f32[256,128]{1,0:T(8,128)S(1)}, f32[256,128]{1,0:T(8,128)S(1)}, u32[]{:S(2)}, u32[]{:S(2)}) collective-permute-start(f32[256,128]{1,0:T(8,128)S(1)} %get-tuple-element.210.token_ref), channel_id=1, source_target_pairs={{0,4},{4,0},{8,12},{12,8},{1,5},{5,1},{9,13},{13,9},{2,6},{6,2},{1... | collective-permute-start | bytes 393224 | tf_op jit(solution)/shard_map/ppermute | solution.py:440
  86.5 8.7 %collective-permute-start.56 = (f32[256,128]{1,0:T(8,128)S(1)}, f32[256,128]{1,0:T(8,128)S(1)}, u32[]{:S(2)}, u32[]{:S(2)}) collective-permute-start(f32[256,128]{1,0:T(8,128)S(1)} %get-tuple-element.213.token_ref), channel_id=1, source_target_pairs={{0,4},{4,0},{8,12},{12,8},{1,5},{5,1},{9,13},{13,9},{2,6},{6,2},{1... | collective-permute-start | bytes 393224 | tf_op jit(solution)/shard_map/ppermute | solution.py:440
  89.3 8.9 %collective-permute-start.58 = (f32[256,128]{1,0:T(8,128)S(1)}, f32[256,128]{1,0:T(8,128)S(1)}, u32[]{:S(2)}, u32[]{:S(2)}) collective-permute-start(f32[256,128]{1,0:T(8,128)S(1)} %get-tuple-element.216.token_ref), channel_id=1, source_target_pairs={{0,4},{4,0},{8,12},{12,8},{1,5},{5,1},{9,13},{13,9},{2,6},{6,2},{1... | collective-permute-start | bytes 393224 | tf_op jit(solution)/shard_map/ppermute | solution.py:440
  92.1 9.2 %collective-permute-start.60 = (f32[256,128]{1,0:T(8,128)S(1)}, f32[256,128]{1,0:T(8,128)S(1)}, u32[]{:S(2)}, u32[]{:S(2)}) collective-permute-start(f32[256,128]{1,0:T(8,128)S(1)} %get-tuple-element.219.token_ref), channel_id=1, source_target_pairs={{0,4},{4,0},{8,12},{12,8},{1,5},{5,1},{9,13},{13,9},{2,6},{6,2},{1... | collective-permute-start | bytes 393224 | tf_op jit(solution)/shard_map/ppermute | solution.py:440
  115.2 8.4 %collective-permute-start.70 = (f32[512,128]{1,0:T(8,128)S(1)}, f32[512,128]{1,0:T(8,128)S(1)}, u32[]{:S(2)}, u32[]{:S(2)}) collective-permute-start(f32[512,128]{1,0:T(8,128)S(1)} %add.3.token_ref.part_ref), channel_id=1, source_target_pairs={{0,2},{2,0},{1,3},{3,1},{4,6},{6,4},{5,7},{7,5},{8,10},{10,8},{9,1... | collective-permute-start | bytes 786440 | tf_op jit(solution)/shard_map/ppermute | solution.py:477
  (45 other events, 260.7 us)

commit v7 on v6

--- a/solution.py
+++ b/solution.py
@@ -21,6 +21,7 @@
 OUTER_LAG = 3
 INNER_LAG = 2
 BATCH = 3
+PIECES = 2
 
 
 def adam_move(values, gradient, first_moment, square, counter):
@@ -172,49 +173,53 @@
         store.wait()
 
 
-def half_share(start, at, width, pair_ref, new, mat_ref, grad_ref, out_ref):
+def half_share(start, at, width, pair_ref, new, mat_ref, grad_ref, out_refs):
     high, low = split(new)
     twice = jnp.concatenate([high, high], axis=1)
     pair = jnp.concatenate([high, low], axis=1)
-    rank, half = new.shape[1], out_ref.shape[0]
+    rank, piece = new.shape[1], out_refs[0].shape[0]
+    half = piece * len(out_refs)
     rows = pl.ds(pl.multiple_of(start * half, half), half)
     slopes = slopes_of(pair_ref[rows, :], twice, mat_ref[rows, pl.ds(at, width)])
     term = jnp.dot(slopes, pair, preferred_element_type=F32)
-    out_ref[...] = grad_ref[rows, :] + term[:, :rank] + term[:, rank:]
+    total = grad_ref[rows, :] + term[:, :rank] + term[:, rank:]
+    for index, out_ref in enumerate(out_refs):
+        out_ref[...] = total[index * piece : (index + 1) * piece]
 
 
 def send_kernel(
     at, rows_total, token_ref, outer_ref, high_ref, pair_ref, mat_ref, far_ref, near_ref, col_ref, mean_ref,
-    square_ref, grad_ref, new_ref, out_ref,
+    square_ref, grad_ref, new_ref, *out_refs,
 ):
     del token_ref
     gradient = pick(outer_ref, far_ref, near_ref) / rows_total
     new, _, _ = adam_move(col_ref[...], gradient, mean_ref[...], square_ref[...], START + 2)
     new_ref[...] = new
-    half_share(1 - high_ref[0], at, new.shape[0], pair_ref, new, mat_ref, grad_ref, out_ref)
-
-
-def keep_kernel(at, token_ref, high_ref, pair_ref, mat_ref, new_ref, grad_ref, out_ref):
-    del token_ref
-    half_share(high_ref[0], at, new_ref.shape[0], pair_ref, new_ref[...], mat_ref, grad_ref, out_ref)
-
-
-def row_kernel(cols_total, token_ref, high_ref, part_ref, other_ref, row_ref, mean_ref, square_ref, new_ref):
-    del token_ref
-    half = part_ref.shape[0]
-    own = pl.ds(pl.multiple_of(high_ref[0] * half, half), half)
+    half_share(1 - high_ref[0], at, new.shape[0], pair_ref, new, mat_ref, grad_ref, out_refs)
+
+
+def keep_kernel(at, token_ref, high_ref, pair_ref, mat_ref, new_ref, grad_ref, *out_refs):
+    del token_ref
+    half_share(high_ref[0], at, new_ref.shape[0], pair_ref, new_ref[...], mat_ref, grad_ref, out_refs)
+
+
+def row_kernel(index, cols_total, token_ref, high_ref, part_ref, other_ref, row_ref, mean_ref, square_ref, new_ref):
+    del token_ref
+    piece, half = part_ref.shape[0], row_ref.shape[0] // 2
+    own = pl.ds(pl.multiple_of(high_ref[0] * half + index * piece, piece), piece)
     gradient = (part_ref[...] + other_ref[...]) / cols_total
     new_ref[...], _, _ = adam_move(row_ref[own, :], gradient, mean_ref[own, :], square_ref[own, :], START + 1)
 
 
-def join_kernel(high_ref, new_ref, other_ref, out_hbm, sems):
-    half = new_ref.shape[0]
-    own = pl.multiple_of(high_ref[0] * half, half)
-    far = pl.multiple_of((1 - high_ref[0]) * half, half)
-    stores = [
-        pltpu.make_async_copy(new_ref, out_hbm.at[pl.ds(own, half), :], sems.at[0]),
-        pltpu.make_async_copy(other_ref, out_hbm.at[pl.ds(far, half), :], sems.at[1]),
-    ]
+def join_kernel(high_ref, *refs):
+    *piece_refs, out_hbm, sems = refs
+    piece, stores = piece_refs[0].shape[0], []
+    half = out_hbm.shape[0] // 2
+    for index, piece_ref in enumerate(piece_refs):
+        far, place = divmod(index, PIECES)
+        start = (high_ref[0] if far == 0 else 1 - high_ref[0]) * half + place * piece
+        target = out_hbm.at[pl.ds(pl.multiple_of(start, piece), piece), :]
+        stores.append(pltpu.make_async_copy(piece_ref, target, sems.at[index]))
     for store in stores:
         store.start()
     for store in stores:
@@ -335,18 +340,18 @@
     def halves(self, index, far, near, token):
         at = self.chunks[index][0]
         rows, rank = self.row.shape
-        half = (VMEM, (rows // 2, rank), F32)
+        pieces = [(VMEM, (rows // 2 // PIECES, rank), F32)] * PIECES
         ins = [(VMEM, array) for array in (far, near, *self.moved[index], self.grad)]
-        self.new[index], send = call(
+        self.new[index], *send = call(
             functools.partial(send_kernel, at, self.rows_total), "send",
             [(ANY, token), (SMEM, self.outer), (SMEM, self.high), (VMEM, self.pair), (VMEM, self.matrix), *ins],
-            [self.chunk(index), half],
-        )
-        (keep,) = call(
+            [self.chunk(index), *pieces],
+        )
+        keep = call(
             functools.partial(keep_kernel, at), "keep",
-            [(ANY, send), (SMEM, self.high)]
+            [(ANY, send[0]), (SMEM, self.high)]
             + [(VMEM, array) for array in (self.pair, self.matrix, self.new[index], self.grad)],
-            [half],
+            pieces,
         )
         self.ends = keep, send
 
@@ -469,23 +474,29 @@
 def row_step(work, row_mean, row_square, cols_total):
     high = work.high
     rows, rank = work.row.shape
-    half = (VMEM, (rows // 2, rank), F32)
+    small = (VMEM, (rows // 2 // PIECES, rank), F32)
     swap = [(0, 1), (1, 0), (2, 3), (3, 2)]
     across = [(0, 2), (2, 0), (1, 3), (3, 1)]
     keep, send = work.ends
-    part = keep + lax.ppermute(send, "col", swap)
-    other = lax.ppermute(part, "col", across)
-    new_cols, stored = work.new_cols(part)
-    ins = [(VMEM, array) for array in (part, other, work.row, row_mean, row_square)]
-    (new,) = call(
-        functools.partial(row_kernel, cols_total), "row", [(ANY, stored), (SMEM, high), *ins], [half]
-    )
-    other = lax.ppermute(new, "col", swap)
+    parts = [kept + lax.ppermute(sent, "col", swap) for kept, sent in zip(keep, send, strict=True)]
+    others = [lax.ppermute(part, "col", across) for part in parts]
+    new_cols, token = work.new_cols(parts[-1])
+    news = []
+    for index in range(PIECES):
+        arrays = (parts[index], others[index], work.row, row_mean, row_square)
+        (new,) = call(
+            functools.partial(row_kernel, index, cols_total), "row",
+            [(ANY, token), (SMEM, high)] + [(VMEM, array) for array in arrays],
+            [small],
+        )
+        news.append(new)
+        token = new
+    swapped = [lax.ppermute(new, "col", swap) for new in news]
     (out,) = call(
         join_kernel, "join",
-        [(SMEM, high), (VMEM, new), (VMEM, other)],
+        [(SMEM, high)] + [(VMEM, array) for array in (*news, *swapped)],
         [(HBM, work.row.shape, F32)],
-        scratch=[pltpu.SemaphoreType.DMA((2,))],
+        scratch=[pltpu.SemaphoreType.DMA((2 * PIECES,))],
     )
     return out, new_cols
 

time: 127 us -> 126 us (level)
  waiting for transfers between devices: 12.3 us -> 10.4 us
  starting transfers between devices: 71.9 us -> 73.5 us
    ppermute x3 -> x6, waiting for transfers between devices: 7.97 us -> 6.05 us  [the longest x2 4.67 us: row_step(): others = [lax.ppermute(part, 'col', across) for part in parts]]
    ppermute x3 -> x6, starting transfers between devices: 1.7 us -> 3.29 us  [the longest x2 2.16 us: row_step(): others = [lax.ppermute(part, 'col', across) for part in parts]]
    pallas_call x117 -> x118, Pallas kernels: 39.7 us -> 39.8 us  [call(): pl.pallas_call(kernel, out_shape=[jax.ShapeDtypeStruct(shape, kind) for _...]
  transfers between devices with their start and end apart: 72 -> 75, of which waited for: 6 -> 8; matrix products, arithmetic and copies ran while one was open for 0% -> 0% of each run, Pallas kernels for 28% -> 29%
where the time goes in v7:
time: 126 us
  starting transfers between devices  73.5 us (58%)
  Pallas kernels  39.8 us (32%)
  waiting for transfers between devices  10.4 us (8%)
  between operations  2.47 us (2%)
    ppermute x37, starting transfers between devices, line_columns(): from_outer[k] = lax.ppermute(payload, 'row', outer_pairs)  67.7 us
    pallas_call x118, Pallas kernels, call(): pl.pallas_call(kernel, out_shape=[jax.ShapeDtypeStruct(shape, kind) for _...  39.8 us
    ppermute x2, waiting for transfers between devices, row_step(): others = [lax.ppermute(part, 'col', across) for part in parts]  4.67 us
    ppermute x37, waiting for transfers between devices, line_columns(): from_outer[k] = lax.ppermute(payload, 'row', outer_pairs)  4.29 us
  transfers between devices with their start and end apart: 75, of which 8 were waited for; matrix products, arithmetic and copies ran while one was open for 0% of the time, Pallas kernels for 29%

profile of v7, /device:TPU:0, one launch (start us, length us, event | category | flops | bytes accessed | tf_op | source)
XLA Modules:
  0.0 126.2 jit_solution(3941245210575915322)
XLA Ops:
  0.6 2.3 %first.1 = (bf16[1024,256]{1,0:T(8,128)(2,1)S(1)}, bf16[1024,256]{1,0:T(8,128)(2,1)S(1)}, bf16[256,1024]{1,0:T(8,128)(2,1)S(1)}, f32[256,128]{1,0:T(8,128)S(1)}, f32[256,128]{1,0:T(8,128)S(1)}) custom-call(s32[1]{0:T(128)} %bitcast.1.outer_ref, s32[1]{0:T(128)} %bitcast.high_ref, f32[1024,128]{1,0:T(8,128)} %row_ref.3, f32[4096,128]{1,0:T(8,128)} %col_hbm.3, ...), custom_call_target="tpu_custom_call" | custom-call | flops 1 | bytes 1 | tf_op jit(solution)/shard_map/first/pallas_call | solution.py:236
  3.0 3.1 %collective-permute-start = (f32[256,128]{1,0:T(8,128)S(1)}, f32[256,128]{1,0:T(8,128)S(1)}, u32[]{:S(2)}, u32[]{:S(2)}) collective-permute-start(f32[256,128]{1,0:T(8,128)S(1)} %merge.39), channel_id=1, source_target_pairs={{0,4},{4,0},{8,12},{12,8},{1,5},{5,1},{9,13},{13,9},{2,6},{6,2},{1... | collective-permute-start | bytes 393224 | tf_op jit(solution)/shard_map/ppermute | solution.py:445
  6.2 4.1 %third.1 = (f32[4096,128]{1,0:T(8,128)S(1)}, bf16[1024,4096]{1,0:T(8,128)(2,1)S(1)}, f32[256,128]{1,0:T(8,128)S(1)}) custom-call(f32[256,128]{1,0:T(8,128)S(1)} %merge.37.token_ref, f32[4096,128]{1,0:T(8,128)} %col_hbm.3, bf16[1024,4096]{1,0:T(8,128)(2,1)} %mat_hbm.3, bf16[1024,256]{1,0:T(8,128)(2,1)S(1)} %get-tuple-element.158.twice_ref, ...), custom_call_target="tpu_custom_call" | custom-call | flops 1 | bytes 1 | tf_op jit(solution)/shard_map/third/pallas_call | solution.py:236
  10.3 2.1 %collective-permute-start.2 = (f32[256,128]{1,0:T(8,128)S(1)}, f32[256,128]{1,0:T(8,128)S(1)}, u32[]{:S(2)}, u32[]{:S(2)}) collective-permute-start(f32[256,128]{1,0:T(8,128)S(1)} %merge.38.token_ref), channel_id=1, source_target_pairs={{0,4},{4,0},{8,12},{12,8},{1,5},{5,1},{9,13},{13,9},{2,6},{6,2},{1... | collective-permute-start | bytes 393224 | tf_op jit(solution)/shard_map/ppermute | solution.py:445
  13.2 3.2 %collective-permute-start.4 = (f32[256,128]{1,0:T(8,128)S(1)}, f32[256,128]{1,0:T(8,128)S(1)}, u32[]{:S(2)}, u32[]{:S(2)}) collective-permute-start(f32[256,128]{1,0:T(8,128)S(1)} %merge.40.token_ref), channel_id=1, source_target_pairs={{0,4},{4,0},{8,12},{12,8},{1,5},{5,1},{9,13},{13,9},{2,6},{6,2},{1... | collective-permute-start | bytes 393224 | tf_op jit(solution)/shard_map/ppermute | solution.py:445
  21.2 2.1 %collective-permute-start.10 = (f32[256,128]{1,0:T(8,128)S(1)}, f32[256,128]{1,0:T(8,128)S(1)}, u32[]{:S(2)}, u32[]{:S(2)}) collective-permute-start(f32[256,128]{1,0:T(8,128)S(1)} %get-tuple-element.165.token_ref), channel_id=1, source_target_pairs={{0,4},{4,0},{8,12},{12,8},{1,5},{5,1},{9,13},{13,9},{2,6},{6,2},{1... | collective-permute-start | bytes 393224 | tf_op jit(solution)/shard_map/ppermute | solution.py:445
  24.1 2.5 %collective-permute-start.12 = (f32[256,128]{1,0:T(8,128)S(1)}, f32[256,128]{1,0:T(8,128)S(1)}, u32[]{:S(2)}, u32[]{:S(2)}) collective-permute-start(f32[256,128]{1,0:T(8,128)S(1)} %get-tuple-element.166.token_ref), channel_id=1, source_target_pairs={{0,4},{4,0},{8,12},{12,8},{1,5},{5,1},{9,13},{13,9},{2,6},{6,2},{1... | collective-permute-start | bytes 393224 | tf_op jit(solution)/shard_map/ppermute | solution.py:445
  27.5 1.9 %collective-permute-start.14 = (f32[256,128]{1,0:T(8,128)S(1)}, f32[256,128]{1,0:T(8,128)S(1)}, u32[]{:S(2)}, u32[]{:S(2)}) collective-permute-start(f32[256,128]{1,0:T(8,128)S(1)} %get-tuple-element.167.token_ref), channel_id=1, source_target_pairs={{0,4},{4,0},{8,12},{12,8},{1,5},{5,1},{9,13},{13,9},{2,6},{6,2},{1... | collective-permute-start | bytes 393224 | tf_op jit(solution)/shard_map/ppermute | solution.py:445
  30.3 1.9 %collective-permute-start.16 = (f32[256,128]{1,0:T(8,128)S(1)}, f32[256,128]{1,0:T(8,128)S(1)}, u32[]{:S(2)}, u32[]{:S(2)}) collective-permute-start(f32[256,128]{1,0:T(8,128)S(1)} %get-tuple-element.168.token_ref), channel_id=1, source_target_pairs={{0,4},{4,0},{8,12},{12,8},{1,5},{5,1},{9,13},{13,9},{2,6},{6,2},{1... | collective-permute-start | bytes 393224 | tf_op jit(solution)/shard_map/ppermute | solution.py:445
  33.1 1.9 %collective-permute-start.18 = (f32[256,128]{1,0:T(8,128)S(1)}, f32[256,128]{1,0:T(8,128)S(1)}, u32[]{:S(2)}, u32[]{:S(2)}) collective-permute-start(f32[256,128]{1,0:T(8,128)S(1)} %get-tuple-element.169.token_ref), channel_id=1, source_target_pairs={{0,4},{4,0},{8,12},{12,8},{1,5},{5,1},{9,13},{13,9},{2,6},{6,2},{1... | collective-permute-start | bytes 393224 | tf_op jit(solution)/shard_map/ppermute | solution.py:445
  35.9 1.9 %collective-permute-start.20 = (f32[256,128]{1,0:T(8,128)S(1)}, f32[256,128]{1,0:T(8,128)S(1)}, u32[]{:S(2)}, u32[]{:S(2)}) collective-permute-start(f32[256,128]{1,0:T(8,128)S(1)} %get-tuple-element.170.token_ref), channel_id=1, source_target_pairs={{0,4},{4,0},{8,12},{12,8},{1,5},{5,1},{9,13},{13,9},{2,6},{6,2},{1... | collective-permute-start | bytes 393224 | tf_op jit(solution)/shard_map/ppermute | solution.py:445
  38.7 1.9 %collective-permute-start.22 = (f32[256,128]{1,0:T(8,128)S(1)}, f32[256,128]{1,0:T(8,128)S(1)}, u32[]{:S(2)}, u32[]{:S(2)}) collective-permute-start(f32[256,128]{1,0:T(8,128)S(1)} %get-tuple-element.171.token_ref), channel_id=1, source_target_pairs={{0,4},{4,0},{8,12},{12,8},{1,5},{5,1},{9,13},{13,9},{2,6},{6,2},{1... | collective-permute-start | bytes 393224 | tf_op jit(solution)/shard_map/ppermute | solution.py:445
  41.5 1.9 %collective-permute-start.24 = (f32[256,128]{1,0:T(8,128)S(1)}, f32[256,128]{1,0:T(8,128)S(1)}, u32[]{:S(2)}, u32[]{:S(2)}) collective-permute-start(f32[256,128]{1,0:T(8,128)S(1)} %get-tuple-element.172.token_ref), channel_id=1, source_target_pairs={{0,4},{4,0},{8,12},{12,8},{1,5},{5,1},{9,13},{13,9},{2,6},{6,2},{1... | collective-permute-start | bytes 393224 | tf_op jit(solution)/shard_map/ppermute | solution.py:445
  44.3 1.9 %collective-permute-start.26 = (f32[256,128]{1,0:T(8,128)S(1)}, f32[256,128]{1,0:T(8,128)S(1)}, u32[]{:S(2)}, u32[]{:S(2)}) collective-permute-start(f32[256,128]{1,0:T(8,128)S(1)} %get-tuple-element.173.token_ref), channel_id=1, source_target_pairs={{0,4},{4,0},{8,12},{12,8},{1,5},{5,1},{9,13},{13,9},{2,6},{6,2},{1... | collective-permute-start | bytes 393224 | tf_op jit(solution)/shard_map/ppermute | solution.py:445
  47.1 1.9 %collective-permute-start.28 = (f32[256,128]{1,0:T(8,128)S(1)}, f32[256,128]{1,0:T(8,128)S(1)}, u32[]{:S(2)}, u32[]{:S(2)}) collective-permute-start(f32[256,128]{1,0:T(8,128)S(1)} %get-tuple-element.174.token_ref), channel_id=1, source_target_pairs={{0,4},{4,0},{8,12},{12,8},{1,5},{5,1},{9,13},{13,9},{2,6},{6,2},{1... | collective-permute-start | bytes 393224 | tf_op jit(solution)/shard_map/ppermute | solution.py:445
  52.8 1.9 %collective-permute-start.32 = (f32[256,128]{1,0:T(8,128)S(1)}, f32[256,128]{1,0:T(8,128)S(1)}, u32[]{:S(2)}, u32[]{:S(2)}) collective-permute-start(f32[256,128]{1,0:T(8,128)S(1)} %get-tuple-element.180.token_ref), channel_id=1, source_target_pairs={{0,4},{4,0},{8,12},{12,8},{1,5},{5,1},{9,13},{13,9},{2,6},{6,2},{1... | collective-permute-start | bytes 393224 | tf_op jit(solution)/shard_map/ppermute | solution.py:445
  58.4 1.9 %collective-permute-start.36 = (f32[256,128]{1,0:T(8,128)S(1)}, f32[256,128]{1,0:T(8,128)S(1)}, u32[]{:S(2)}, u32[]{:S(2)}) collective-permute-start(f32[256,128]{1,0:T(8,128)S(1)} %get-tuple-element.186.token_ref), channel_id=1, source_target_pairs={{0,4},{4,0},{8,12},{12,8},{1,5},{5,1},{9,13},{13,9},{2,6},{6,2},{1... | collective-permute-start | bytes 393224 | tf_op jit(solution)/shard_map/ppermute | solution.py:445
  61.2 1.9 %collective-permute-start.38 = (f32[256,128]{1,0:T(8,128)S(1)}, f32[256,128]{1,0:T(8,128)S(1)}, u32[]{:S(2)}, u32[]{:S(2)}) collective-permute-start(f32[256,128]{1,0:T(8,128)S(1)} %get-tuple-element.189.token_ref), channel_id=1, source_target_pairs={{0,4},{4,0},{8,12},{12,8},{1,5},{5,1},{9,13},{13,9},{2,6},{6,2},{1... | collective-permute-start | bytes 393224 | tf_op jit(solution)/shard_map/ppermute | solution.py:445
  64.0 1.9 %collective-permute-start.40 = (f32[256,128]{1,0:T(8,128)S(1)}, f32[256,128]{1,0:T(8,128)S(1)}, u32[]{:S(2)}, u32[]{:S(2)}) collective-permute-start(f32[256,128]{1,0:T(8,128)S(1)} %get-tuple-element.192.token_ref), channel_id=1, source_target_pairs={{0,4},{4,0},{8,12},{12,8},{1,5},{5,1},{9,13},{13,9},{2,6},{6,2},{1... | collective-permute-start | bytes 393224 | tf_op jit(solution)/shard_map/ppermute | solution.py:445
  66.8 1.9 %collective-permute-start.42 = (f32[256,128]{1,0:T(8,128)S(1)}, f32[256,128]{1,0:T(8,128)S(1)}, u32[]{:S(2)}, u32[]{:S(2)}) collective-permute-start(f32[256,128]{1,0:T(8,128)S(1)} %get-tuple-element.195.token_ref), channel_id=1, source_target_pairs={{0,4},{4,0},{8,12},{12,8},{1,5},{5,1},{9,13},{13,9},{2,6},{6,2},{1... | collective-permute-start | bytes 393224 | tf_op jit(solution)/shard_map/ppermute | solution.py:445
  69.6 1.9 %collective-permute-start.44 = (f32[256,128]{1,0:T(8,128)S(1)}, f32[256,128]{1,0:T(8,128)S(1)}, u32[]{:S(2)}, u32[]{:S(2)}) collective-permute-start(f32[256,128]{1,0:T(8,128)S(1)} %get-tuple-element.198.token_ref), channel_id=1, source_target_pairs={{0,4},{4,0},{8,12},{12,8},{1,5},{5,1},{9,13},{13,9},{2,6},{6,2},{1... | collective-permute-start | bytes 393224 | tf_op jit(solution)/shard_map/ppermute | solution.py:445
  72.5 1.9 %collective-permute-start.46 = (f32[256,128]{1,0:T(8,128)S(1)}, f32[256,128]{1,0:T(8,128)S(1)}, u32[]{:S(2)}, u32[]{:S(2)}) collective-permute-start(f32[256,128]{1,0:T(8,128)S(1)} %get-tuple-element.201.token_ref), channel_id=1, source_target_pairs={{0,4},{4,0},{8,12},{12,8},{1,5},{5,1},{9,13},{13,9},{2,6},{6,2},{1... | collective-permute-start | bytes 393224 | tf_op jit(solution)/shard_map/ppermute | solution.py:445
  75.3 1.9 %collective-permute-start.48 = (f32[256,128]{1,0:T(8,128)S(1)}, f32[256,128]{1,0:T(8,128)S(1)}, u32[]{:S(2)}, u32[]{:S(2)}) collective-permute-start(f32[256,128]{1,0:T(8,128)S(1)} %get-tuple-element.204.token_ref), channel_id=1, source_target_pairs={{0,4},{4,0},{8,12},{12,8},{1,5},{5,1},{9,13},{13,9},{2,6},{6,2},{1... | collective-permute-start | bytes 393224 | tf_op jit(solution)/shard_map/ppermute | solution.py:445
  78.1 1.9 %collective-permute-start.50 = (f32[256,128]{1,0:T(8,128)S(1)}, f32[256,128]{1,0:T(8,128)S(1)}, u32[]{:S(2)}, u32[]{:S(2)}) collective-permute-start(f32[256,128]{1,0:T(8,128)S(1)} %get-tuple-element.207.token_ref), channel_id=1, source_target_pairs={{0,4},{4,0},{8,12},{12,8},{1,5},{5,1},{9,13},{13,9},{2,6},{6,2},{1... | collective-permute-start | bytes 393224 | tf_op jit(solution)/shard_map/ppermute | solution.py:445
  80.9 1.9 %collective-permute-start.52 = (f32[256,128]{1,0:T(8,128)S(1)}, f32[256,128]{1,0:T(8,128)S(1)}, u32[]{:S(2)}, u32[]{:S(2)}) collective-permute-start(f32[256,128]{1,0:T(8,128)S(1)} %get-tuple-element.210.token_ref), channel_id=1, source_target_pairs={{0,4},{4,0},{8,12},{12,8},{1,5},{5,1},{9,13},{13,9},{2,6},{6,2},{1... | collective-permute-start | bytes 393224 | tf_op jit(solution)/shard_map/ppermute | solution.py:445
  83.7 1.9 %collective-permute-start.54 = (f32[256,128]{1,0:T(8,128)S(1)}, f32[256,128]{1,0:T(8,128)S(1)}, u32[]{:S(2)}, u32[]{:S(2)}) collective-permute-start(f32[256,128]{1,0:T(8,128)S(1)} %get-tuple-element.213.token_ref), channel_id=1, source_target_pairs={{0,4},{4,0},{8,12},{12,8},{1,5},{5,1},{9,13},{13,9},{2,6},{6,2},{1... | collective-permute-start | bytes 393224 | tf_op jit(solution)/shard_map/ppermute | solution.py:445
  86.5 1.9 %collective-permute-start.56 = (f32[256,128]{1,0:T(8,128)S(1)}, f32[256,128]{1,0:T(8,128)S(1)}, u32[]{:S(2)}, u32[]{:S(2)}) collective-permute-start(f32[256,128]{1,0:T(8,128)S(1)} %get-tuple-element.216.token_ref), channel_id=1, source_target_pairs={{0,4},{4,0},{8,12},{12,8},{1,5},{5,1},{9,13},{13,9},{2,6},{6,2},{1... | collective-permute-start | bytes 393224 | tf_op jit(solution)/shard_map/ppermute | solution.py:445
  89.3 1.9 %collective-permute-start.58 = (f32[256,128]{1,0:T(8,128)S(1)}, f32[256,128]{1,0:T(8,128)S(1)}, u32[]{:S(2)}, u32[]{:S(2)}) collective-permute-start(f32[256,128]{1,0:T(8,128)S(1)} %get-tuple-element.219.token_ref), channel_id=1, source_target_pairs={{0,4},{4,0},{8,12},{12,8},{1,5},{5,1},{9,13},{13,9},{2,6},{6,2},{1... | collective-permute-start | bytes 393224 | tf_op jit(solution)/shard_map/ppermute | solution.py:445
  92.1 1.9 %collective-permute-start.60 = (f32[256,128]{1,0:T(8,128)S(1)}, f32[256,128]{1,0:T(8,128)S(1)}, u32[]{:S(2)}, u32[]{:S(2)}) collective-permute-start(f32[256,128]{1,0:T(8,128)S(1)} %get-tuple-element.222.token_ref), channel_id=1, source_target_pairs={{0,4},{4,0},{8,12},{12,8},{1,5},{5,1},{9,13},{13,9},{2,6},{6,2},{1... | collective-permute-start | bytes 393224 | tf_op jit(solution)/shard_map/ppermute | solution.py:445
  108.5 2.2 %collective-permute-done.67.far_ref = f32[256,128]{1,0:T(8,128)S(1)} collective-permute-done((f32[256,128]{1,0:T(8,128)S(1)}, f32[256,128]{1,0:T(8,128)S(1)}, u32[]{:S(2)}, u32[]{:S(2)}) %collective-permute-start.67) | collective-permute-done | bytes 131104 | tf_op jit(solution)/shard_map/ppermute | solution.py:445
  118.7 2.8 %collective-permute-done.71.other_ref = f32[256,128]{1,0:T(8,128)S(1)} collective-permute-done((f32[256,128]{1,0:T(8,128)S(1)}, f32[256,128]{1,0:T(8,128)S(1)}, u32[]{:S(2)}, u32[]{:S(2)}) %collective-permute-start.71) | collective-permute-done | bytes 131104 | tf_op jit(solution)/shard_map/ppermute | solution.py:482
  121.6 1.9 %collective-permute-done.72.other_ref = f32[256,128]{1,0:T(8,128)S(1)} collective-permute-done((f32[256,128]{1,0:T(8,128)S(1)}, f32[256,128]{1,0:T(8,128)S(1)}, u32[]{:S(2)}, u32[]{:S(2)}) %collective-permute-start.72) | collective-permute-done | bytes 131104 | tf_op jit(solution)/shard_map/ppermute | solution.py:482
  (248 shorter events, 55.7 us)
Async XLA Ops:
  3.0 10.1 %collective-permute-start = (f32[256,128]{1,0:T(8,128)S(1)}, f32[256,128]{1,0:T(8,128)S(1)}, u32[]{:S(2)}, u32[]{:S(2)}) collective-permute-start(f32[256,128]{1,0:T(8,128)S(1)} %merge.39), channel_id=1, source_target_pairs={{0,4},{4,0},{8,12},{12,8},{1,5},{5,1},{9,13},{13,9},{2,6},{6,2},{1... | collective-permute-start | bytes 393224 | tf_op jit(solution)/shard_map/ppermute | solution.py:445
  6.1 11.0 %collective-permute-start.1 = (f32[256,128]{1,0:T(8,128)S(1)}, f32[256,128]{1,0:T(8,128)S(1)}, u32[]{:S(2)}, u32[]{:S(2)}) collective-permute-start(f32[256,128]{1,0:T(8,128)S(1)} %merge.37.token_ref), channel_id=1, source_target_pairs={{0,4},{4,0},{8,12},{12,8},{1,5},{5,1},{9,13},{13,9},{2,6},{6,2},{1... | collective-permute-start | bytes 393224 | tf_op jit(solution)/shard_map/ppermute | solution.py:445
  10.3 8.2 %collective-permute-start.2 = (f32[256,128]{1,0:T(8,128)S(1)}, f32[256,128]{1,0:T(8,128)S(1)}, u32[]{:S(2)}, u32[]{:S(2)}) collective-permute-start(f32[256,128]{1,0:T(8,128)S(1)} %merge.38.token_ref), channel_id=1, source_target_pairs={{0,4},{4,0},{8,12},{12,8},{1,5},{5,1},{9,13},{13,9},{2,6},{6,2},{1... | collective-permute-start | bytes 393224 | tf_op jit(solution)/shard_map/ppermute | solution.py:445
  13.2 7.8 %collective-permute-start.4 = (f32[256,128]{1,0:T(8,128)S(1)}, f32[256,128]{1,0:T(8,128)S(1)}, u32[]{:S(2)}, u32[]{:S(2)}) collective-permute-start(f32[256,128]{1,0:T(8,128)S(1)} %merge.40.token_ref), channel_id=1, source_target_pairs={{0,4},{4,0},{8,12},{12,8},{1,5},{5,1},{9,13},{13,9},{2,6},{6,2},{1... | collective-permute-start | bytes 393224 | tf_op jit(solution)/shard_map/ppermute | solution.py:445
  18.7 8.6 %collective-permute-start.8 = (f32[256,128]{1,0:T(8,128)S(1)}, f32[256,128]{1,0:T(8,128)S(1)}, u32[]{:S(2)}, u32[]{:S(2)}) collective-permute-start(f32[256,128]{1,0:T(8,128)S(1)} %get-tuple-element.164.token_ref), channel_id=1, source_target_pairs={{0,4},{4,0},{8,12},{12,8},{1,5},{5,1},{9,13},{13,9},{2,6},{6,2},{1... | collective-permute-start | bytes 393224 | tf_op jit(solution)/shard_map/ppermute | solution.py:445
  21.2 9.0 %collective-permute-start.10 = (f32[256,128]{1,0:T(8,128)S(1)}, f32[256,128]{1,0:T(8,128)S(1)}, u32[]{:S(2)}, u32[]{:S(2)}) collective-permute-start(f32[256,128]{1,0:T(8,128)S(1)} %get-tuple-element.165.token_ref), channel_id=1, source_target_pairs={{0,4},{4,0},{8,12},{12,8},{1,5},{5,1},{9,13},{13,9},{2,6},{6,2},{1... | collective-permute-start | bytes 393224 | tf_op jit(solution)/shard_map/ppermute | solution.py:445
  24.1 8.8 %collective-permute-start.12 = (f32[256,128]{1,0:T(8,128)S(1)}, f32[256,128]{1,0:T(8,128)S(1)}, u32[]{:S(2)}, u32[]{:S(2)}) collective-permute-start(f32[256,128]{1,0:T(8,128)S(1)} %get-tuple-element.166.token_ref), channel_id=1, source_target_pairs={{0,4},{4,0},{8,12},{12,8},{1,5},{5,1},{9,13},{13,9},{2,6},{6,2},{1... | collective-permute-start | bytes 393224 | tf_op jit(solution)/shard_map/ppermute | solution.py:445
  27.5 8.3 %collective-permute-start.14 = (f32[256,128]{1,0:T(8,128)S(1)}, f32[256,128]{1,0:T(8,128)S(1)}, u32[]{:S(2)}, u32[]{:S(2)}) collective-permute-start(f32[256,128]{1,0:T(8,128)S(1)} %get-tuple-element.167.token_ref), channel_id=1, source_target_pairs={{0,4},{4,0},{8,12},{12,8},{1,5},{5,1},{9,13},{13,9},{2,6},{6,2},{1... | collective-permute-start | bytes 393224 | tf_op jit(solution)/shard_map/ppermute | solution.py:445
  30.3 8.3 %collective-permute-start.16 = (f32[256,128]{1,0:T(8,128)S(1)}, f32[256,128]{1,0:T(8,128)S(1)}, u32[]{:S(2)}, u32[]{:S(2)}) collective-permute-start(f32[256,128]{1,0:T(8,128)S(1)} %get-tuple-element.168.token_ref), channel_id=1, source_target_pairs={{0,4},{4,0},{8,12},{12,8},{1,5},{5,1},{9,13},{13,9},{2,6},{6,2},{1... | collective-permute-start | bytes 393224 | tf_op jit(solution)/shard_map/ppermute | solution.py:445
  33.1 8.3 %collective-permute-start.18 = (f32[256,128]{1,0:T(8,128)S(1)}, f32[256,128]{1,0:T(8,128)S(1)}, u32[]{:S(2)}, u32[]{:S(2)}) collective-permute-start(f32[256,128]{1,0:T(8,128)S(1)} %get-tuple-element.169.token_ref), channel_id=1, source_target_pairs={{0,4},{4,0},{8,12},{12,8},{1,5},{5,1},{9,13},{13,9},{2,6},{6,2},{1... | collective-permute-start | bytes 393224 | tf_op jit(solution)/shard_map/ppermute | solution.py:445
  35.9 8.3 %collective-permute-start.20 = (f32[256,128]{1,0:T(8,128)S(1)}, f32[256,128]{1,0:T(8,128)S(1)}, u32[]{:S(2)}, u32[]{:S(2)}) collective-permute-start(f32[256,128]{1,0:T(8,128)S(1)} %get-tuple-element.170.token_ref), channel_id=1, source_target_pairs={{0,4},{4,0},{8,12},{12,8},{1,5},{5,1},{9,13},{13,9},{2,6},{6,2},{1... | collective-permute-start | bytes 393224 | tf_op jit(solution)/shard_map/ppermute | solution.py:445
  38.7 8.3 %collective-permute-start.22 = (f32[256,128]{1,0:T(8,128)S(1)}, f32[256,128]{1,0:T(8,128)S(1)}, u32[]{:S(2)}, u32[]{:S(2)}) collective-permute-start(f32[256,128]{1,0:T(8,128)S(1)} %get-tuple-element.171.token_ref), channel_id=1, source_target_pairs={{0,4},{4,0},{8,12},{12,8},{1,5},{5,1},{9,13},{13,9},{2,6},{6,2},{1... | collective-permute-start | bytes 393224 | tf_op jit(solution)/shard_map/ppermute | solution.py:445
  41.5 8.3 %collective-permute-start.24 = (f32[256,128]{1,0:T(8,128)S(1)}, f32[256,128]{1,0:T(8,128)S(1)}, u32[]{:S(2)}, u32[]{:S(2)}) collective-permute-start(f32[256,128]{1,0:T(8,128)S(1)} %get-tuple-element.172.token_ref), channel_id=1, source_target_pairs={{0,4},{4,0},{8,12},{12,8},{1,5},{5,1},{9,13},{13,9},{2,6},{6,2},{1... | collective-permute-start | bytes 393224 | tf_op jit(solution)/shard_map/ppermute | solution.py:445
  44.3 8.3 %collective-permute-start.26 = (f32[256,128]{1,0:T(8,128)S(1)}, f32[256,128]{1,0:T(8,128)S(1)}, u32[]{:S(2)}, u32[]{:S(2)}) collective-permute-start(f32[256,128]{1,0:T(8,128)S(1)} %get-tuple-element.173.token_ref), channel_id=1, source_target_pairs={{0,4},{4,0},{8,12},{12,8},{1,5},{5,1},{9,13},{13,9},{2,6},{6,2},{1... | collective-permute-start | bytes 393224 | tf_op jit(solution)/shard_map/ppermute | solution.py:445
  47.1 8.3 %collective-permute-start.28 = (f32[256,128]{1,0:T(8,128)S(1)}, f32[256,128]{1,0:T(8,128)S(1)}, u32[]{:S(2)}, u32[]{:S(2)}) collective-permute-start(f32[256,128]{1,0:T(8,128)S(1)} %get-tuple-element.174.token_ref), channel_id=1, source_target_pairs={{0,4},{4,0},{8,12},{12,8},{1,5},{5,1},{9,13},{13,9},{2,6},{6,2},{1... | collective-permute-start | bytes 393224 | tf_op jit(solution)/shard_map/ppermute | solution.py:445
  50.0 8.3 %collective-permute-start.30 = (f32[256,128]{1,0:T(8,128)S(1)}, f32[256,128]{1,0:T(8,128)S(1)}, u32[]{:S(2)}, u32[]{:S(2)}) collective-permute-start(f32[256,128]{1,0:T(8,128)S(1)} %get-tuple-element.177.token_ref), channel_id=1, source_target_pairs={{0,4},{4,0},{8,12},{12,8},{1,5},{5,1},{9,13},{13,9},{2,6},{6,2},{1... | collective-permute-start | bytes 393224 | tf_op jit(solution)/shard_map/ppermute | solution.py:445
  52.8 8.3 %collective-permute-start.32 = (f32[256,128]{1,0:T(8,128)S(1)}, f32[256,128]{1,0:T(8,128)S(1)}, u32[]{:S(2)}, u32[]{:S(2)}) collective-permute-start(f32[256,128]{1,0:T(8,128)S(1)} %get-tuple-element.180.token_ref), channel_id=1, source_target_pairs={{0,4},{4,0},{8,12},{12,8},{1,5},{5,1},{9,13},{13,9},{2,6},{6,2},{1... | collective-permute-start | bytes 393224 | tf_op jit(solution)/shard_map/ppermute | solution.py:445
  55.8 8.1 %collective-permute-start.34 = (f32[256,128]{1,0:T(8,128)S(1)}, f32[256,128]{1,0:T(8,128)S(1)}, u32[]{:S(2)}, u32[]{:S(2)}) collective-permute-start(f32[256,128]{1,0:T(8,128)S(1)} %get-tuple-element.183.token_ref), channel_id=1, source_target_pairs={{0,4},{4,0},{8,12},{12,8},{1,5},{5,1},{9,13},{13,9},{2,6},{6,2},{1... | collective-permute-start | bytes 393224 | tf_op jit(solution)/shard_map/ppermute | solution.py:445
  58.4 8.3 %collective-permute-start.36 = (f32[256,128]{1,0:T(8,128)S(1)}, f32[256,128]{1,0:T(8,128)S(1)}, u32[]{:S(2)}, u32[]{:S(2)}) collective-permute-start(f32[256,128]{1,0:T(8,128)S(1)} %get-tuple-element.186.token_ref), channel_id=1, source_target_pairs={{0,4},{4,0},{8,12},{12,8},{1,5},{5,1},{9,13},{13,9},{2,6},{6,2},{1... | collective-permute-start | bytes 393224 | tf_op jit(solution)/shard_map/ppermute | solution.py:445
  61.2 8.3 %collective-permute-start.38 = (f32[256,128]{1,0:T(8,128)S(1)}, f32[256,128]{1,0:T(8,128)S(1)}, u32[]{:S(2)}, u32[]{:S(2)}) collective-permute-start(f32[256,128]{1,0:T(8,128)S(1)} %get-tuple-element.189.token_ref), channel_id=1, source_target_pairs={{0,4},{4,0},{8,12},{12,8},{1,5},{5,1},{9,13},{13,9},{2,6},{6,2},{1... | collective-permute-start | bytes 393224 | tf_op jit(solution)/shard_map/ppermute | solution.py:445
  64.0 8.3 %collective-permute-start.40 = (f32[256,128]{1,0:T(8,128)S(1)}, f32[256,128]{1,0:T(8,128)S(1)}, u32[]{:S(2)}, u32[]{:S(2)}) collective-permute-start(f32[256,128]{1,0:T(8,128)S(1)} %get-tuple-element.192.token_ref), channel_id=1, source_target_pairs={{0,4},{4,0},{8,12},{12,8},{1,5},{5,1},{9,13},{13,9},{2,6},{6,2},{1... | collective-permute-start | bytes 393224 | tf_op jit(solution)/shard_map/ppermute | solution.py:445
  66.8 8.3 %collective-permute-start.42 = (f32[256,128]{1,0:T(8,128)S(1)}, f32[256,128]{1,0:T(8,128)S(1)}, u32[]{:S(2)}, u32[]{:S(2)}) collective-permute-start(f32[256,128]{1,0:T(8,128)S(1)} %get-tuple-element.195.token_ref), channel_id=1, source_target_pairs={{0,4},{4,0},{8,12},{12,8},{1,5},{5,1},{9,13},{13,9},{2,6},{6,2},{1... | collective-permute-start | bytes 393224 | tf_op jit(solution)/shard_map/ppermute | solution.py:445
  69.6 8.3 %collective-permute-start.44 = (f32[256,128]{1,0:T(8,128)S(1)}, f32[256,128]{1,0:T(8,128)S(1)}, u32[]{:S(2)}, u32[]{:S(2)}) collective-permute-start(f32[256,128]{1,0:T(8,128)S(1)} %get-tuple-element.198.token_ref), channel_id=1, source_target_pairs={{0,4},{4,0},{8,12},{12,8},{1,5},{5,1},{9,13},{13,9},{2,6},{6,2},{1... | collective-permute-start | bytes 393224 | tf_op jit(solution)/shard_map/ppermute | solution.py:445
  72.5 8.3 %collective-permute-start.46 = (f32[256,128]{1,0:T(8,128)S(1)}, f32[256,128]{1,0:T(8,128)S(1)}, u32[]{:S(2)}, u32[]{:S(2)}) collective-permute-start(f32[256,128]{1,0:T(8,128)S(1)} %get-tuple-element.201.token_ref), channel_id=1, source_target_pairs={{0,4},{4,0},{8,12},{12,8},{1,5},{5,1},{9,13},{13,9},{2,6},{6,2},{1... | collective-permute-start | bytes 393224 | tf_op jit(solution)/shard_map/ppermute | solution.py:445
  75.3 8.3 %collective-permute-start.48 = (f32[256,128]{1,0:T(8,128)S(1)}, f32[256,128]{1,0:T(8,128)S(1)}, u32[]{:S(2)}, u32[]{:S(2)}) collective-permute-start(f32[256,128]{1,0:T(8,128)S(1)} %get-tuple-element.204.token_ref), channel_id=1, source_target_pairs={{0,4},{4,0},{8,12},{12,8},{1,5},{5,1},{9,13},{13,9},{2,6},{6,2},{1... | collective-permute-start | bytes 393224 | tf_op jit(solution)/shard_map/ppermute | solution.py:445
  78.1 8.3 %collective-permute-start.50 = (f32[256,128]{1,0:T(8,128)S(1)}, f32[256,128]{1,0:T(8,128)S(1)}, u32[]{:S(2)}, u32[]{:S(2)}) collective-permute-start(f32[256,128]{1,0:T(8,128)S(1)} %get-tuple-element.207.token_ref), channel_id=1, source_target_pairs={{0,4},{4,0},{8,12},{12,8},{1,5},{5,1},{9,13},{13,9},{2,6},{6,2},{1... | collective-permute-start | bytes 393224 | tf_op jit(solution)/shard_map/ppermute | solution.py:445
  80.9 8.3 %collective-permute-start.52 = (f32[256,128]{1,0:T(8,128)S(1)}, f32[256,128]{1,0:T(8,128)S(1)}, u32[]{:S(2)}, u32[]{:S(2)}) collective-permute-start(f32[256,128]{1,0:T(8,128)S(1)} %get-tuple-element.210.token_ref), channel_id=1, source_target_pairs={{0,4},{4,0},{8,12},{12,8},{1,5},{5,1},{9,13},{13,9},{2,6},{6,2},{1... | collective-permute-start | bytes 393224 | tf_op jit(solution)/shard_map/ppermute | solution.py:445
  83.7 8.3 %collective-permute-start.54 = (f32[256,128]{1,0:T(8,128)S(1)}, f32[256,128]{1,0:T(8,128)S(1)}, u32[]{:S(2)}, u32[]{:S(2)}) collective-permute-start(f32[256,128]{1,0:T(8,128)S(1)} %get-tuple-element.213.token_ref), channel_id=1, source_target_pairs={{0,4},{4,0},{8,12},{12,8},{1,5},{5,1},{9,13},{13,9},{2,6},{6,2},{1... | collective-permute-start | bytes 393224 | tf_op jit(solution)/shard_map/ppermute | solution.py:445
  86.5 8.7 %collective-permute-start.56 = (f32[256,128]{1,0:T(8,128)S(1)}, f32[256,128]{1,0:T(8,128)S(1)}, u32[]{:S(2)}, u32[]{:S(2)}) collective-permute-start(f32[256,128]{1,0:T(8,128)S(1)} %get-tuple-element.216.token_ref), channel_id=1, source_target_pairs={{0,4},{4,0},{8,12},{12,8},{1,5},{5,1},{9,13},{13,9},{2,6},{6,2},{1... | collective-permute-start | bytes 393224 | tf_op jit(solution)/shard_map/ppermute | solution.py:445
  89.3 8.9 %collective-permute-start.58 = (f32[256,128]{1,0:T(8,128)S(1)}, f32[256,128]{1,0:T(8,128)S(1)}, u32[]{:S(2)}, u32[]{:S(2)}) collective-permute-start(f32[256,128]{1,0:T(8,128)S(1)} %get-tuple-element.219.token_ref), channel_id=1, source_target_pairs={{0,4},{4,0},{8,12},{12,8},{1,5},{5,1},{9,13},{13,9},{2,6},{6,2},{1... | collective-permute-start | bytes 393224 | tf_op jit(solution)/shard_map/ppermute | solution.py:445
  92.1 9.2 %collective-permute-start.60 = (f32[256,128]{1,0:T(8,128)S(1)}, f32[256,128]{1,0:T(8,128)S(1)}, u32[]{:S(2)}, u32[]{:S(2)}) collective-permute-start(f32[256,128]{1,0:T(8,128)S(1)} %get-tuple-element.222.token_ref), channel_id=1, source_target_pairs={{0,4},{4,0},{8,12},{12,8},{1,5},{5,1},{9,13},{13,9},{2,6},{6,2},{1... | collective-permute-start | bytes 393224 | tf_op jit(solution)/shard_map/ppermute | solution.py:445
  95.3 7.6 %collective-permute-start.62 = (f32[256,128]{1,0:T(8,128)S(1)}, f32[256,128]{1,0:T(8,128)S(1)}, u32[]{:S(2)}, u32[]{:S(2)}) collective-permute-start(f32[256,128]{1,0:T(8,128)S(1)} %merge.69.token_ref.near_ref), channel_id=1, source_target_pairs={{0,4},{4,0},{8,12},{12,8},{1,5},{5,1},{9,13},{13,9},{2,6},{6,2},{1... | collective-permute-start | bytes 393224 | tf_op jit(solution)/shard_map/ppermute | solution.py:445
  (48 other events, 262.3 us)

commit v8 on v7

--- a/solution.py
+++ b/solution.py
@@ -21,7 +21,7 @@
 OUTER_LAG = 3
 INNER_LAG = 2
 BATCH = 3
-PIECES = 2
+PIECES = 4
 
 
 def adam_move(values, gradient, first_moment, square, counter):

time: 126 us -> 127 us (level)
  starting transfers between devices: 73.5 us -> 76.6 us
  waiting for transfers between devices: 10.4 us -> 7.77 us
    ppermute x2 -> x4, waiting for transfers between devices: 4.67 us -> 2.48 us  [row_step(): others = [lax.ppermute(part, 'col', across) for part in parts]]
    ppermute x2 -> x4, starting transfers between devices: 2.16 us -> 4.31 us  [row_step(): others = [lax.ppermute(part, 'col', across) for part in parts]]
    pallas_call x118 -> x120, Pallas kernels: 39.8 us -> 39.8 us  [call(): pl.pallas_call(kernel, out_shape=[jax.ShapeDtypeStruct(shape, kind) for _...]
  transfers between devices with their start and end apart: 75 -> 81, of which waited for: 8 -> 9; matrix products, arithmetic and copies ran while one was open for 0% -> 0% of each run, Pallas kernels for 29% -> 28%
where the time goes in v8:
time: 127 us
  starting transfers between devices  76.6 us (60%)
  Pallas kernels  39.8 us (31%)
  waiting for transfers between devices  7.77 us (6%)
  between operations  2.55 us (2%)
    ppermute x37, starting transfers between devices, line_columns(): from_outer[k] = lax.ppermute(payload, 'row', outer_pairs)  67.7 us
    pallas_call x120, Pallas kernels, call(): pl.pallas_call(kernel, out_shape=[jax.ShapeDtypeStruct(shape, kind) for _...  39.8 us
    ppermute x4, starting transfers between devices, row_step(): others = [lax.ppermute(part, 'col', across) for part in parts]  4.31 us
    ppermute x37, waiting for transfers between devices, line_columns(): from_outer[k] = lax.ppermute(payload, 'row', outer_pairs)  4.29 us
  transfers between devices with their start and end apart: 81, of which 9 were waited for; matrix products, arithmetic and copies ran while one was open for 0% of the time, Pallas kernels for 28%

profile of v8, /device:TPU:0, one launch (start us, length us, event | category | flops | bytes accessed | tf_op | source)
XLA Modules:
  0.0 126.8 jit_solution(6406681167146469983)
XLA Ops:
  0.6 2.3 %first.1 = (bf16[1024,256]{1,0:T(8,128)(2,1)S(1)}, bf16[1024,256]{1,0:T(8,128)(2,1)S(1)}, bf16[256,1024]{1,0:T(8,128)(2,1)S(1)}, f32[256,128]{1,0:T(8,128)S(1)}, f32[256,128]{1,0:T(8,128)S(1)}) custom-call(s32[1]{0:T(128)} %bitcast.1.outer_ref, s32[1]{0:T(128)} %bitcast.high_ref, f32[1024,128]{1,0:T(8,128)} %row_ref.7, f32[4096,128]{1,0:T(8,128)} %col_hbm.3, ...), custom_call_target="tpu_custom_call" | custom-call | flops 1 | bytes 1 | tf_op jit(solution)/shard_map/first/pallas_call | solution.py:236
  3.0 3.1 %collective-permute-start = (f32[256,128]{1,0:T(8,128)S(1)}, f32[256,128]{1,0:T(8,128)S(1)}, u32[]{:S(2)}, u32[]{:S(2)}) collective-permute-start(f32[256,128]{1,0:T(8,128)S(1)} %merge.39), channel_id=1, source_target_pairs={{0,4},{4,0},{8,12},{12,8},{1,5},{5,1},{9,13},{13,9},{2,6},{6,2},{1... | collective-permute-start | bytes 393224 | tf_op jit(solution)/shard_map/ppermute | solution.py:445
  6.2 4.1 %third.1 = (f32[4096,128]{1,0:T(8,128)S(1)}, bf16[1024,4096]{1,0:T(8,128)(2,1)S(1)}, f32[256,128]{1,0:T(8,128)S(1)}) custom-call(f32[256,128]{1,0:T(8,128)S(1)} %merge.37.token_ref, f32[4096,128]{1,0:T(8,128)} %col_hbm.3, bf16[1024,4096]{1,0:T(8,128)(2,1)} %mat_hbm.3, bf16[1024,256]{1,0:T(8,128)(2,1)S(1)} %get-tuple-element.162.twice_ref, ...), custom_call_target="tpu_custom_call" | custom-call | flops 1 | bytes 1 | tf_op jit(solution)/shard_map/third/pallas_call | solution.py:236
  10.3 2.1 %collective-permute-start.2 = (f32[256,128]{1,0:T(8,128)S(1)}, f32[256,128]{1,0:T(8,128)S(1)}, u32[]{:S(2)}, u32[]{:S(2)}) collective-permute-start(f32[256,128]{1,0:T(8,128)S(1)} %merge.38.token_ref), channel_id=1, source_target_pairs={{0,4},{4,0},{8,12},{12,8},{1,5},{5,1},{9,13},{13,9},{2,6},{6,2},{1... | collective-permute-start | bytes 393224 | tf_op jit(solution)/shard_map/ppermute | solution.py:445
  13.2 3.2 %collective-permute-start.4 = (f32[256,128]{1,0:T(8,128)S(1)}, f32[256,128]{1,0:T(8,128)S(1)}, u32[]{:S(2)}, u32[]{:S(2)}) collective-permute-start(f32[256,128]{1,0:T(8,128)S(1)} %merge.40.token_ref), channel_id=1, source_target_pairs={{0,4},{4,0},{8,12},{12,8},{1,5},{5,1},{9,13},{13,9},{2,6},{6,2},{1... | collective-permute-start | bytes 393224 | tf_op jit(solution)/shard_map/ppermute | solution.py:445
  21.2 2.1 %collective-permute-start.10 = (f32[256,128]{1,0:T(8,128)S(1)}, f32[256,128]{1,0:T(8,128)S(1)}, u32[]{:S(2)}, u32[]{:S(2)}) collective-permute-start(f32[256,128]{1,0:T(8,128)S(1)} %get-tuple-element.169.token_ref), channel_id=1, source_target_pairs={{0,4},{4,0},{8,12},{12,8},{1,5},{5,1},{9,13},{13,9},{2,6},{6,2},{1... | collective-permute-start | bytes 393224 | tf_op jit(solution)/shard_map/ppermute | solution.py:445
  24.1 2.5 %collective-permute-start.12 = (f32[256,128]{1,0:T(8,128)S(1)}, f32[256,128]{1,0:T(8,128)S(1)}, u32[]{:S(2)}, u32[]{:S(2)}) collective-permute-start(f32[256,128]{1,0:T(8,128)S(1)} %get-tuple-element.170.token_ref), channel_id=1, source_target_pairs={{0,4},{4,0},{8,12},{12,8},{1,5},{5,1},{9,13},{13,9},{2,6},{6,2},{1... | collective-permute-start | bytes 393224 | tf_op jit(solution)/shard_map/ppermute | solution.py:445
  27.5 1.9 %collective-permute-start.14 = (f32[256,128]{1,0:T(8,128)S(1)}, f32[256,128]{1,0:T(8,128)S(1)}, u32[]{:S(2)}, u32[]{:S(2)}) collective-permute-start(f32[256,128]{1,0:T(8,128)S(1)} %get-tuple-element.171.token_ref), channel_id=1, source_target_pairs={{0,4},{4,0},{8,12},{12,8},{1,5},{5,1},{9,13},{13,9},{2,6},{6,2},{1... | collective-permute-start | bytes 393224 | tf_op jit(solution)/shard_map/ppermute | solution.py:445
  30.3 1.9 %collective-permute-start.16 = (f32[256,128]{1,0:T(8,128)S(1)}, f32[256,128]{1,0:T(8,128)S(1)}, u32[]{:S(2)}, u32[]{:S(2)}) collective-permute-start(f32[256,128]{1,0:T(8,128)S(1)} %get-tuple-element.172.token_ref), channel_id=1, source_target_pairs={{0,4},{4,0},{8,12},{12,8},{1,5},{5,1},{9,13},{13,9},{2,6},{6,2},{1... | collective-permute-start | bytes 393224 | tf_op jit(solution)/shard_map/ppermute | solution.py:445
  33.1 1.9 %collective-permute-start.18 = (f32[256,128]{1,0:T(8,128)S(1)}, f32[256,128]{1,0:T(8,128)S(1)}, u32[]{:S(2)}, u32[]{:S(2)}) collective-permute-start(f32[256,128]{1,0:T(8,128)S(1)} %get-tuple-element.173.token_ref), channel_id=1, source_target_pairs={{0,4},{4,0},{8,12},{12,8},{1,5},{5,1},{9,13},{13,9},{2,6},{6,2},{1... | collective-permute-start | bytes 393224 | tf_op jit(solution)/shard_map/ppermute | solution.py:445
  35.9 1.9 %collective-permute-start.20 = (f32[256,128]{1,0:T(8,128)S(1)}, f32[256,128]{1,0:T(8,128)S(1)}, u32[]{:S(2)}, u32[]{:S(2)}) collective-permute-start(f32[256,128]{1,0:T(8,128)S(1)} %get-tuple-element.174.token_ref), channel_id=1, source_target_pairs={{0,4},{4,0},{8,12},{12,8},{1,5},{5,1},{9,13},{13,9},{2,6},{6,2},{1... | collective-permute-start | bytes 393224 | tf_op jit(solution)/shard_map/ppermute | solution.py:445
  38.7 1.9 %collective-permute-start.22 = (f32[256,128]{1,0:T(8,128)S(1)}, f32[256,128]{1,0:T(8,128)S(1)}, u32[]{:S(2)}, u32[]{:S(2)}) collective-permute-start(f32[256,128]{1,0:T(8,128)S(1)} %get-tuple-element.175.token_ref), channel_id=1, source_target_pairs={{0,4},{4,0},{8,12},{12,8},{1,5},{5,1},{9,13},{13,9},{2,6},{6,2},{1... | collective-permute-start | bytes 393224 | tf_op jit(solution)/shard_map/ppermute | solution.py:445
  41.5 1.9 %collective-permute-start.24 = (f32[256,128]{1,0:T(8,128)S(1)}, f32[256,128]{1,0:T(8,128)S(1)}, u32[]{:S(2)}, u32[]{:S(2)}) collective-permute-start(f32[256,128]{1,0:T(8,128)S(1)} %get-tuple-element.176.token_ref), channel_id=1, source_target_pairs={{0,4},{4,0},{8,12},{12,8},{1,5},{5,1},{9,13},{13,9},{2,6},{6,2},{1... | collective-permute-start | bytes 393224 | tf_op jit(solution)/shard_map/ppermute | solution.py:445
  44.3 1.9 %collective-permute-start.26 = (f32[256,128]{1,0:T(8,128)S(1)}, f32[256,128]{1,0:T(8,128)S(1)}, u32[]{:S(2)}, u32[]{:S(2)}) collective-permute-start(f32[256,128]{1,0:T(8,128)S(1)} %get-tuple-element.177.token_ref), channel_id=1, source_target_pairs={{0,4},{4,0},{8,12},{12,8},{1,5},{5,1},{9,13},{13,9},{2,6},{6,2},{1... | collective-permute-start | bytes 393224 | tf_op jit(solution)/shard_map/ppermute | solution.py:445
  47.1 1.9 %collective-permute-start.28 = (f32[256,128]{1,0:T(8,128)S(1)}, f32[256,128]{1,0:T(8,128)S(1)}, u32[]{:S(2)}, u32[]{:S(2)}) collective-permute-start(f32[256,128]{1,0:T(8,128)S(1)} %get-tuple-element.178.token_ref), channel_id=1, source_target_pairs={{0,4},{4,0},{8,12},{12,8},{1,5},{5,1},{9,13},{13,9},{2,6},{6,2},{1... | collective-permute-start | bytes 393224 | tf_op jit(solution)/shard_map/ppermute | solution.py:445
  52.8 1.9 %collective-permute-start.32 = (f32[256,128]{1,0:T(8,128)S(1)}, f32[256,128]{1,0:T(8,128)S(1)}, u32[]{:S(2)}, u32[]{:S(2)}) collective-permute-start(f32[256,128]{1,0:T(8,128)S(1)} %get-tuple-element.184.token_ref), channel_id=1, source_target_pairs={{0,4},{4,0},{8,12},{12,8},{1,5},{5,1},{9,13},{13,9},{2,6},{6,2},{1... | collective-permute-start | bytes 393224 | tf_op jit(solution)/shard_map/ppermute | solution.py:445
  58.4 1.9 %collective-permute-start.36 = (f32[256,128]{1,0:T(8,128)S(1)}, f32[256,128]{1,0:T(8,128)S(1)}, u32[]{:S(2)}, u32[]{:S(2)}) collective-permute-start(f32[256,128]{1,0:T(8,128)S(1)} %get-tuple-element.190.token_ref), channel_id=1, source_target_pairs={{0,4},{4,0},{8,12},{12,8},{1,5},{5,1},{9,13},{13,9},{2,6},{6,2},{1... | collective-permute-start | bytes 393224 | tf_op jit(solution)/shard_map/ppermute | solution.py:445
  61.2 1.9 %collective-permute-start.38 = (f32[256,128]{1,0:T(8,128)S(1)}, f32[256,128]{1,0:T(8,128)S(1)}, u32[]{:S(2)}, u32[]{:S(2)}) collective-permute-start(f32[256,128]{1,0:T(8,128)S(1)} %get-tuple-element.193.token_ref), channel_id=1, source_target_pairs={{0,4},{4,0},{8,12},{12,8},{1,5},{5,1},{9,13},{13,9},{2,6},{6,2},{1... | collective-permute-start | bytes 393224 | tf_op jit(solution)/shard_map/ppermute | solution.py:445
  64.0 1.9 %collective-permute-start.40 = (f32[256,128]{1,0:T(8,128)S(1)}, f32[256,128]{1,0:T(8,128)S(1)}, u32[]{:S(2)}, u32[]{:S(2)}) collective-permute-start(f32[256,128]{1,0:T(8,128)S(1)} %get-tuple-element.196.token_ref), channel_id=1, source_target_pairs={{0,4},{4,0},{8,12},{12,8},{1,5},{5,1},{9,13},{13,9},{2,6},{6,2},{1... | collective-permute-start | bytes 393224 | tf_op jit(solution)/shard_map/ppermute | solution.py:445
  66.8 1.9 %collective-permute-start.42 = (f32[256,128]{1,0:T(8,128)S(1)}, f32[256,128]{1,0:T(8,128)S(1)}, u32[]{:S(2)}, u32[]{:S(2)}) collective-permute-start(f32[256,128]{1,0:T(8,128)S(1)} %get-tuple-element.199.token_ref), channel_id=1, source_target_pairs={{0,4},{4,0},{8,12},{12,8},{1,5},{5,1},{9,13},{13,9},{2,6},{6,2},{1... | collective-permute-start | bytes 393224 | tf_op jit(solution)/shard_map/ppermute | solution.py:445
  69.6 1.9 %collective-permute-start.44 = (f32[256,128]{1,0:T(8,128)S(1)}, f32[256,128]{1,0:T(8,128)S(1)}, u32[]{:S(2)}, u32[]{:S(2)}) collective-permute-start(f32[256,128]{1,0:T(8,128)S(1)} %get-tuple-element.202.token_ref), channel_id=1, source_target_pairs={{0,4},{4,0},{8,12},{12,8},{1,5},{5,1},{9,13},{13,9},{2,6},{6,2},{1... | collective-permute-start | bytes 393224 | tf_op jit(solution)/shard_map/ppermute | solution.py:445
  72.5 1.9 %collective-permute-start.46 = (f32[256,128]{1,0:T(8,128)S(1)}, f32[256,128]{1,0:T(8,128)S(1)}, u32[]{:S(2)}, u32[]{:S(2)}) collective-permute-start(f32[256,128]{1,0:T(8,128)S(1)} %get-tuple-element.205.token_ref), channel_id=1, source_target_pairs={{0,4},{4,0},{8,12},{12,8},{1,5},{5,1},{9,13},{13,9},{2,6},{6,2},{1... | collective-permute-start | bytes 393224 | tf_op jit(solution)/shard_map/ppermute | solution.py:445
  75.3 1.9 %collective-permute-start.48 = (f32[256,128]{1,0:T(8,128)S(1)}, f32[256,128]{1,0:T(8,128)S(1)}, u32[]{:S(2)}, u32[]{:S(2)}) collective-permute-start(f32[256,128]{1,0:T(8,128)S(1)} %get-tuple-element.208.token_ref), channel_id=1, source_target_pairs={{0,4},{4,0},{8,12},{12,8},{1,5},{5,1},{9,13},{13,9},{2,6},{6,2},{1... | collective-permute-start | bytes 393224 | tf_op jit(solution)/shard_map/ppermute | solution.py:445
  78.1 1.9 %collective-permute-start.50 = (f32[256,128]{1,0:T(8,128)S(1)}, f32[256,128]{1,0:T(8,128)S(1)}, u32[]{:S(2)}, u32[]{:S(2)}) collective-permute-start(f32[256,128]{1,0:T(8,128)S(1)} %get-tuple-element.211.token_ref), channel_id=1, source_target_pairs={{0,4},{4,0},{8,12},{12,8},{1,5},{5,1},{9,13},{13,9},{2,6},{6,2},{1... | collective-permute-start | bytes 393224 | tf_op jit(solution)/shard_map/ppermute | solution.py:445
  80.9 1.9 %collective-permute-start.52 = (f32[256,128]{1,0:T(8,128)S(1)}, f32[256,128]{1,0:T(8,128)S(1)}, u32[]{:S(2)}, u32[]{:S(2)}) collective-permute-start(f32[256,128]{1,0:T(8,128)S(1)} %get-tuple-element.214.token_ref), channel_id=1, source_target_pairs={{0,4},{4,0},{8,12},{12,8},{1,5},{5,1},{9,13},{13,9},{2,6},{6,2},{1... | collective-permute-start | bytes 393224 | tf_op jit(solution)/shard_map/ppermute | solution.py:445
  83.7 1.9 %collective-permute-start.54 = (f32[256,128]{1,0:T(8,128)S(1)}, f32[256,128]{1,0:T(8,128)S(1)}, u32[]{:S(2)}, u32[]{:S(2)}) collective-permute-start(f32[256,128]{1,0:T(8,128)S(1)} %get-tuple-element.217.token_ref), channel_id=1, source_target_pairs={{0,4},{4,0},{8,12},{12,8},{1,5},{5,1},{9,13},{13,9},{2,6},{6,2},{1... | collective-permute-start | bytes 393224 | tf_op jit(solution)/shard_map/ppermute | solution.py:445
  86.5 1.9 %collective-permute-start.56 = (f32[256,128]{1,0:T(8,128)S(1)}, f32[256,128]{1,0:T(8,128)S(1)}, u32[]{:S(2)}, u32[]{:S(2)}) collective-permute-start(f32[256,128]{1,0:T(8,128)S(1)} %get-tuple-element.220.token_ref), channel_id=1, source_target_pairs={{0,4},{4,0},{8,12},{12,8},{1,5},{5,1},{9,13},{13,9},{2,6},{6,2},{1... | collective-permute-start | bytes 393224 | tf_op jit(solution)/shard_map/ppermute | solution.py:445
  89.3 1.9 %collective-permute-start.58 = (f32[256,128]{1,0:T(8,128)S(1)}, f32[256,128]{1,0:T(8,128)S(1)}, u32[]{:S(2)}, u32[]{:S(2)}) collective-permute-start(f32[256,128]{1,0:T(8,128)S(1)} %get-tuple-element.223.token_ref), channel_id=1, source_target_pairs={{0,4},{4,0},{8,12},{12,8},{1,5},{5,1},{9,13},{13,9},{2,6},{6,2},{1... | collective-permute-start | bytes 393224 | tf_op jit(solution)/shard_map/ppermute | solution.py:445
  92.1 1.9 %collective-permute-start.60 = (f32[256,128]{1,0:T(8,128)S(1)}, f32[256,128]{1,0:T(8,128)S(1)}, u32[]{:S(2)}, u32[]{:S(2)}) collective-permute-start(f32[256,128]{1,0:T(8,128)S(1)} %get-tuple-element.226.token_ref), channel_id=1, source_target_pairs={{0,4},{4,0},{8,12},{12,8},{1,5},{5,1},{9,13},{13,9},{2,6},{6,2},{1... | collective-permute-start | bytes 393224 | tf_op jit(solution)/shard_map/ppermute | solution.py:445
  105.6 1.9 %collective-permute-start.68 = (f32[256,128]{1,0:T(8,128)S(1)}, f32[256,128]{1,0:T(8,128)S(1)}, u32[]{:S(2)}, u32[]{:S(2)}) collective-permute-start(f32[256,128]{1,0:T(8,128)S(1)} %merge.73.token_ref.near_ref), channel_id=1, source_target_pairs={{0,4},{4,0},{8,12},{12,8},{1,5},{5,1},{9,13},{13,9},{2,6},{6,2},{1... | collective-permute-start | bytes 393224 | tf_op jit(solution)/shard_map/ppermute | solution.py:445
  108.5 2.2 %collective-permute-done.67.far_ref = f32[256,128]{1,0:T(8,128)S(1)} collective-permute-done((f32[256,128]{1,0:T(8,128)S(1)}, f32[256,128]{1,0:T(8,128)S(1)}, u32[]{:S(2)}, u32[]{:S(2)}) %collective-permute-start.67) | collective-permute-done | bytes 131104 | tf_op jit(solution)/shard_map/ppermute | solution.py:445
  121.1 1.9 %collective-permute-done.73.other_ref = f32[128,128]{1,0:T(8,128)S(1)} collective-permute-done((f32[128,128]{1,0:T(8,128)S(1)}, f32[128,128]{1,0:T(8,128)S(1)}, u32[]{:S(2)}, u32[]{:S(2)}) %collective-permute-start.73) | collective-permute-done | bytes 65568 | tf_op jit(solution)/shard_map/ppermute | solution.py:482
  (264 shorter events, 57.2 us)
Async XLA Ops:
  3.0 10.1 %collective-permute-start = (f32[256,128]{1,0:T(8,128)S(1)}, f32[256,128]{1,0:T(8,128)S(1)}, u32[]{:S(2)}, u32[]{:S(2)}) collective-permute-start(f32[256,128]{1,0:T(8,128)S(1)} %merge.39), channel_id=1, source_target_pairs={{0,4},{4,0},{8,12},{12,8},{1,5},{5,1},{9,13},{13,9},{2,6},{6,2},{1... | collective-permute-start | bytes 393224 | tf_op jit(solution)/shard_map/ppermute | solution.py:445
  6.1 11.0 %collective-permute-start.1 = (f32[256,128]{1,0:T(8,128)S(1)}, f32[256,128]{1,0:T(8,128)S(1)}, u32[]{:S(2)}, u32[]{:S(2)}) collective-permute-start(f32[256,128]{1,0:T(8,128)S(1)} %merge.37.token_ref), channel_id=1, source_target_pairs={{0,4},{4,0},{8,12},{12,8},{1,5},{5,1},{9,13},{13,9},{2,6},{6,2},{1... | collective-permute-start | bytes 393224 | tf_op jit(solution)/shard_map/ppermute | solution.py:445
  10.3 8.2 %collective-permute-start.2 = (f32[256,128]{1,0:T(8,128)S(1)}, f32[256,128]{1,0:T(8,128)S(1)}, u32[]{:S(2)}, u32[]{:S(2)}) collective-permute-start(f32[256,128]{1,0:T(8,128)S(1)} %merge.38.token_ref), channel_id=1, source_target_pairs={{0,4},{4,0},{8,12},{12,8},{1,5},{5,1},{9,13},{13,9},{2,6},{6,2},{1... | collective-permute-start | bytes 393224 | tf_op jit(solution)/shard_map/ppermute | solution.py:445
  13.2 7.8 %collective-permute-start.4 = (f32[256,128]{1,0:T(8,128)S(1)}, f32[256,128]{1,0:T(8,128)S(1)}, u32[]{:S(2)}, u32[]{:S(2)}) collective-permute-start(f32[256,128]{1,0:T(8,128)S(1)} %merge.40.token_ref), channel_id=1, source_target_pairs={{0,4},{4,0},{8,12},{12,8},{1,5},{5,1},{9,13},{13,9},{2,6},{6,2},{1... | collective-permute-start | bytes 393224 | tf_op jit(solution)/shard_map/ppermute | solution.py:445
  18.7 8.6 %collective-permute-start.8 = (f32[256,128]{1,0:T(8,128)S(1)}, f32[256,128]{1,0:T(8,128)S(1)}, u32[]{:S(2)}, u32[]{:S(2)}) collective-permute-start(f32[256,128]{1,0:T(8,128)S(1)} %get-tuple-element.168.token_ref), channel_id=1, source_target_pairs={{0,4},{4,0},{8,12},{12,8},{1,5},{5,1},{9,13},{13,9},{2,6},{6,2},{1... | collective-permute-start | bytes 393224 | tf_op jit(solution)/shard_map/ppermute | solution.py:445
  21.2 9.0 %collective-permute-start.10 = (f32[256,128]{1,0:T(8,128)S(1)}, f32[256,128]{1,0:T(8,128)S(1)}, u32[]{:S(2)}, u32[]{:S(2)}) collective-permute-start(f32[256,128]{1,0:T(8,128)S(1)} %get-tuple-element.169.token_ref), channel_id=1, source_target_pairs={{0,4},{4,0},{8,12},{12,8},{1,5},{5,1},{9,13},{13,9},{2,6},{6,2},{1... | collective-permute-start | bytes 393224 | tf_op jit(solution)/shard_map/ppermute | solution.py:445
  24.1 8.8 %collective-permute-start.12 = (f32[256,128]{1,0:T(8,128)S(1)}, f32[256,128]{1,0:T(8,128)S(1)}, u32[]{:S(2)}, u32[]{:S(2)}) collective-permute-start(f32[256,128]{1,0:T(8,128)S(1)} %get-tuple-element.170.token_ref), channel_id=1, source_target_pairs={{0,4},{4,0},{8,12},{12,8},{1,5},{5,1},{9,13},{13,9},{2,6},{6,2},{1... | collective-permute-start | bytes 393224 | tf_op jit(solution)/shard_map/ppermute | solution.py:445
  27.5 8.3 %collective-permute-start.14 = (f32[256,128]{1,0:T(8,128)S(1)}, f32[256,128]{1,0:T(8,128)S(1)}, u32[]{:S(2)}, u32[]{:S(2)}) collective-permute-start(f32[256,128]{1,0:T(8,128)S(1)} %get-tuple-element.171.token_ref), channel_id=1, source_target_pairs={{0,4},{4,0},{8,12},{12,8},{1,5},{5,1},{9,13},{13,9},{2,6},{6,2},{1... | collective-permute-start | bytes 393224 | tf_op jit(solution)/shard_map/ppermute | solution.py:445
  30.3 8.3 %collective-permute-start.16 = (f32[256,128]{1,0:T(8,128)S(1)}, f32[256,128]{1,0:T(8,128)S(1)}, u32[]{:S(2)}, u32[]{:S(2)}) collective-permute-start(f32[256,128]{1,0:T(8,128)S(1)} %get-tuple-element.172.token_ref), channel_id=1, source_target_pairs={{0,4},{4,0},{8,12},{12,8},{1,5},{5,1},{9,13},{13,9},{2,6},{6,2},{1... | collective-permute-start | bytes 393224 | tf_op jit(solution)/shard_map/ppermute | solution.py:445
  33.1 8.3 %collective-permute-start.18 = (f32[256,128]{1,0:T(8,128)S(1)}, f32[256,128]{1,0:T(8,128)S(1)}, u32[]{:S(2)}, u32[]{:S(2)}) collective-permute-start(f32[256,128]{1,0:T(8,128)S(1)} %get-tuple-element.173.token_ref), channel_id=1, source_target_pairs={{0,4},{4,0},{8,12},{12,8},{1,5},{5,1},{9,13},{13,9},{2,6},{6,2},{1... | collective-permute-start | bytes 393224 | tf_op jit(solution)/shard_map/ppermute | solution.py:445
  35.9 8.3 %collective-permute-start.20 = (f32[256,128]{1,0:T(8,128)S(1)}, f32[256,128]{1,0:T(8,128)S(1)}, u32[]{:S(2)}, u32[]{:S(2)}) collective-permute-start(f32[256,128]{1,0:T(8,128)S(1)} %get-tuple-element.174.token_ref), channel_id=1, source_target_pairs={{0,4},{4,0},{8,12},{12,8},{1,5},{5,1},{9,13},{13,9},{2,6},{6,2},{1... | collective-permute-start | bytes 393224 | tf_op jit(solution)/shard_map/ppermute | solution.py:445
  38.7 8.3 %collective-permute-start.22 = (f32[256,128]{1,0:T(8,128)S(1)}, f32[256,128]{1,0:T(8,128)S(1)}, u32[]{:S(2)}, u32[]{:S(2)}) collective-permute-start(f32[256,128]{1,0:T(8,128)S(1)} %get-tuple-element.175.token_ref), channel_id=1, source_target_pairs={{0,4},{4,0},{8,12},{12,8},{1,5},{5,1},{9,13},{13,9},{2,6},{6,2},{1... | collective-permute-start | bytes 393224 | tf_op jit(solution)/shard_map/ppermute | solution.py:445
  41.5 8.3 %collective-permute-start.24 = (f32[256,128]{1,0:T(8,128)S(1)}, f32[256,128]{1,0:T(8,128)S(1)}, u32[]{:S(2)}, u32[]{:S(2)}) collective-permute-start(f32[256,128]{1,0:T(8,128)S(1)} %get-tuple-element.176.token_ref), channel_id=1, source_target_pairs={{0,4},{4,0},{8,12},{12,8},{1,5},{5,1},{9,13},{13,9},{2,6},{6,2},{1... | collective-permute-start | bytes 393224 | tf_op jit(solution)/shard_map/ppermute | solution.py:445
  44.3 8.3 %collective-permute-start.26 = (f32[256,128]{1,0:T(8,128)S(1)}, f32[256,128]{1,0:T(8,128)S(1)}, u32[]{:S(2)}, u32[]{:S(2)}) collective-permute-start(f32[256,128]{1,0:T(8,128)S(1)} %get-tuple-element.177.token_ref), channel_id=1, source_target_pairs={{0,4},{4,0},{8,12},{12,8},{1,5},{5,1},{9,13},{13,9},{2,6},{6,2},{1... | collective-permute-start | bytes 393224 | tf_op jit(solution)/shard_map/ppermute | solution.py:445
  47.1 8.3 %collective-permute-start.28 = (f32[256,128]{1,0:T(8,128)S(1)}, f32[256,128]{1,0:T(8,128)S(1)}, u32[]{:S(2)}, u32[]{:S(2)}) collective-permute-start(f32[256,128]{1,0:T(8,128)S(1)} %get-tuple-element.178.token_ref), channel_id=1, source_target_pairs={{0,4},{4,0},{8,12},{12,8},{1,5},{5,1},{9,13},{13,9},{2,6},{6,2},{1... | collective-permute-start | bytes 393224 | tf_op jit(solution)/shard_map/ppermute | solution.py:445
  50.0 8.3 %collective-permute-start.30 = (f32[256,128]{1,0:T(8,128)S(1)}, f32[256,128]{1,0:T(8,128)S(1)}, u32[]{:S(2)}, u32[]{:S(2)}) collective-permute-start(f32[256,128]{1,0:T(8,128)S(1)} %get-tuple-element.181.token_ref), channel_id=1, source_target_pairs={{0,4},{4,0},{8,12},{12,8},{1,5},{5,1},{9,13},{13,9},{2,6},{6,2},{1... | collective-permute-start | bytes 393224 | tf_op jit(solution)/shard_map/ppermute | solution.py:445
  52.8 8.3 %collective-permute-start.32 = (f32[256,128]{1,0:T(8,128)S(1)}, f32[256,128]{1,0:T(8,128)S(1)}, u32[]{:S(2)}, u32[]{:S(2)}) collective-permute-start(f32[256,128]{1,0:T(8,128)S(1)} %get-tuple-element.184.token_ref), channel_id=1, source_target_pairs={{0,4},{4,0},{8,12},{12,8},{1,5},{5,1},{9,13},{13,9},{2,6},{6,2},{1... | collective-permute-start | bytes 393224 | tf_op jit(solution)/shard_map/ppermute | solution.py:445
  55.8 8.1 %collective-permute-start.34 = (f32[256,128]{1,0:T(8,128)S(1)}, f32[256,128]{1,0:T(8,128)S(1)}, u32[]{:S(2)}, u32[]{:S(2)}) collective-permute-start(f32[256,128]{1,0:T(8,128)S(1)} %get-tuple-element.187.token_ref), channel_id=1, source_target_pairs={{0,4},{4,0},{8,12},{12,8},{1,5},{5,1},{9,13},{13,9},{2,6},{6,2},{1... | collective-permute-start | bytes 393224 | tf_op jit(solution)/shard_map/ppermute | solution.py:445
  58.4 8.3 %collective-permute-start.36 = (f32[256,128]{1,0:T(8,128)S(1)}, f32[256,128]{1,0:T(8,128)S(1)}, u32[]{:S(2)}, u32[]{:S(2)}) collective-permute-start(f32[256,128]{1,0:T(8,128)S(1)} %get-tuple-element.190.token_ref), channel_id=1, source_target_pairs={{0,4},{4,0},{8,12},{12,8},{1,5},{5,1},{9,13},{13,9},{2,6},{6,2},{1... | collective-permute-start | bytes 393224 | tf_op jit(solution)/shard_map/ppermute | solution.py:445
  61.2 8.3 %collective-permute-start.38 = (f32[256,128]{1,0:T(8,128)S(1)}, f32[256,128]{1,0:T(8,128)S(1)}, u32[]{:S(2)}, u32[]{:S(2)}) collective-permute-start(f32[256,128]{1,0:T(8,128)S(1)} %get-tuple-element.193.token_ref), channel_id=1, source_target_pairs={{0,4},{4,0},{8,12},{12,8},{1,5},{5,1},{9,13},{13,9},{2,6},{6,2},{1... | collective-permute-start | bytes 393224 | tf_op jit(solution)/shard_map/ppermute | solution.py:445
  64.0 8.3 %collective-permute-start.40 = (f32[256,128]{1,0:T(8,128)S(1)}, f32[256,128]{1,0:T(8,128)S(1)}, u32[]{:S(2)}, u32[]{:S(2)}) collective-permute-start(f32[256,128]{1,0:T(8,128)S(1)} %get-tuple-element.196.token_ref), channel_id=1, source_target_pairs={{0,4},{4,0},{8,12},{12,8},{1,5},{5,1},{9,13},{13,9},{2,6},{6,2},{1... | collective-permute-start | bytes 393224 | tf_op jit(solution)/shard_map/ppermute | solution.py:445
  66.8 8.3 %collective-permute-start.42 = (f32[256,128]{1,0:T(8,128)S(1)}, f32[256,128]{1,0:T(8,128)S(1)}, u32[]{:S(2)}, u32[]{:S(2)}) collective-permute-start(f32[256,128]{1,0:T(8,128)S(1)} %get-tuple-element.199.token_ref), channel_id=1, source_target_pairs={{0,4},{4,0},{8,12},{12,8},{1,5},{5,1},{9,13},{13,9},{2,6},{6,2},{1... | collective-permute-start | bytes 393224 | tf_op jit(solution)/shard_map/ppermute | solution.py:445
  69.6 8.3 %collective-permute-start.44 = (f32[256,128]{1,0:T(8,128)S(1)}, f32[256,128]{1,0:T(8,128)S(1)}, u32[]{:S(2)}, u32[]{:S(2)}) collective-permute-start(f32[256,128]{1,0:T(8,128)S(1)} %get-tuple-element.202.token_ref), channel_id=1, source_target_pairs={{0,4},{4,0},{8,12},{12,8},{1,5},{5,1},{9,13},{13,9},{2,6},{6,2},{1... | collective-permute-start | bytes 393224 | tf_op jit(solution)/shard_map/ppermute | solution.py:445
  72.5 8.3 %collective-permute-start.46 = (f32[256,128]{1,0:T(8,128)S(1)}, f32[256,128]{1,0:T(8,128)S(1)}, u32[]{:S(2)}, u32[]{:S(2)}) collective-permute-start(f32[256,128]{1,0:T(8,128)S(1)} %get-tuple-element.205.token_ref), channel_id=1, source_target_pairs={{0,4},{4,0},{8,12},{12,8},{1,5},{5,1},{9,13},{13,9},{2,6},{6,2},{1... | collective-permute-start | bytes 393224 | tf_op jit(solution)/shard_map/ppermute | solution.py:445
  75.3 8.3 %collective-permute-start.48 = (f32[256,128]{1,0:T(8,128)S(1)}, f32[256,128]{1,0:T(8,128)S(1)}, u32[]{:S(2)}, u32[]{:S(2)}) collective-permute-start(f32[256,128]{1,0:T(8,128)S(1)} %get-tuple-element.208.token_ref), channel_id=1, source_target_pairs={{0,4},{4,0},{8,12},{12,8},{1,5},{5,1},{9,13},{13,9},{2,6},{6,2},{1... | collective-permute-start | bytes 393224 | tf_op jit(solution)/shard_map/ppermute | solution.py:445
  78.1 8.3 %collective-permute-start.50 = (f32[256,128]{1,0:T(8,128)S(1)}, f32[256,128]{1,0:T(8,128)S(1)}, u32[]{:S(2)}, u32[]{:S(2)}) collective-permute-start(f32[256,128]{1,0:T(8,128)S(1)} %get-tuple-element.211.token_ref), channel_id=1, source_target_pairs={{0,4},{4,0},{8,12},{12,8},{1,5},{5,1},{9,13},{13,9},{2,6},{6,2},{1... | collective-permute-start | bytes 393224 | tf_op jit(solution)/shard_map/ppermute | solution.py:445
  80.9 8.3 %collective-permute-start.52 = (f32[256,128]{1,0:T(8,128)S(1)}, f32[256,128]{1,0:T(8,128)S(1)}, u32[]{:S(2)}, u32[]{:S(2)}) collective-permute-start(f32[256,128]{1,0:T(8,128)S(1)} %get-tuple-element.214.token_ref), channel_id=1, source_target_pairs={{0,4},{4,0},{8,12},{12,8},{1,5},{5,1},{9,13},{13,9},{2,6},{6,2},{1... | collective-permute-start | bytes 393224 | tf_op jit(solution)/shard_map/ppermute | solution.py:445
  83.7 8.3 %collective-permute-start.54 = (f32[256,128]{1,0:T(8,128)S(1)}, f32[256,128]{1,0:T(8,128)S(1)}, u32[]{:S(2)}, u32[]{:S(2)}) collective-permute-start(f32[256,128]{1,0:T(8,128)S(1)} %get-tuple-element.217.token_ref), channel_id=1, source_target_pairs={{0,4},{4,0},{8,12},{12,8},{1,5},{5,1},{9,13},{13,9},{2,6},{6,2},{1... | collective-permute-start | bytes 393224 | tf_op jit(solution)/shard_map/ppermute | solution.py:445
  86.5 8.7 %collective-permute-start.56 = (f32[256,128]{1,0:T(8,128)S(1)}, f32[256,128]{1,0:T(8,128)S(1)}, u32[]{:S(2)}, u32[]{:S(2)}) collective-permute-start(f32[256,128]{1,0:T(8,128)S(1)} %get-tuple-element.220.token_ref), channel_id=1, source_target_pairs={{0,4},{4,0},{8,12},{12,8},{1,5},{5,1},{9,13},{13,9},{2,6},{6,2},{1... | collective-permute-start | bytes 393224 | tf_op jit(solution)/shard_map/ppermute | solution.py:445
  89.3 8.9 %collective-permute-start.58 = (f32[256,128]{1,0:T(8,128)S(1)}, f32[256,128]{1,0:T(8,128)S(1)}, u32[]{:S(2)}, u32[]{:S(2)}) collective-permute-start(f32[256,128]{1,0:T(8,128)S(1)} %get-tuple-element.223.token_ref), channel_id=1, source_target_pairs={{0,4},{4,0},{8,12},{12,8},{1,5},{5,1},{9,13},{13,9},{2,6},{6,2},{1... | collective-permute-start | bytes 393224 | tf_op jit(solution)/shard_map/ppermute | solution.py:445
  92.1 9.2 %collective-permute-start.60 = (f32[256,128]{1,0:T(8,128)S(1)}, f32[256,128]{1,0:T(8,128)S(1)}, u32[]{:S(2)}, u32[]{:S(2)}) collective-permute-start(f32[256,128]{1,0:T(8,128)S(1)} %get-tuple-element.226.token_ref), channel_id=1, source_target_pairs={{0,4},{4,0},{8,12},{12,8},{1,5},{5,1},{9,13},{13,9},{2,6},{6,2},{1... | collective-permute-start | bytes 393224 | tf_op jit(solution)/shard_map/ppermute | solution.py:445
  95.3 7.6 %collective-permute-start.62 = (f32[256,128]{1,0:T(8,128)S(1)}, f32[256,128]{1,0:T(8,128)S(1)}, u32[]{:S(2)}, u32[]{:S(2)}) collective-permute-start(f32[256,128]{1,0:T(8,128)S(1)} %merge.69.token_ref.near_ref), channel_id=1, source_target_pairs={{0,4},{4,0},{8,12},{12,8},{1,5},{5,1},{9,13},{13,9},{2,6},{6,2},{1... | collective-permute-start | bytes 393224 | tf_op jit(solution)/shard_map/ppermute | solution.py:445
  (54 other events, 279.4 us)
